TPU v7x, 32 devices: a whole 2x2x4 slice. The times are simulated.
32 devices in a mesh: dp: 4 (over y, x), seq: 8 (over z, core).
Axes of the slice: x: 2, y: 2, z: 4, core: 2. Of those that a mesh axis runs over, the one named last changes fastest.
Arguments:
- queries: bfloat16 [4, 1024, 2048], P('dp', 'seq'), may hold values from -6 to 6
- attended_grad: bfloat16 [4, 1024, 2048], P('dp', 'seq'), may hold values from -6 to 6
- neighbour_pool: bfloat16 [4, 32, 128, 896], P('dp', 'seq'), may hold values from -6 to 6
- stretch_slot: int32 [4, 16], P('dp'), may hold values from 0 to 31, as said below
- enc_gain: float32 [896], replicated, may hold values from 0.1 to 1.9
- enc_up: bfloat16 [896, 1792], replicated, may hold values from -0.1875 to 0.1875
- enc_down: bfloat16 [1792, 896], replicated, may hold values from -0.125 to 0.125
- key_weight: bfloat16 [896, 2048], P(None, 'seq'), may hold values from -0.1875 to 0.1875
- value_weight: bfloat16 [896, 2048], P(None, 'seq'), may hold values from -0.1875 to 0.1875
Outputs:
- attended: bfloat16 [4, 1024, 2048], P('dp', 'seq')
- query_grad: bfloat16 [4, 1024, 2048], P('dp', 'seq')
- pool_grad: bfloat16 [4, 32, 128, 896], P('dp', 'seq')
- key_weight_grad: float32 [896, 2048], P(None, 'seq')
- value_weight_grad: float32 [896, 2048], P(None, 'seq')
Inputs may be any that keep to these rules, and one draw needn't show every extreme that they name: `stretch_slot`: slot s is held by the device s // 4 along seq. No slot is named twice within a sequence, and in every sequence some device holds 4 named slots.
All inputs are finite; a program needn't handle non-finite values.
Results may differ from a plain program's by a relative error of at most 0.03.
Values may be sent and summed in bfloat16 or wider, within the bound.
No kernel may reach another device: no remote copies, remote signals or barrier semaphores. Data moves between devices by JAX's collectives and lax.ppermute only.
A program may use at most 128 MiB of HBM per device.

v0:
```python
import math

import jax
import jax.numpy as jnp
from jax import lax
from jax.sharding import PartitionSpec as P

STRETCH = 64
HD = 128


epsilon = 1e-06


def encode_rows(row_block, gain_vector, up_matrix, down_matrix):
    row_values = row_block.astype(jnp.float32)
    inverse = lax.rsqrt(jnp.mean(row_values * row_values, axis=-1, keepdims=True) + epsilon)
    normed = (row_values * inverse * gain_vector).astype(jnp.bfloat16)
    before = jnp.dot(normed, up_matrix, preferred_element_type=jnp.float32)
    activity = jax.nn.gelu(before).astype(jnp.bfloat16)
    encoded = (
        row_values + jnp.dot(activity, down_matrix, preferred_element_type=jnp.float32)
    ).astype(jnp.bfloat16)
    return (encoded, before, inverse)


def encode_backward(encoded_grad, row_block, before, inverse, gain_vector, up_matrix, down_matrix):
    activity_grad = jnp.einsum(
        "rd,fd->rf", encoded_grad, down_matrix, preferred_element_type=jnp.float32
    )
    unused_value, gelu_back = jax.vjp(jax.nn.gelu, before)
    before_grad = gelu_back(activity_grad)[0].astype(jnp.bfloat16)
    normed_grad = jnp.einsum(
        "rf,df->rd", before_grad, up_matrix, preferred_element_type=jnp.float32
    )
    row_values = row_block.astype(jnp.float32)
    scaled_grad = gain_vector * normed_grad
    cubed = inverse * inverse * inverse
    result = (
        encoded_grad.astype(jnp.float32)
        + inverse * scaled_grad
        - row_values * cubed * jnp.mean(row_values * scaled_grad, axis=-1, keepdims=True)
    )
    return result.astype(jnp.bfloat16)


def on_device(
    queries,
    attended_grad,
    neighbour_pool,
    stretch_slot,
    enc_gain,
    enc_up,
    enc_down,
    key_weight,
    value_weight,
):
    groups = lax.axis_size("seq")
    token_count = queries.shape[1]
    stretch_count = token_count // STRETCH
    holding = neighbour_pool.shape[1]
    neighbour_span = neighbour_pool.shape[2]
    feature_width = neighbour_pool.shape[3]
    piece_rows = neighbour_span // groups
    all_slots = stretch_slot[0]
    total_stretches = all_slots.shape[0]
    middle_index = all_slots % holding * groups + all_slots // holding
    flat_position = jnp.arange(holding * groups, dtype=jnp.int32)
    position_slot = flat_position % groups * holding + flat_position // groups
    slot_match = all_slots[:, None] == position_slot[None, :]
    slot_user = jnp.sum(
        jnp.where(slot_match, jnp.arange(total_stretches, dtype=jnp.int32)[:, None], 0), axis=0
    )
    slot_named = jnp.any(slot_match, axis=0)
    pool_rows = neighbour_pool[0]
    pool_flat = pool_rows.reshape(holding * neighbour_span, feature_width)
    empty_value = jnp.zeros((), jnp.bfloat16)
    key_full, value_full = (
        lax.all_gather(key_weight, "seq", axis=1, tiled=True),
        lax.all_gather(value_weight, "seq", axis=1, tiled=True),
    )
    own_encoded, own_before, own_inverse = encode_rows(pool_flat, enc_gain, enc_up, enc_down)
    pieces = own_encoded.reshape(holding, neighbour_span, feature_width).reshape(
        holding, groups, piece_rows, feature_width
    )
    received = lax.all_to_all(pieces, "seq", split_axis=1, concat_axis=1, tiled=True)
    middle_rows = received.reshape(holding * groups, piece_rows, feature_width)[middle_index]
    gathered = lax.all_to_all(
        middle_rows.reshape(groups, stretch_count, piece_rows, feature_width),
        "seq",
        split_axis=0,
        concat_axis=2,
        tiled=True,
    )
    encoded_rows = gathered.reshape(stretch_count * neighbour_span, feature_width)
    head_count = key_full.shape[1] // HD
    score_scale = 1.0 / math.sqrt(HD)
    key_rows = jnp.dot(encoded_rows, key_full, preferred_element_type=jnp.float32).astype(
        jnp.bfloat16
    )
    value_rows = jnp.dot(encoded_rows, value_full, preferred_element_type=jnp.float32).astype(
        jnp.bfloat16
    )
    query_blocks = queries.reshape(stretch_count, STRETCH, head_count, HD)
    grad_blocks = attended_grad.reshape(stretch_count, STRETCH, head_count, HD)
    key_blocks = key_rows.reshape(stretch_count, neighbour_span, head_count, HD)
    value_blocks = value_rows.reshape(stretch_count, neighbour_span, head_count, HD)
    scores = (
        jnp.einsum("cqhe,ckhe->chqk", query_blocks, key_blocks, preferred_element_type=jnp.float32)
        * score_scale
    )
    exponent = jnp.exp(scores)
    weights = exponent / jnp.sum(exponent, axis=-1, keepdims=True)
    probabilities = weights.astype(jnp.bfloat16)
    attended = (
        jnp.einsum(
            "chqk,ckhe->cqhe", probabilities, value_blocks, preferred_element_type=jnp.float32
        )
        .astype(jnp.bfloat16)
        .reshape(queries.shape)
    )
    prob_grad = jnp.einsum(
        "cqhe,ckhe->chqk", grad_blocks, value_blocks, preferred_element_type=jnp.float32
    )
    score_grad = (
        weights * (prob_grad - jnp.sum(weights * prob_grad, axis=-1, keepdims=True)) * score_scale
    ).astype(jnp.bfloat16)
    query_grad = (
        jnp.einsum("chqk,ckhe->cqhe", score_grad, key_blocks, preferred_element_type=jnp.float32)
        .astype(jnp.bfloat16)
        .reshape(queries.shape)
    )
    key_grad = (
        jnp.einsum("chqk,cqhe->ckhe", score_grad, query_blocks, preferred_element_type=jnp.float32)
        .astype(jnp.bfloat16)
        .reshape(stretch_count * neighbour_span, -1)
    )
    value_grad = (
        jnp.einsum(
            "chqk,cqhe->ckhe", probabilities, grad_blocks, preferred_element_type=jnp.float32
        )
        .astype(jnp.bfloat16)
        .reshape(stretch_count * neighbour_span, -1)
    )
    key_part = jnp.einsum("rd,rh->dh", encoded_rows, key_grad, preferred_element_type=jnp.float32)
    value_part = jnp.einsum(
        "rd,rh->dh", encoded_rows, value_grad, preferred_element_type=jnp.float32
    )
    key_share, value_share = (
        lax.psum_scatter(
            key_part.astype(jnp.bfloat16), "seq", scatter_dimension=1, tiled=True
        ).astype(jnp.float32),
        lax.psum_scatter(
            value_part.astype(jnp.bfloat16), "seq", scatter_dimension=1, tiled=True
        ).astype(jnp.float32),
    )
    key_weight_grad, value_weight_grad = (
        lax.psum(key_share.astype(jnp.bfloat16), "dp").astype(jnp.float32),
        lax.psum(value_share.astype(jnp.bfloat16), "dp").astype(jnp.float32),
    )
    encoded_grad = (
        jnp.einsum("rh,dh->rd", key_grad, key_full, preferred_element_type=jnp.float32)
        + jnp.einsum("rh,dh->rd", value_grad, value_full, preferred_element_type=jnp.float32)
    ).astype(jnp.bfloat16)
    split_rows = lax.all_to_all(
        encoded_grad.reshape(1, stretch_count, neighbour_span, feature_width),
        "seq",
        split_axis=2,
        concat_axis=0,
        tiled=True,
    )
    middle_rows = split_rows.reshape(total_stretches, piece_rows, feature_width)
    placed = jnp.where(slot_named[:, None, None], middle_rows[slot_user], empty_value)
    returned = lax.all_to_all(
        placed.reshape(holding, groups, piece_rows, feature_width),
        "seq",
        split_axis=1,
        concat_axis=1,
        tiled=True,
    )
    slot_grad = returned.reshape(holding * neighbour_span, feature_width)
    pool_grad = encode_backward(
        slot_grad, pool_flat, own_before, own_inverse, enc_gain, enc_up, enc_down
    )
    return (
        attended,
        query_grad,
        pool_grad.reshape(1, holding, neighbour_span, feature_width),
        key_weight_grad,
        value_weight_grad,
    )


def solution(mesh):
    return jax.shard_map(
        on_device,
        mesh=mesh,
        in_specs=(
            P("dp", "seq", None),
            P("dp", "seq", None),
            P("dp", "seq", None, None),
            P("dp", None),
            P(),
            P(),
            P(),
            P(None, "seq"),
            P(None, "seq"),
        ),
        out_specs=(
            P("dp", "seq", None),
            P("dp", "seq", None),
            P("dp", "seq", None, None),
            P(None, "seq"),
            P(None, "seq"),
        ),
        check_vma=False,
    )
```

profile of v0, /device:TPU:0, one launch (start us, length us, event | category | flops | bytes accessed | tf_op | source)
XLA Modules:
  0.0 321.2 jit_solution(5199705527767122434)
XLA Ops:
  11.6 2.1 fusion.88
  13.8 2.3 fusion.12
  17.1 6.3 %all-to-all-start = ((bf16[4,8,16,896]{3,2,0,1:T(8,128)(2,1)}), bf16[4,8,16,896]{3,2,0,1:T(8,128)(2,1)}, u32[]{:S(2)}, u32[]{:S(2)}) async-start(bf16[4,8,16,896]{3,2,0,1:T(8,128)(2,1)} %copy.89), calls=%async_computation | async-start | bytes 1835008 | tf_op jit(solution)/shard_map/all_to_all | solution.py:86
  23.5 45.4 %all-to-all-done = bf16[4,8,16,896]{3,2,0,1:T(8,128)(2,1)} async-done(((bf16[4,8,16,896]{3,2,0,1:T(8,128)(2,1)}), bf16[4,8,16,896]{3,2,0,1:T(8,128)(2,1)}, u32[]{:S(2)}, u32[]{:S(2)}) %all-to-all-start) | async-done | bytes 917536 | tf_op jit(solution)/shard_map/all_to_all | solution.py:86
  68.9 2.2 copy.90
  71.1 2.5 gather_fusion
  73.6 4.1 %all-to-all-start.1 = ((bf16[8,2,16,896]{3,2,1,0:T(8,128)(2,1)}), bf16[8,2,16,896]{3,2,1,0:T(8,128)(2,1)}, u32[]{:S(2)}, u32[]{:S(2)}) async-start(bf16[8,2,16,896]{3,2,1,0:T(8,128)(2,1)} %bitcast.144), calls=%async_computation.1 | async-start | bytes 917504 | tf_op jit(solution)/shard_map/all_to_all | solution.py:88
  81.7 16.8 %all-to-all-done.1 = bf16[8,2,16,896]{3,2,1,0:T(8,128)(2,1)} async-done(((bf16[8,2,16,896]{3,2,1,0:T(8,128)(2,1)}), bf16[8,2,16,896]{3,2,1,0:T(8,128)(2,1)}, u32[]{:S(2)}, u32[]{:S(2)}) %all-to-all-start.1) | async-done | bytes 458784 | tf_op jit(solution)/shard_map/all_to_all | solution.py:88
  100.3 3.4 %fusion.25 = bf16[32,8,16,128]{3,1,2,0:T(8,128)(2,1)S(1)} fusion(bf16[256,896]{1,0:T(8,128)(2,1)} %bitcast.124, bf16[896,2048]{1,0:T(8,128)(2,1)} %all-gather.3.cloned.1.call-done), kind=kOutput, calls=%fused_computation.40 | convolution fusion | flops 940048384 | bytes 5177344 | tf_op jit(solution)/shard_map/dot_general | solution.py:101
  105.0 20.4 %all-gather.5.cloned.1.call-done = bf16[896,2048]{1,0:T(8,128)(2,1)} async-done(((bf16[896,256]{1,0:T(8,128)(2,1)}), bf16[896,2048]{1,0:T(8,128)(2,1)}) %all-gather.5.cloned.1.call-update) | async-done | bytes 3670032 | tf_op jit(solution)/shard_map/all_gather | solution.py:79
  125.4 3.5 %fusion.26 = bf16[32,8,16,128]{3,1,2,0:T(8,128)(2,1)S(1)} fusion(bf16[256,896]{1,0:T(8,128)(2,1)} %bitcast.125, bf16[896,2048]{1,0:T(8,128)(2,1)} %all-gather.5.cloned.1.call-done), kind=kOutput, calls=%fused_computation.41 | convolution fusion | flops 940048384 | bytes 5177344 | tf_op jit(solution)/shard_map/dot_general | solution.py:98
  133.4 4.3 %fusion.23 = bf16[2,128,16,128]{3,1,2,0:T(8,128)(2,1)} fusion(f32[2,16,64,128]{3,2,1,0:T(8,128)} %fusion.56, f32[2,16,64,128]{3,2,1,0:T(8,128)} %convolution_bitcast_fusion, bf16[2,64,16,128]{3,2,1,0:T(8,128)(2,1)} %bitcast.128), kind=kOutput, calls=%fused_computation.38 | convolution fusion | flops 68946048 | bytes 3670016 | tf_op jit(solution)/shard_map/chqk,cqhe->ckhe/dot_general | solution.py:134
  140.5 4.1 %convolution_convert_fusion.1 = bf16[896,2048]{1,0:T(8,128)(2,1)} fusion(bf16[256,896]{1,0:T(8,128)(2,1)} %bitcast.126, bf16[32,8,16,128]{3,2,1,0:T(8,128)(2,1)S(1)} %bitcast.134), kind=kOutput, calls=%fused_computation.14 | convolution fusion | flops 941359104 | bytes 5177344 | tf_op jit(solution)/shard_map/rd,rh->dh/dot_general | solution.py:145
  144.8 3.5 %fusion.24 = bf16[2,128,16,128]{3,1,2,0:T(8,128)(2,1)} fusion(bf16[2,64,16,128]{3,2,1,0:T(8,128)(2,1)} %bitcast.141, f32[2,16,64,128]{3,2,1,0:T(8,128)} %copy-done.9), kind=kOutput, calls=%fused_computation.39 | convolution fusion | flops 68159616 | bytes 2621440 | tf_op jit(solution)/shard_map/chqk,cqhe->ckhe/dot_general | solution.py:139
  151.2 4.0 %convolution_convert_fusion = bf16[896,2048]{1,0:T(8,128)(2,1)} fusion(bf16[256,896]{1,0:T(8,128)(2,1)} %bitcast.127, bf16[32,8,16,128]{3,2,1,0:T(8,128)(2,1)S(1)} %bitcast.136), kind=kOutput, calls=%fused_computation.13 | convolution fusion | flops 941359104 | bytes 5177344 | tf_op jit(solution)/shard_map/rd,rh->dh/dot_general | solution.py:146
  155.3 3.8 %fusion.39 = f32[256,896]{1,0:T(8,128)S(1)} fusion(bf16[896,2048]{1,0:T(8,128)(2,1)} %all-gather.5.cloned.1.call-done, bf16[32,8,16,128]{3,2,1,0:T(8,128)(2,1)} %bitcast.135), kind=kOutput, calls=%fused_computation.59 | convolution fusion | flops 939524096 | bytes 5636096 | tf_op jit(solution)/shard_map/rh,dh->rd/dot_general | solution.py:162
  161.7 4.1 %all-to-all-start.2 = ((bf16[1,2,128,896]{3,1,0,2:T(2,128)(2,1)}), bf16[1,2,128,896]{3,1,0,2:T(2,128)(2,1)}, u32[]{:S(2)}, u32[]{:S(2)}) async-start(bf16[1,2,128,896]{3,1,0,2:T(2,128)(2,1)} %copy.105), calls=%async_computation.2 | async-start | bytes 917504 | tf_op jit(solution)/shard_map/all_to_all | solution.py:165
  166.2 21.3 %all-to-all-done.2 = bf16[1,2,128,896]{3,1,0,2:T(2,128)(2,1)} async-done(((bf16[1,2,128,896]{3,1,0,2:T(2,128)(2,1)}), bf16[1,2,128,896]{3,1,0,2:T(2,128)(2,1)}, u32[]{:S(2)}, u32[]{:S(2)}) %all-to-all-start.2) | async-done | bytes 458784 | tf_op jit(solution)/shard_map/all_to_all | solution.py:165
  189.4 2.6 gather_fusion.1
  192.0 2.3 copy_select_fusion
  194.2 4.2 %all-to-all-start.3 = ((bf16[4,8,16,896]{3,2,0,1:T(8,128)(2,1)}), bf16[4,8,16,896]{3,2,0,1:T(8,128)(2,1)}, u32[]{:S(2)}, u32[]{:S(2)}) async-start(bf16[4,8,16,896]{3,2,0,1:T(8,128)(2,1)} %copy_select_fusion), calls=%async_computation.3 | async-start | bytes 1835008 | tf_op jit(solution)/shard_map/all_to_all | solution.py:174
  198.8 3.2 fusion.34
  201.9 2.2 copy.95
  204.1 2.1 reshape.248
  206.2 4.0 %fusion.35 = bf16[2,64,16,128]{3,1,2,0:T(8,128)(2,1)} fusion(f32[2,16,64,128]{3,2,1,0:T(8,128)} %fusion.56, f32[2,16,64,128]{3,2,1,0:T(8,128)} %convolution_bitcast_fusion, bf16[2,128,16,128]{3,2,1,0:T(8,128)(2,1)} %bitcast.131), kind=kOutput, calls=%fused_computation.55 | convolution fusion | flops 68683904 | bytes 3670016 | tf_op jit(solution)/shard_map/chqk,ckhe->cqhe/dot_general | solution.py:129
  210.1 2.2 copy.99
  214.4 18.3 %all-to-all-done.3 = bf16[4,8,16,896]{3,2,0,1:T(8,128)(2,1)} async-done(((bf16[4,8,16,896]{3,2,0,1:T(8,128)(2,1)}), bf16[4,8,16,896]{3,2,0,1:T(8,128)(2,1)}, u32[]{:S(2)}, u32[]{:S(2)}) %all-to-all-start.3) | async-done | bytes 917536 | tf_op jit(solution)/shard_map/all_to_all | solution.py:174
  232.7 2.2 copy.109
  234.9 18.5 %reduce-scatter.5.cloned.1.call-done = bf16[896,256]{1,0:T(8,128)(2,1)} async-done(((bf16[896,2048]{1,0:T(8,128)(2,1)}), bf16[896,256]{1,0:T(8,128)(2,1)}) %reduce-scatter.5.cloned.1.call-update) | async-done | bytes 458768 | tf_op jit(solution)/shard_map/reduce_scatter | solution.py:153
  253.4 9.2 %fusion.16 = (f32[512]{0:T(512)S(1)}, f32[512,896]{1,0:T(8,128)}) fusion(bf16[1,4,128,896]{3,2,1,0:T(8,128)(2,1)} %param.11, f32[896]{0:T(1024)S(1)} %copy-done.10, bf16[896,1792]{1,0:T(8,128)(2,1)S(1)} %copy-done, f32[512,1792]{1,0:T(8,128)} %copy-done.14, bf16[512,896]{1,0:T(8,128)(2,1)} %bitcast.140, bf16[1792,896]{1,0:T(8,128)(2,1)} %param.15), kind=kOutput, calls=%fused_computation.30 | convolution fusion | flops 3308518912 | bytes 13768192 | tf_op jit(solution)/shard_map/rf,df->rd/dot_general | solution.py:33
  262.6 3.5 %fusion.15 = bf16[512,896]{1,0:T(8,128)(2,1)} fusion(bf16[1,4,128,896]{3,2,1,0:T(8,128)(2,1)} %param.11, f32[512,896]{1,0:T(8,128)} %get-tuple-element.8, f32[512]{0:T(512)S(1)} %broadcast_multiply_fusion, f32[512]{0:T(512)S(1)} %multiply_multiply_fusion.2, f32[896]{0:T(1024)S(1)} %copy-done.10, f32[512]{0:T(512)S(1)} %rsqrt_bitcast_fusion, ...), kind=kLoop, calls=%fused_computation.29 | loop fusion | flops 4128768 | bytes 4597248 | tf_op jit(solution)/shard_map/convert_element_type | solution.py:44
  266.1 44.5 %all-reduce.3.cloned.1.call-done = (bf16[896,256]{1,0:T(8,128)(2,1)}, bf16[896,256]{1,0:T(8,128)(2,1)}) async-done(((bf16[896,256]{1,0:T(8,128)(2,1)}, bf16[896,256]{1,0:T(8,128)(2,1)}), (bf16[896,256]{1,0:T(8,128)(2,1)}, bf16[896,256]{1,0:T(8,128)(2,1)})) %all-reduce.3.cloned.1.call-update) | async-done | bytes 917520 | tf_op jit(solution)/shard_map/psum | solution.py:158
  (74 shorter events, 34.2 us)
Async XLA Ops:
  7.2 4.4 %copy-start = (bf16[896,1792]{1,0:T(8,128)(2,1)S(1)}, bf16[896,1792]{1,0:T(8,128)(2,1)}, u32[]{:S(2)}) copy-start(bf16[896,1792]{1,0:T(8,128)(2,1)} %param.14) | copy-start | bytes 9633796
  7.2 93.1 %all-gather.3.cloned.1.call-start = ((), (), s32[]{:S(2)}) async-start(), calls=%async_computation.6 | async-start | bytes 4128768 | tf_op jit(solution)/shard_map/all_gather | solution.py:80
  7.9 117.5 %all-gather.5.cloned.1.call-start = ((), (), s32[]{:S(2)}) async-start(), calls=%async_computation.7 | async-start | bytes 4128768 | tf_op jit(solution)/shard_map/all_gather | solution.py:79
  11.6 2.1 copy-start.1
  11.6 2.2 copy-start.12
  13.8 2.3 copy-start.14
  16.1 7.3 %copy-start.13 = (s32[1,16]{1,0:T(1,128)S(1)}, s32[1,16]{1,0:T(1,128)}, u32[]{:S(2)}) copy-start(s32[1,16]{1,0:T(1,128)} %param.12) | copy-start | bytes 196
  17.1 51.8 %all-to-all-start = ((bf16[4,8,16,896]{3,2,0,1:T(8,128)(2,1)}), bf16[4,8,16,896]{3,2,0,1:T(8,128)(2,1)}, u32[]{:S(2)}, u32[]{:S(2)}) async-start(bf16[4,8,16,896]{3,2,0,1:T(8,128)(2,1)} %copy.89), calls=%async_computation | async-start | bytes 1835008 | tf_op jit(solution)/shard_map/all_to_all | solution.py:86
  73.6 24.8 %all-to-all-start.1 = ((bf16[8,2,16,896]{3,2,1,0:T(8,128)(2,1)}), bf16[8,2,16,896]{3,2,1,0:T(8,128)(2,1)}, u32[]{:S(2)}, u32[]{:S(2)}) async-start(bf16[8,2,16,896]{3,2,1,0:T(8,128)(2,1)} %bitcast.144), calls=%async_computation.1 | async-start | bytes 917504 | tf_op jit(solution)/shard_map/all_to_all | solution.py:88
  77.7 157.1 %reduce-scatter.3.cloned.1.call-start = ((), (), s32[]{:S(2)}) async-start(), calls=%async_computation.8 | async-start | bytes 4128768 | tf_op jit(solution)/shard_map/reduce_scatter | solution.py:150
  125.4 3.8 %copy-start.2 = (bf16[16,8,16,128]{3,2,1,0:T(8,128)(2,1)S(1)}, bf16[16,8,16,128]{3,2,1,0:T(8,128)(2,1)}, u32[]{:S(2)}) copy-start(bf16[16,8,16,128]{3,2,1,0:T(8,128)(2,1)} %copy.111) | copy-start | bytes 1572868
  128.9 2.6 copy-start.4
  128.9 2.6 copy-start.8
  129.2 1.0 copy-start.3
  130.1 1.3 copy-start.9
  139.5 1.0 copy-start.5
  144.6 108.8 %reduce-scatter.5.cloned.1.call-start = ((), (), s32[]{:S(2)}) async-start(), calls=%async_computation.9 | async-start | bytes 4128768 | tf_op jit(solution)/shard_map/reduce_scatter | solution.py:153
  150.2 1.1 copy-start.6
  155.2 3.9 %copy-start.7 = (bf16[2,128,16,128]{3,2,1,0:T(8,128)(2,1)S(1)}, bf16[2,128,16,128]{3,2,1,0:T(8,128)(2,1)}, u32[]{:S(2)}) copy-start(bf16[2,128,16,128]{3,2,1,0:T(8,128)(2,1)} %copy-done.6) | copy-start | bytes 3145732
  155.2 3.9 %copy-start.11 = (bf16[896,2048]{1,0:T(8,128)(2,1)S(1)}, bf16[896,2048]{1,0:T(8,128)(2,1)}, u32[]{:S(2)}) copy-start(bf16[896,2048]{1,0:T(8,128)(2,1)} %all-gather.3.cloned.1.call-done) | copy-start | bytes 11010052
  161.7 25.8 %all-to-all-start.2 = ((bf16[1,2,128,896]{3,1,0,2:T(2,128)(2,1)}), bf16[1,2,128,896]{3,1,0,2:T(2,128)(2,1)}, u32[]{:S(2)}, u32[]{:S(2)}) async-start(bf16[1,2,128,896]{3,1,0,2:T(2,128)(2,1)} %copy.105), calls=%async_computation.2 | async-start | bytes 917504 | tf_op jit(solution)/shard_map/all_to_all | solution.py:165
  194.2 38.5 %all-to-all-start.3 = ((bf16[4,8,16,896]{3,2,0,1:T(8,128)(2,1)}), bf16[4,8,16,896]{3,2,0,1:T(8,128)(2,1)}, u32[]{:S(2)}, u32[]{:S(2)}) async-start(bf16[4,8,16,896]{3,2,0,1:T(8,128)(2,1)} %copy_select_fusion), calls=%async_computation.3 | async-start | bytes 1835008 | tf_op jit(solution)/shard_map/all_to_all | solution.py:174
  198.5 112.2 %all-reduce.3.cloned.1.call-start = ((), (), s32[]{:S(2)}) async-start(), calls=%async_computation.10 | async-start | bytes 1835008 | tf_op jit(solution)/shard_map/psum | solution.py:158
  206.1 47.2 %copy-start.10 = (f32[896]{0:T(1024)S(1)}, f32[896]{0:T(1024)}, u32[]{:S(2)}) copy-start(f32[896]{0:T(1024)} %param.13) | copy-start | bytes 10756
Sparse Core Ops, SparseCore 0:
  9.6 65.1 all-gather.2
  76.4 49.0 all-gather.4
  144.7 52.6 reduce-scatter.2
  199.5 53.7 reduce-scatter.4
  256.3 54.2 all-reduce.2
where the time goes:
time: 323 us; the launch traced here: 321 us
  waiting for transfers between devices  187 us (58%)
  matrix products  51.3 us (16%)
  local copies, waits for them, and re-layouts  35.5 us (11%)
  starting transfers between devices  19.4 us (6%)
  other arithmetic  14.2 us (4%)
  between operations  14.1 us (4%)
    all_to_all x1, waiting for transfers between devices, on_device(): lax.all_to_all(pieces, 'seq', split_axis=1, concat_axis=1, tiled=True)  45.4 us
    psum x1, waiting for transfers between devices, on_device(): lax.psum(key_share.astype(jnp.bfloat16), 'dp').astype(jnp.float32)  44.5 us
    all_to_all x1, waiting for transfers between devices, on_device(): lax.all_to_all(encoded_grad.reshape(1, stretch_count, neighbour_span, fea...  21.3 us
    all_gather x1, waiting for transfers between devices, on_device(): lax.all_gather(key_weight, 'seq', axis=1, tiled=True)  20.4 us
    reduce_scatter x1, waiting for transfers between devices, on_device(): lax.psum_scatter(value_part.astype(jnp.bfloat16), 'seq', scatter_dimensio...  18.5 us
    all_to_all x1, waiting for transfers between devices, on_device(): lax.all_to_all(placed.reshape(holding, groups, piece_rows, feature_width)...  18.3 us
    all_to_all x1, waiting for transfers between devices, on_device(): lax.all_to_all(middle_rows.reshape(groups, stretch_count, piece_rows, fea...  16.8 us
    dot_general x1, matrix products, encode_backward(): jnp.einsum('rf,df->rd', before_grad, up_matrix, preferred_element_type=jn...  9.23 us
  transfers between devices with their start and end apart: 9, of which 7 were waited for; matrix products, arithmetic and copies ran while one was open for 24% of the time, Pallas kernels for 0%

commit v1 on v0

v1 whole, which is shorter than its diff:
```python
import functools
import math

import jax
import jax.numpy as jnp
from jax import lax
from jax.experimental import pallas as pl
from jax.experimental.pallas import tpu as pltpu
from jax.sharding import Mesh, PartitionSpec as P

STRETCH = 64
HD = 128
EPSILON = 1e-06
GELU_RATE = math.sqrt(2.0 / math.pi)
GELU_CUBE = 0.044715
VMEM_BYTES = 28 * 1024 * 1024
SMALL_VMEM_BYTES = 12 * 1024 * 1024
SEQ = ("z", "core")


def dot(left, right):
    return jnp.dot(left, right, preferred_element_type=jnp.float32)


def dot_nt(left, right):
    return lax.dot_general(left, right, (((1,), (1,)), ((), ())), preferred_element_type=jnp.float32)


def dot_tn(left, right):
    return lax.dot_general(left, right, (((0,), (0,)), ((), ())), preferred_element_type=jnp.float32)


def stated(microseconds):
    return pl.CostEstimate(
        flops=microseconds * 1_000_000_000, bytes_accessed=microseconds * 3_000_000, transcendentals=0
    )


def in_hbm(value):
    return pltpu.with_memory_space_constraint(value, pltpu.HBM)


def merge_rows(block):
    pieces, rows, width = block.shape
    if rows % 16 == 0:
        return block.reshape(pieces * rows, width)
    return block.astype(jnp.float32).reshape(pieces * rows, width).astype(jnp.bfloat16)


def inverse_of(row_values):
    return lax.rsqrt(jnp.mean(row_values * row_values, axis=-1, keepdims=True) + EPSILON)


def encode_kernel(slots, rows_ref, gain_ref, up_ref, down_ref, *refs):
    enc_ref, used_ref, slope_ref, normed, total = refs[-5:]
    step = pl.program_id(0)
    count, piece, width = used_ref.shape

    @pl.when(step == 0)
    def _():
        for g in range(count):
            used_ref[g] = rows_ref[slots[g]]
        row_values = used_ref[...].astype(jnp.float32).reshape(count * piece, width)
        normed[...] = (row_values * inverse_of(row_values) * gain_ref[...]).astype(jnp.bfloat16)
        total[...] = row_values

    before = dot(normed[...], up_ref[...])
    square = before * before
    bend = jnp.tanh(GELU_RATE * before * (1.0 + GELU_CUBE * square))
    half = 0.5 * (1.0 + bend)
    activity = (before * half).astype(jnp.bfloat16)
    slope = half + 0.5 * before * (1.0 - bend * bend) * (
        GELU_RATE * (1.0 + 3.0 * GELU_CUBE * square)
    )
    slope_ref[...] = slope.astype(slope_ref.dtype)
    total[...] += dot(activity, down_ref[...])

    @pl.when(step == pl.num_programs(0) - 1)
    def _():
        enc_ref[...] = total[...].reshape(count, piece, width).astype(jnp.bfloat16)


def encode_rows(slots, rows, gain, up, down, after):
    count = slots.shape[0]
    piece, width = rows.shape[1:]
    hidden = up.shape[1]
    chunk = hidden // 2
    whole = lambda *shape: pl.BlockSpec(shape, lambda f, s: (0,) * len(shape))
    return pl.pallas_call(
        encode_kernel,
        grid_spec=pltpu.PrefetchScalarGridSpec(
            num_scalar_prefetch=1,
            grid=(hidden // chunk,),
            in_specs=[
                whole(*rows.shape),
                whole(1, width),
                pl.BlockSpec((width, chunk), lambda f, s: (0, f)),
                pl.BlockSpec((chunk, width), lambda f, s: (f, 0)),
            ]
            + [pl.BlockSpec(memory_space=pl.ANY)] * len(after),
            out_specs=[
                whole(count, piece, width),
                whole(count, piece, width),
                pl.BlockSpec((count * piece, chunk), lambda f, s: (0, f)),
            ],
            scratch_shapes=[
                pltpu.VMEM((count * piece, width), jnp.bfloat16),
                pltpu.VMEM((count * piece, width), jnp.float32),
            ],
        ),
        out_shape=[
            pltpu.HBM((count, piece, width), jnp.bfloat16),
            pltpu.HBM((count, piece, width), jnp.bfloat16),
            pltpu.HBM((count * piece, hidden), jnp.bfloat16),
        ],
        compiler_params=pltpu.CompilerParams(vmem_limit_bytes=VMEM_BYTES),
        cost_estimate=pl.CostEstimate(
            flops=4 * count * piece * width * hidden,
            bytes_accessed=2 * rows.size + 4 * width * hidden + 8 * count * piece * width,
            transcendentals=count * piece * hidden,
        ),
    )(slots, rows, gain, up, in_hbm(down), *after)


def back_kernel(slots, grad_ref, used_ref, slope_ref, gain_ref, up_ref, down_ref, *refs):
    out_ref, total = refs[-2:]
    step = pl.program_id(0)
    count, piece, width = used_ref.shape
    grads = merge_rows(grad_ref[...])

    @pl.when(step == 0)
    def _():
        out_ref[...] = jnp.zeros_like(out_ref)
        total[...] = jnp.zeros_like(total)

    activity_grad = dot_nt(grads, down_ref[...])
    before_grad = (activity_grad * slope_ref[...]).astype(jnp.bfloat16)
    total[...] += dot_nt(before_grad, up_ref[...])

    @pl.when(step == pl.num_programs(0) - 1)
    def _():
        row_values = used_ref[...].astype(jnp.float32).reshape(count * piece, width)
        inverse = inverse_of(row_values)
        scaled = gain_ref[...] * total[...]
        result = (
            grads.astype(jnp.float32)
            + inverse * scaled
            - row_values
            * (inverse * inverse * inverse)
            * jnp.mean(row_values * scaled, axis=-1, keepdims=True)
        )
        result = result.reshape(count, piece, width).astype(jnp.bfloat16)
        for g in range(count):
            out_ref[slots[g]] = result[g]


def encode_back(slots, grads, used, slope, gain, up, down, slot_count, after):
    count, piece, width = used.shape
    hidden = up.shape[1]
    chunk = hidden // 2
    whole = lambda *shape: pl.BlockSpec(shape, lambda f, s: (0,) * len(shape))
    return pl.pallas_call(
        back_kernel,
        grid_spec=pltpu.PrefetchScalarGridSpec(
            num_scalar_prefetch=1,
            grid=(hidden // chunk,),
            in_specs=[
                whole(count, piece, width),
                whole(count, piece, width),
                pl.BlockSpec((count * piece, chunk), lambda f, s: (0, f)),
                whole(1, width),
                pl.BlockSpec((width, chunk), lambda f, s: (0, f)),
                pl.BlockSpec((chunk, width), lambda f, s: (f, 0)),
            ]
            + [pl.BlockSpec(memory_space=pl.ANY)] * len(after),
            out_specs=whole(slot_count, piece, width),
            scratch_shapes=[pltpu.VMEM((count * piece, width), jnp.float32)],
        ),
        out_shape=pltpu.HBM((slot_count, piece, width), jnp.bfloat16),
        compiler_params=pltpu.CompilerParams(vmem_limit_bytes=VMEM_BYTES),
        cost_estimate=pl.CostEstimate(
            flops=4 * count * piece * width * hidden,
            bytes_accessed=4 * width * hidden + 8 * count * piece * width + 2 * count * piece * hidden,
            transcendentals=0,
        ),
    )(slots, grads, in_hbm(used), in_hbm(slope), gain, up, in_hbm(down), *after)


def attend_kernel(kinds, lines, last, plan, *refs):
    refs = list(refs)
    take = lambda count: [refs.pop(0) for _ in range(count)]
    steps = len(kinds)
    own_enc, other_enc = take(2)
    token_refs = (take(2), take(2))
    weight_refs = [take({"whole": 1, "columns": 2, "rows": lines}[kind]) for kind in kinds]
    if last:
        (back_in,) = take(1)
        take(4)
    out_refs = (take(2), take(2))
    back_refs = take(2 if last else 1)
    grad_halves = take(2)
    rows, rows_t, back, weight = refs
    step = pl.program_id(0)
    shares, mine, piece, width = own_enc.shape
    span = shares * piece
    scale = 1.0 / math.sqrt(HD)
    part_rows, columns = width // lines, weight.shape[1] // 2

    @pl.when(step == 0)
    def _():
        for s in range(2 * mine):
            source = own_enc if s < mine else other_enc
            rows[s * span : (s + 1) * span, :] = merge_rows(source[:, s % mine])
        rows_t[...] = rows[...].T
        back[...] = back_in[...] if last else jnp.zeros_like(back)

    for shard, (kind, found) in enumerate(zip(kinds, weight_refs)):

        @pl.when(step == shard)
        def _(kind=kind, found=found):
            if kind == "whole":
                weight[...] = found[0][...]
            elif kind == "columns":
                weight[:, :columns] = found[0][...]
                weight[:, columns:] = found[1][...]
            else:
                for i in range(lines):
                    start = pl.multiple_of(plan[steps + i] * part_rows, 16)
                    weight[pl.ds(start, part_rows), :] = found[i][...]

    both = dot(rows[...], weight[...]).astype(jnp.bfloat16)
    pairs = [(s, h) for s in range(2 * mine) for h in range(columns // HD)]

    def tokens_of(s, h):
        tokens = slice((s % mine) * STRETCH, (s % mine + 1) * STRETCH)
        return s // mine, tokens, slice(h * HD, (h + 1) * HD)

    def token_block(kind, s, h):
        side, tokens, cols = tokens_of(s, h)
        return token_refs[side][kind][tokens, cols]

    query = [token_block(0, s, h) for s, h in pairs]
    grad = [token_block(1, s, h) for s, h in pairs]
    key = [both[s * span : (s + 1) * span, h * HD : (h + 1) * HD] for s, h in pairs]
    value = [
        both[s * span : (s + 1) * span, columns + h * HD : columns + (h + 1) * HD] for s, h in pairs
    ]
    count = range(len(pairs))
    scores = jnp.concatenate([dot_nt(query[i], key[i]) for i in count], axis=0)
    prob_grad = jnp.concatenate([dot_nt(grad[i], value[i]) for i in count], axis=0)
    exponent = jnp.exp(scores * scale)
    weights = exponent * (1.0 / jnp.sum(exponent, axis=-1, keepdims=True))
    mean_grad = jnp.sum(weights * prob_grad, axis=-1, keepdims=True)
    probabilities = weights.astype(jnp.bfloat16)
    score_grad = (weights * (prob_grad - mean_grad) * scale).astype(jnp.bfloat16)
    prob = [probabilities[i * STRETCH : (i + 1) * STRETCH] for i in count]
    score = [score_grad[i * STRETCH : (i + 1) * STRETCH] for i in count]
    for i, (s, h) in enumerate(pairs):
        side, tokens, cols = tokens_of(s, h)
        out_refs[side][0][tokens, cols] = dot(prob[i], value[i]).astype(jnp.bfloat16)
        out_refs[side][1][tokens, cols] = dot(score[i], key[i]).astype(jnp.bfloat16)
    key_grad = [dot_tn(score[i], query[i]).astype(jnp.bfloat16) for i in count]
    value_grad = [dot_tn(prob[i], grad[i]).astype(jnp.bfloat16) for i in count]
    heads = columns // HD
    both_grad = jnp.concatenate(
        [
            jnp.concatenate(
                key_grad[s * heads : (s + 1) * heads] + value_grad[s * heads : (s + 1) * heads], axis=1
            )
            for s in range(2 * mine)
        ],
        axis=0,
    )
    for i in range(lines):
        start = pl.multiple_of(plan[steps + i] * part_rows, 16)
        part_grad = dot(rows_t[pl.ds(start, part_rows), :], both_grad).astype(jnp.bfloat16)
        grad_halves[2 * i // lines][i % (lines // 2), 0] = part_grad
    back[...] += dot_nt(both_grad, weight[...])

    @pl.when(step == steps - 1)
    def _():
        if not last:
            back_refs[0][...] = back[...]
        else:
            for s in range(2 * mine):
                block = back[s * span : (s + 1) * span, :].reshape(shares, piece, width)
                back_refs[s // mine][:, s % mine] = block.astype(jnp.bfloat16)


def attend(plan, lines, own_enc, other_enc, token_arrays, shards, earlier=None):
    last = earlier is not None
    steps = len(shards)
    kinds, arrays = [kind for kind, _ in shards], sum([found for _, found in shards], [])
    shares, mine, piece, width = own_enc.shape
    tokens, all_columns = token_arrays[0].shape
    columns = all_columns // shares
    part_rows = width // lines
    span = shares * piece
    all_rows = 2 * mine * span
    whole = lambda *shape: pl.BlockSpec(shape, lambda j, p: (0,) * len(shape))
    token_spec = pl.BlockSpec((tokens, columns), lambda j, p: (0, p[j]))
    enc_spec = whole(*own_enc.shape)
    out = functools.partial(jax.ShapeDtypeStruct, dtype=jnp.bfloat16)
    operands = [plan, own_enc, other_enc, *map(in_hbm, token_arrays), *arrays]
    in_specs = [enc_spec] * 2 + [token_spec] * 4 + [whole(*value.shape) for value in arrays]
    back_shapes, aliases = [jax.ShapeDtypeStruct((all_rows, width), jnp.float32)], {}
    if last:
        aliases = {len(operands) + 1 + i: i for i in range(4)}
        operands += [earlier[4], *map(in_hbm, earlier[:4])]
        in_specs += [whole(all_rows, width)] + [pl.BlockSpec(memory_space=pl.ANY)] * 4
        back_shapes = [out(own_enc.shape)] * 2
    return pl.pallas_call(
        functools.partial(attend_kernel, kinds, lines, last),
        grid_spec=pltpu.PrefetchScalarGridSpec(
            num_scalar_prefetch=1,
            grid=(steps,),
            in_specs=in_specs,
            out_specs=[token_spec] * 4
            + [whole(*shape.shape) for shape in back_shapes]
            + [pl.BlockSpec((lines // 2, 1, part_rows, 2 * columns), lambda j, p: (0, j, 0, 0))] * 2,
            scratch_shapes=[
                pltpu.VMEM((all_rows, width), jnp.bfloat16),
                pltpu.VMEM((width, all_rows), jnp.bfloat16),
                pltpu.VMEM((all_rows, width), jnp.float32),
                pltpu.VMEM((width, 2 * columns), jnp.bfloat16),
            ],
        ),
        out_shape=[pltpu.HBM((tokens, all_columns), jnp.bfloat16)] * 4
        + back_shapes
        + [pltpu.HBM((lines // 2, steps, part_rows, 2 * columns), jnp.bfloat16)] * 2,
        input_output_aliases=aliases,
        compiler_params=pltpu.CompilerParams(vmem_limit_bytes=VMEM_BYTES),
        cost_estimate=pl.CostEstimate(
            flops=12 * all_rows * width * steps * columns,
            bytes_accessed=8 * width * steps * columns + 8 * own_enc.size + 16 * tokens * steps * columns,
            transcendentals=2 * mine * STRETCH * span * steps * columns // HD,
        ),
    )(*operands)


def sum_kernel(count, sizes, *refs):
    terms, outs = refs[:count], refs[len(refs) - len(sizes) :]
    block = 0
    for size, out in zip(sizes, outs):
        for i in range(size):
            total = terms[0][block].astype(jnp.float32)
            for term in terms[1:]:
                total = total + term[block].astype(jnp.float32)
            out[i] = total.astype(jnp.bfloat16)
            block += 1


def sum_blocks(terms, sizes, after=(), to_hbm=False):
    blocks, rows, columns = terms[0].shape
    tiles = 2 if rows % 32 == 0 else 1
    spec = lambda size: pl.BlockSpec((size, rows // tiles, columns), lambda i: (0, i, 0))
    return pl.pallas_call(
        functools.partial(sum_kernel, len(terms), sizes),
        grid=(tiles,),
        in_specs=[spec(blocks)] * len(terms) + [pl.BlockSpec(memory_space=pl.ANY)] * len(after),
        out_specs=[spec(size) for size in sizes],
        out_shape=[
            (pltpu.HBM if to_hbm else jax.ShapeDtypeStruct)((size, rows, columns), jnp.bfloat16)
            for size in sizes
        ],
        compiler_params=pltpu.CompilerParams(vmem_limit_bytes=SMALL_VMEM_BYTES),
        cost_estimate=pl.CostEstimate(
            flops=len(terms) * blocks * rows * columns,
            bytes_accessed=2 * (len(terms) + 1) * blocks * rows * columns,
            transcendentals=0,
        ),
    )(*terms, *after)


def join_kernel(count, plan, *refs):
    parts, outs = refs[:count], refs[count:]
    part_rows, columns = parts[0].shape[0], outs[0].shape[1]
    for i, part in enumerate(parts):
        start = pl.multiple_of(plan[i] * part_rows, 16)
        for k, out in enumerate(outs):
            out[pl.ds(start, part_rows), :] = part[:, k * columns : (k + 1) * columns].astype(out.dtype)


def join_parts(plan, parts, outs, dtype, microseconds):
    part_rows, columns = parts[0].shape
    width = part_rows * len(parts)
    whole = lambda *shape: pl.BlockSpec(shape, lambda j, p: (0,) * len(shape))
    return pl.pallas_call(
        functools.partial(join_kernel, len(parts)),
        grid_spec=pltpu.PrefetchScalarGridSpec(
            num_scalar_prefetch=1,
            grid=(1,),
            in_specs=[whole(part_rows, columns)] * len(parts),
            out_specs=[whole(width, columns // outs)] * outs,
        ),
        out_shape=[jax.ShapeDtypeStruct((width, columns // outs), dtype)] * outs,
        compiler_params=pltpu.CompilerParams(vmem_limit_bytes=SMALL_VMEM_BYTES),
        cost_estimate=stated(microseconds),
    )(plan, *parts)


def swap_cores(value):
    return lax.ppermute(value, "core", [(0, 1), (1, 0)])


def swap_chips(value, shift):
    return lax.ppermute(value, "z", [(z, z ^ shift) for z in range(lax.axis_size("z"))])


def line_bit(core, stage, stages):
    return 1 << stage if core == 0 else 1 << (stages - 1 - stage)


def swap_lines(value, stage, stages):
    lines = lax.axis_size("line")
    pairs = [
        (line * 2 + core, (line ^ line_bit(core, stage, stages)) * 2 + core)
        for line in range(lines)
        for core in range(2)
    ]
    return lax.ppermute(value, ("line", "core"), pairs)


def gather_lines(value, stages):
    found = [value]
    for stage in range(stages):
        found = found + [swap_lines(item, stage, stages) for item in found]
    return found


def on_device(
    queries,
    attended_grad,
    neighbour_pool,
    stretch_slot,
    enc_gain,
    enc_up,
    enc_down,
    key_weight,
    value_weight,
):
    chips, lines = lax.axis_size("z"), lax.axis_size("line")
    stages = lines.bit_length() - 1
    groups = 2 * chips
    core, chip, line = lax.axis_index("core"), lax.axis_index("z"), lax.axis_index("line")
    tokens, all_columns = queries.shape[1:]
    mine = tokens // STRETCH
    holding, span, width = neighbour_pool.shape[1:]
    piece = span // groups
    columns = key_weight.shape[1]
    slots = stretch_slot[0]
    gain = enc_gain.reshape(1, width)

    offsets = [
        [sum(line_bit(c, s, stages) for s in range(stages) if i >> s & 1) for i in range(lines)]
        for c in range(2)
    ]
    part_lines = line ^ jnp.where(
        core == 0, jnp.array(offsets[0], jnp.int32), jnp.array(offsets[1], jnp.int32)
    )
    part_lines = part_lines.astype(jnp.int32)

    part_rows = width // lines
    part = jnp.concatenate(
        [
            lax.dynamic_slice_in_dim(weight, line * part_rows, part_rows, 0)
            for weight in (key_weight, value_weight)
        ],
        axis=1,
    )
    odd, even = range(1, chips, 2), range(2, chips, 2)
    part = {0: part}
    shift = chips // 2
    while shift > 1:
        part |= {s | shift: swap_chips(value, shift) for s, value in part.items()}
        shift //= 2
    part[1] = swap_chips(part[0], 1)

    pieces = neighbour_pool[0].reshape(holding, groups, piece, width).transpose(1, 0, 2, 3)
    received = lax.all_to_all(pieces, SEQ, split_axis=0, concat_axis=0, tiled=True)
    received = received.reshape(groups * holding, piece, width)

    token_arrays = [queries[0], attended_grad[0]]
    token_arrays += [swap_cores(value) for value in token_arrays]

    encoded, used, slope = encode_rows(slots, received, gain, enc_up, enc_down, [])
    encoded, part = lax.optimization_barrier((encoded, part))
    part |= {s | 1: swap_chips(part[s], 1) for s in even}
    own_enc = lax.all_to_all(
        encoded.reshape(groups, mine, piece, width), SEQ, split_axis=0, concat_axis=0, tiled=True
    )
    shards = {0: ("columns", [in_hbm(key_weight), in_hbm(value_weight)])}
    for shift in range(1, chips):
        found = gather_lines(part[shift], stages)
        if shift == 1 or shift in even:
            shards[shift] = ("whole", [*join_parts(part_lines, found, 1, jnp.bfloat16, 4)])
        else:
            shards[shift] = ("rows", found)
    other_enc = swap_cores(own_enc)

    steps = ([0, *even], [*odd])
    plans = [
        jnp.concatenate([jnp.stack([(chip ^ shift) * 2 + core for shift in shifts]), part_lines])
        for shifts in steps
    ]
    parted = [[shards[shift] for shift in shifts] for shifts in steps]
    first = attend(plans[0], lines, own_enc, other_enc, token_arrays, parted[0])
    last = attend(plans[1], lines, own_enc, other_enc, token_arrays, parted[1], first[:5])
    outs, own_back, other_back = last[:4], last[4], last[5]

    rows = groups * mine * piece
    (back,) = sum_blocks(
        [own_back.reshape(1, rows, width), swap_cores(other_back).reshape(1, rows, width)],
        (1,),
        to_hbm=True,
    )
    split_rows = lax.all_to_all(
        back.reshape(groups, mine, piece, width), SEQ, split_axis=0, concat_axis=0, tiled=True
    )

    count = chips // 2
    first_halves = [first[5], swap_lines(first[6], stages - 1, stages)]
    last_halves = [last[6], swap_lines(last[7], stages - 1, stages)]
    after = [in_hbm(back)]
    for stage in reversed(range(stages)):
        size = first_halves[0].size // (part_rows * 2 * columns)
        sizes = (size // 2, size // 2) if stage else (1,) * count
        flat = lambda halves: [value.reshape(size, part_rows, 2 * columns) for value in halves]
        first_flat, last_flat = flat(first_halves), flat(last_halves)
        if stage == stages - 1:
            first_flat[0], last_flat[0] = in_hbm(first_flat[0]), in_hbm(last_flat[0])
        first_sums = sum_blocks(first_flat, sizes, after)
        last_sums = sum_blocks(last_flat, sizes, [first_sums[0]])
        after = [last_sums[0]]
        if stage:
            first_halves = [first_sums[0], swap_lines(first_sums[1], stage - 1, stages)]
            last_halves = [last_sums[0], swap_lines(last_sums[1], stage - 1, stages)]
    terms = {0: first_sums[0]}
    terms |= {shift: swap_chips(value, shift) for value, shift in zip(first_sums[1:], even)}
    terms |= {shift: swap_chips(value, shift) for value, shift in zip(last_sums, odd)}
    placed = encode_back(
        slots,
        split_rows.reshape(groups * mine, piece, width),
        used,
        slope,
        gain,
        enc_up,
        enc_down,
        groups * holding,
        [],
    )
    (share,) = sum_blocks([*terms.values()], (1,), [in_hbm(placed)])
    share = share[0]
    if lax.axis_size("far") > 1:
        share = lax.psum(share, "far")
    weight_grads = join_parts(part_lines, gather_lines(share, stages), 2, jnp.float32, 10)

    returned = lax.all_to_all(
        placed.reshape(groups, holding, piece, width), SEQ, split_axis=0, concat_axis=0, tiled=True
    )
    pool_grad = returned.transpose(1, 0, 2, 3).reshape(1, holding, span, width)

    is_own = (lax.broadcasted_iota(jnp.int32, (1, all_columns), 1) // columns) % 2 == core
    outs = [jnp.where(is_own, outs[i], swap_cores(outs[2 + i]))[None] for i in range(2)]
    return outs[0], outs[1], pool_grad, weight_grads[0], weight_grads[1]


def solution(mesh):
    dp, seq = mesh.shape["dp"], mesh.shape["seq"]
    lines = 4 if dp % 4 == 0 else dp
    fine = Mesh(
        mesh.devices.reshape(dp // lines, lines, seq // 2, 2), ("far", "line", "z", "core")
    )
    dp_axes = ("far", "line")
    return jax.shard_map(
        on_device,
        mesh=fine,
        in_specs=(
            P(dp_axes, SEQ, None),
            P(dp_axes, SEQ, None),
            P(dp_axes, SEQ, None, None),
            P(dp_axes, None),
            P(),
            P(),
            P(),
            P(None, SEQ),
            P(None, SEQ),
        ),
        out_specs=(
            P(dp_axes, SEQ, None),
            P(dp_axes, SEQ, None),
            P(dp_axes, SEQ, None, None),
            P(None, SEQ),
            P(None, SEQ),
        ),
        check_vma=False,
    )
```

time: 323 us -> 175 us (0.54)
  waiting for transfers between devices: 187 us -> 66.2 us
  matrix products: 51.3 us -> 0 us
  Pallas kernels: 0 us -> 43.8 us
  starting transfers between devices: 19.4 us -> 53.1 us
  local copies, waits for them, and re-layouts: 35.5 us -> 8.31 us
  between operations: 14.1 us -> 0.81 us
  other arithmetic: 14.2 us -> 2.38 us
    all_to_all x4, waiting for transfers between devices: 102 us -> 32.3 us  [the longest x1 18.9 us: on_device(): lax.all_to_all(pieces, SEQ, split_axis=0, concat_axis=0, tiled=True)]
    dot_general x15 -> x0, matrix products: 51.3 us -> none  [the longest x1 9.23 us: encode_backward(): jnp.einsum('rf,df->rd', before_grad, up_matrix, preferred_element_type=jn...]
    psum x1 -> x0, waiting for transfers between devices: 44.5 us -> none  [on_device(): lax.psum(key_share.astype(jnp.bfloat16), 'dp').astype(jnp.float32)]
    pallas_call x0 -> x13, Pallas kernels: none -> 43.8 us  [the longest x2 18.3 us: attend(): pl.pallas_call(functools.partial(attend_kernel, kinds, lines, last), grid...]
    ppermute x0 -> x28, waiting for transfers between devices: none -> 34 us  [the longest x16 16.9 us: swap_lines(): return lax.ppermute(value, ('line', 'core'), pairs)]
    ppermute x0 -> x28, starting transfers between devices: none -> 33.8 us  [the longest x16 22.5 us: swap_lines(): return lax.ppermute(value, ('line', 'core'), pairs)]
    all_gather x2 -> x0, waiting for transfers between devices: 20.4 us -> none  [the longest x1 20.4 us: on_device(): lax.all_gather(key_weight, 'seq', axis=1, tiled=True)]
    reduce_scatter x2 -> x0, waiting for transfers between devices: 18.5 us -> none  [the longest x1 18.5 us: on_device(): lax.psum_scatter(value_part.astype(jnp.bfloat16), 'seq', scatter_dimensio...]
  transfers between devices with their start and end apart: 9 -> 32, of which waited for: 7 -> 13; matrix products, arithmetic and copies ran while one was open for 24% -> 2% of each run, Pallas kernels for 0% -> 25%
where the time goes in v1:
time: 175 us
  waiting for transfers between devices  66.2 us (38%)
  starting transfers between devices  53.1 us (30%)
  Pallas kernels  43.8 us (25%)
  local copies, waits for them, and re-layouts  8.31 us (5%)
  other arithmetic  2.38 us (1%)
    ppermute x16, starting transfers between devices, swap_lines(): return lax.ppermute(value, ('line', 'core'), pairs)  22.5 us
    all_to_all x1, waiting for transfers between devices, on_device(): lax.all_to_all(pieces, SEQ, split_axis=0, concat_axis=0, tiled=True)  18.9 us
    pallas_call x2, Pallas kernels, attend(): pl.pallas_call(functools.partial(attend_kernel, kinds, lines, last), grid...  18.3 us
    ppermute x16, waiting for transfers between devices, swap_lines(): return lax.ppermute(value, ('line', 'core'), pairs)  16.9 us
    ppermute x6, waiting for transfers between devices, swap_chips(): lax.ppermute(value, 'z', [(z, z ^ shift) for z in range(lax.axis_size('z'...  15.3 us
    all_to_all x1, waiting for transfers between devices, on_device(): lax.all_to_all(placed.reshape(groups, holding, piece, width), SEQ, split_...  13.4 us
    ppermute x6, starting transfers between devices, swap_chips(): lax.ppermute(value, 'z', [(z, z ^ shift) for z in range(lax.axis_size('z'...  10.8 us
    pallas_call x6, Pallas kernels, sum_blocks(): pl.pallas_call(functools.partial(sum_kernel, len(terms), sizes), grid=(ti...  7.01 us
  transfers between devices with their start and end apart: 32, of which 13 were waited for; matrix products, arithmetic and copies ran while one was open for 2% of the time, Pallas kernels for 25%

profile of v1, /device:TPU:0, one launch (start us, length us, event | category | flops | bytes accessed | tf_op | source)
XLA Modules:
  0.0 174.7 jit_solution(10995921094140676908)
XLA Ops:
  0.7 2.3 %copy.23 = bf16[4,8,16,896]{3,2,0,1:T(8,128)(2,1)} copy(bf16[4,8,16,896]{3,2,1,0:T(8,128)(2,1)} %bitcast.40) | data formatting | bytes 1835008 | tf_op jit(solution)/shard_map/reshape;squeeze | solution.py:479
  3.0 6.3 %all-to-all-start = ((bf16[8,4,16,896]{3,2,1,0:T(8,128)(2,1)}), bf16[8,4,16,896]{3,2,1,0:T(8,128)(2,1)}, u32[]{:S(2)}, u32[]{:S(2)}) async-start(bf16[8,4,16,896]{3,2,1,0:T(8,128)(2,1)} %bitcast.39), calls=%async_computation | async-start | bytes 1835008 | tf_op jit(solution)/shard_map/all_to_all | solution.py:480
  10.3 2.1 %collective-permute-start = (bf16[224,512]{1,0:T(8,128)(2,1)S(1)}, bf16[224,512]{1,0:T(8,128)(2,1)}, u32[]{:S(2)}, u32[]{:S(2)}) collective-permute-start(bf16[224,512]{1,0:T(8,128)(2,1)S(1)} %pad_maximum_fusion), channel_id=1, source_target_pairs={{0,2},{2,0},{4,6},{6,4},{1,3},{3,1},{5,7},{7,5},{8,10},{10,8},{12,... | collective-permute-start | bytes 688136 | tf_op jit(solution)/shard_map/ppermute | solution.py:407
  12.4 2.4 %collective-permute-start.1 = (bf16[224,512]{1,0:T(8,128)(2,1)S(1)}, bf16[224,512]{1,0:T(8,128)(2,1)}, u32[]{:S(2)}, u32[]{:S(2)}) collective-permute-start(bf16[224,512]{1,0:T(8,128)(2,1)S(1)} %pad_maximum_fusion), channel_id=1, source_target_pairs={{0,4},{2,6},{4,0},{6,2},{1,5},{3,7},{5,1},{7,3},{8,12},{10,14},{12... | collective-permute-start | bytes 688136 | tf_op jit(solution)/shard_map/ppermute | solution.py:407
  14.8 18.9 %all-to-all-done = bf16[8,4,16,896]{3,2,1,0:T(8,128)(2,1)} async-done(((bf16[8,4,16,896]{3,2,1,0:T(8,128)(2,1)}), bf16[8,4,16,896]{3,2,1,0:T(8,128)(2,1)}, u32[]{:S(2)}, u32[]{:S(2)}) %all-to-all-start) | async-done | bytes 917536 | tf_op jit(solution)/shard_map/all_to_all | solution.py:480
  33.7 6.8 %shard_map.146 = (bf16[16,16,896]{2,1,0:T(8,128)(2,1)}, bf16[16,16,896]{2,1,0:T(8,128)(2,1)}, bf16[256,1792]{1,0:T(8,128)(2,1)}) custom-call(s32[16]{0:T(128)S(1)} %bitcast.34, bf16[32,16,896]{2,1,0:T(8,128)(2,1)} %bitcast.5.rows_ref, f32[1,896]{1,0:T(1,128)S(1)} %reshape.106.gain_ref, bf16[896,1792]{1,0:T(8,128)(2,1)S(1)} %copy-done, bf16[1792,896]{1,0:T(8,128)(2,1)} %down_ref.3), custom_call_target="tpu_custom_call" | custom-call | flops 1644167168 | bytes 9175040 | tf_op jit(solution)/shard_map/pallas_call | solution.py:89
  40.5 2.6 %collective-permute-done.1.refs_0_ = bf16[224,512]{1,0:T(8,128)(2,1)} collective-permute-done((bf16[224,512]{1,0:T(8,128)(2,1)S(1)}, bf16[224,512]{1,0:T(8,128)(2,1)}, u32[]{:S(2)}, u32[]{:S(2)}) %collective-permute-start.1) | collective-permute-done | bytes 229408 | tf_op jit(solution)/shard_map/ppermute | solution.py:407
  43.1 4.1 %all-to-all-start.1 = ((bf16[8,2,16,896]{3,2,1,0:T(8,128)(2,1)}), bf16[8,2,16,896]{3,2,1,0:T(8,128)(2,1)}, u32[]{:S(2)}, u32[]{:S(2)}) async-start(bf16[8,2,16,896]{3,2,1,0:T(8,128)(2,1)} %bitcast.44), calls=%async_computation.1 | async-start | bytes 917504 | tf_op jit(solution)/shard_map/all_to_all | solution.py:489
  53.1 2.4 %collective-permute-done.12.refs_1_ = bf16[224,512]{1,0:T(8,128)(2,1)} collective-permute-done((bf16[224,512]{1,0:T(8,128)(2,1)}, bf16[224,512]{1,0:T(8,128)(2,1)}, u32[]{:S(2)}, u32[]{:S(2)}) %collective-permute-start.12) | collective-permute-done | bytes 229408 | tf_op jit(solution)/shard_map/ppermute | solution.py:421
  55.5 2.0 %collective-permute-start.14 = (bf16[224,512]{1,0:T(8,128)(2,1)}, bf16[224,512]{1,0:T(8,128)(2,1)S(1)}, u32[]{:S(2)}, u32[]{:S(2)}) collective-permute-start(bf16[224,512]{1,0:T(8,128)(2,1)} %collective-permute-done.12.refs_1_), channel_id=1, source_target_pairs={{0,16},{1,9},{8,24},{9,1},{16,0},{17,25},{24,8},{25,17},{2,18},{3,... | collective-permute-start | bytes 688136 | tf_op jit(solution)/shard_map/ppermute | solution.py:421
  58.3 2.2 %collective-permute-done.5.refs_1_ = bf16[224,512]{1,0:T(8,128)(2,1)} collective-permute-done((bf16[224,512]{1,0:T(8,128)(2,1)}, bf16[224,512]{1,0:T(8,128)(2,1)}, u32[]{:S(2)}, u32[]{:S(2)}) %collective-permute-start.5) | collective-permute-done | bytes 229408 | tf_op jit(solution)/shard_map/ppermute | solution.py:421
  61.1 2.0 %collective-permute-start.7 = (bf16[224,512]{1,0:T(8,128)(2,1)}, bf16[224,512]{1,0:T(8,128)(2,1)}, u32[]{:S(2)}, u32[]{:S(2)}) collective-permute-start(bf16[224,512]{1,0:T(8,128)(2,1)} %collective-permute-done.5.refs_1_), channel_id=1, source_target_pairs={{0,16},{1,9},{8,24},{9,1},{16,0},{17,25},{24,8},{25,17},{2,18},{3,... | collective-permute-start | bytes 688136 | tf_op jit(solution)/shard_map/ppermute | solution.py:421
  69.0 2.2 %collective-permute-start.10 = (bf16[224,512]{1,0:T(8,128)(2,1)}, bf16[224,512]{1,0:T(8,128)(2,1)S(1)}, u32[]{:S(2)}, u32[]{:S(2)}) collective-permute-start(bf16[224,512]{1,0:T(8,128)(2,1)} %collective-permute-done.8.refs_7_), channel_id=1, source_target_pairs={{0,16},{1,9},{8,24},{9,1},{16,0},{17,25},{24,8},{25,17},{2,18},{3,... | collective-permute-start | bytes 688136 | tf_op jit(solution)/shard_map/ppermute | solution.py:421
  73.2 9.2 %shard_map.149 = (bf16[128,2048]{1,0:T(8,128)(2,1)}, bf16[128,2048]{1,0:T(8,128)(2,1)}, bf16[128,2048]{1,0:T(8,128)(2,1)}, bf16[128,2048]{1,0:T(8,128)(2,1)}, f3...) custom-call(s32[6]{0:T(128)S(1)} %get-tuple-element.69.plan, ...), custom_call_target="tpu_custom_call" | custom-call | flops 2818572288 | bytes 6553600 | tf_op jit(solution)/shard_map/pallas_call | solution.py:312
  82.4 1.8 %collective-permute-start.18 = (bf16[2,2,224,512]{3,2,1,0:T(8,128)(2,1)}, bf16[2,2,224,512]{3,2,1,0:T(8,128)(2,1)}, u32[]{:S(2)}, u32[]{:S(2)}) collective-permute-start(bf16[2,2,224,512]{3,2,1,0:T(8,128)(2,1)} %get-tuple-element.54), channel_id=1, source_target_pairs={{0,16},{1,9},{8,24},{9,1},{16,0},{17,25},{24,8},{25,17},{2,18},{3,... | collective-permute-start | bytes 2752520 | tf_op jit(solution)/shard_map/ppermute | solution.py:421
  84.3 9.1 %shard_map.150 = (bf16[128,2048]{1,0:T(8,128)(2,1)}, bf16[128,2048]{1,0:T(8,128)(2,1)}, bf16[128,2048]{1,0:T(8,128)(2,1)}, bf16[128,2048]{1,0:T(8,128)(2,1)}, bf...) custom-call(s32[6]{0:T(128)S(1)} %get-tuple-element.70.plan, ...), custom_call_target="tpu_custom_call", output_to_operand_aliasing={{0}: (13, {}), {1}: (14, {}), {2}: (15, {}), {3}: (16, {})} | custom-call | flops 2818572288 | bytes 6553600 | tf_op jit(solution)/shard_map/pallas_call | solution.py:312
  96.3 5.0 %all-to-all-start.2 = ((bf16[8,2,16,896]{3,2,1,0:T(8,128)(2,1)}), bf16[8,2,16,896]{3,2,1,0:T(8,128)(2,1)}, u32[]{:S(2)}, u32[]{:S(2)}) async-start(bf16[8,2,16,896]{3,2,1,0:T(8,128)(2,1)} %bitcast.37), calls=%async_computation.2 | async-start | bytes 917504 | tf_op jit(solution)/shard_map/all_to_all | solution.py:517
  102.9 2.1 %collective-permute-start.19 = (bf16[2,224,512]{2,1,0:T(8,128)(2,1)S(1)}, bf16[2,224,512]{2,1,0:T(8,128)(2,1)S(1)}, u32[]{:S(2)}, u32[]{:S(2)}) collective-permute-start(bf16[2,224,512]{2,1,0:T(8,128)(2,1)S(1)} %get-tuple-element.56), channel_id=1, source_target_pairs={{0,8},{1,17},{8,0},{9,25},{16,24},{17,1},{24,16},{25,9},{2,10},{3,... | collective-permute-start | bytes 1376264 | tf_op jit(solution)/shard_map/ppermute | solution.py:421
  105.0 2.9 %collective-permute-done.20 = bf16[2,2,224,512]{3,2,1,0:T(8,128)(2,1)} collective-permute-done((bf16[2,2,224,512]{3,2,1,0:T(8,128)(2,1)}, bf16[2,2,224,512]{3,2,1,0:T(8,128)(2,1)}, u32[]{:S(2)}, u32[]{:S(2)}) %collective-permute-start.20) | collective-permute-done | bytes 917536 | tf_op jit(solution)/shard_map/ppermute | solution.py:421
  109.5 2.1 %collective-permute-start.22 = (bf16[2,224,512]{2,1,0:T(8,128)(2,1)S(1)}, bf16[2,224,512]{2,1,0:T(8,128)(2,1)S(1)}, u32[]{:S(2)}, u32[]{:S(2)}) collective-permute-start(bf16[2,224,512]{2,1,0:T(8,128)(2,1)S(1)} %get-tuple-element.62), channel_id=1, source_target_pairs={{0,8},{1,17},{8,0},{9,25},{16,24},{17,1},{24,16},{25,9},{2,10},{3,... | collective-permute-start | bytes 1376264 | tf_op jit(solution)/shard_map/ppermute | solution.py:421
  112.9 5.1 %collective-permute-done.22.refs_1_ = bf16[2,224,512]{2,1,0:T(8,128)(2,1)S(1)} collective-permute-done((bf16[2,224,512]{2,1,0:T(8,128)(2,1)S(1)}, bf16[2,224,512]{2,1,0:T(8,128)(2,1)S(1)}, u32[]{:S(2)}, u32[]{:S(2)}) %collective-permute-start.22) | collective-permute-done | bytes 458784 | tf_op jit(solution)/shard_map/ppermute | solution.py:421
  119.0 2.1 %collective-permute-start.23 = (bf16[1,224,512]{2,1,0:T(8,128)(2,1)}, bf16[1,224,512]{2,1,0:T(8,128)(2,1)}, u32[]{:S(2)}, u32[]{:S(2)}) collective-permute-start(bf16[1,224,512]{2,1,0:T(8,128)(2,1)} %get-tuple-element.63), channel_id=1, source_target_pairs={{0,2},{2,0},{4,6},{6,4},{1,3},{3,1},{5,7},{7,5},{8,10},{10,8},{12,... | collective-permute-start | bytes 688136 | tf_op jit(solution)/shard_map/ppermute | solution.py:407
  121.1 2.4 %collective-permute-start.24 = (bf16[1,224,512]{2,1,0:T(8,128)(2,1)}, bf16[1,224,512]{2,1,0:T(8,128)(2,1)}, u32[]{:S(2)}, u32[]{:S(2)}) collective-permute-start(bf16[1,224,512]{2,1,0:T(8,128)(2,1)} %get-tuple-element.64), channel_id=1, source_target_pairs={{0,6},{2,4},{4,2},{6,0},{1,7},{3,5},{5,3},{7,1},{8,14},{10,12},{12... | collective-permute-start | bytes 688136 | tf_op jit(solution)/shard_map/ppermute | solution.py:407
  123.5 6.5 %shard_map.152.refs_4_ = bf16[32,16,896]{2,1,0:T(8,128)(2,1)} custom-call(s32[16]{0:T(128)S(1)} %bitcast.35, bf16[16,16,896]{2,1,0:T(8,128)(2,1)} %bitcast.16.grad_ref, bf16[16,16,896]{2,1,0:T(8,128)(2,1)} %get-tuple-element.51.used_ref, bf16[256,1792]{1,0:T(8,128)(2,1)} %get-tuple-element.52.slope_ref, f32[1,896]{1,0:T(1,128)S(1)} %reshape.106.gain_ref, ...), custom_call_target="tpu_custom_call" | custom-call | flops 1644167168 | bytes 9175040 | tf_op jit(solution)/shard_map/pallas_call | solution.py:162
  130.0 5.3 %collective-permute-done.24.refs_3_ = bf16[1,224,512]{2,1,0:T(8,128)(2,1)} collective-permute-done((bf16[1,224,512]{2,1,0:T(8,128)(2,1)}, bf16[1,224,512]{2,1,0:T(8,128)(2,1)}, u32[]{:S(2)}, u32[]{:S(2)}) %collective-permute-start.24) | collective-permute-done | bytes 229408 | tf_op jit(solution)/shard_map/ppermute | solution.py:407
  135.3 7.4 %collective-permute-done.21.refs_1_ = bf16[1,224,512]{2,1,0:T(8,128)(2,1)} collective-permute-done((bf16[1,224,512]{2,1,0:T(8,128)(2,1)}, bf16[1,224,512]{2,1,0:T(8,128)(2,1)}, u32[]{:S(2)}, u32[]{:S(2)}) %collective-permute-start.21) | collective-permute-done | bytes 229408 | tf_op jit(solution)/shard_map/ppermute | solution.py:407
  143.9 2.1 %collective-permute-start.25 = (bf16[224,512]{1,0:T(8,128)(2,1)S(1)}, bf16[224,512]{1,0:T(8,128)(2,1)S(1)}, u32[]{:S(2)}, u32[]{:S(2)}) collective-permute-start(bf16[224,512]{1,0:T(8,128)(2,1)S(1)} %bitcast.31), channel_id=1, source_target_pairs={{0,8},{1,17},{8,0},{9,25},{16,24},{17,1},{24,16},{25,9},{2,10},{3,... | collective-permute-start | bytes 688136 | tf_op jit(solution)/shard_map/ppermute | solution.py:421
  146.0 3.9 %all-to-all-start.3 = ((bf16[8,4,16,896]{3,2,1,0:T(8,128)(2,1)}), bf16[8,4,16,896]{3,2,1,0:T(8,128)(2,1)S(1)}, u32[]{:S(2)}, u32[]{:S(2)}) async-start(bf16[8,4,16,896]{3,2,1,0:T(8,128)(2,1)} %bitcast.36), calls=%async_computation.3 | async-start | bytes 1835008 | tf_op jit(solution)/shard_map/all_to_all | solution.py:558
  152.0 2.3 %select_bitcast_fusion = (bf16[1,128,2048]{2,1,0:T(8,128)(2,1)}, bf16[1,128,2048]{2,1,0:T(8,128)(2,1)}) fusion(bf16[128,2048]{1,0:T(8,128)(2,1)S(1)} %copy-done.9, bf16[128,2048]{1,0:T(8,128)(2,1)} %collective-permute-done.16, pred[2048]{0:T(1024)(128)(4,1)S(1)} %fusion.1, bf16[128,2048]{1,0:T(8,128)(2,1)S(1)} %copy-done.8, ...), kind=kLoop, calls=%fused_computation.1 | loop fusion | flops 524288 | bytes 3147776 | tf_op jit(solution)/shard_map/broadcast_in_dim | solution.py:564
  156.0 2.5 %collective-permute-done.27.refs_3_ = bf16[224,512]{1,0:T(8,128)(2,1)S(1)} collective-permute-done((bf16[224,512]{1,0:T(8,128)(2,1)S(1)}, bf16[224,512]{1,0:T(8,128)(2,1)S(1)}, u32[]{:S(2)}, u32[]{:S(2)}) %collective-permute-start.27) | collective-permute-done | bytes 229408 | tf_op jit(solution)/shard_map/ppermute | solution.py:421
  158.4 1.9 %shard_map.158 = (f32[896,256]{1,0:T(8,128)}, f32[896,256]{1,0:T(8,128)}) custom-call(s32[4]{0:T(128)S(1)} %fusion.5.plan, bf16[224,512]{1,0:T(8,128)(2,1)S(1)} %bitcast.33, bf16[224,512]{1,0:T(8,128)(2,1)S(1)} %collective-permute-done.25.refs_1_, bf16[224,512]{1,0:T(8,128)(2,1)S(1)} %collective-permute-done.26.refs_2_, ...), custom_call_target="tpu_custom_call" | custom-call | flops 10000000000 | bytes 30000000 | tf_op jit(solution)/shard_map/pallas_call | solution.py:388
  160.3 13.4 %all-to-all-done.3 = bf16[8,4,16,896]{3,2,1,0:T(8,128)(2,1)S(1)} async-done(((bf16[8,4,16,896]{3,2,1,0:T(8,128)(2,1)}), bf16[8,4,16,896]{3,2,1,0:T(8,128)(2,1)S(1)}, u32[]{:S(2)}, u32[]{:S(2)}) %all-to-all-start.3) | async-done | bytes 917536 | tf_op jit(solution)/shard_map/all_to_all | solution.py:558
  (78 shorter events, 30.8 us)
Async XLA Ops:
  3.0 30.7 %all-to-all-start = ((bf16[8,4,16,896]{3,2,1,0:T(8,128)(2,1)}), bf16[8,4,16,896]{3,2,1,0:T(8,128)(2,1)}, u32[]{:S(2)}, u32[]{:S(2)}) async-start(bf16[8,4,16,896]{3,2,1,0:T(8,128)(2,1)} %bitcast.39), calls=%async_computation | async-start | bytes 1835008 | tf_op jit(solution)/shard_map/all_to_all | solution.py:480
  10.3 30.1 %collective-permute-start = (bf16[224,512]{1,0:T(8,128)(2,1)S(1)}, bf16[224,512]{1,0:T(8,128)(2,1)}, u32[]{:S(2)}, u32[]{:S(2)}) collective-permute-start(bf16[224,512]{1,0:T(8,128)(2,1)S(1)} %pad_maximum_fusion), channel_id=1, source_target_pairs={{0,2},{2,0},{4,6},{6,4},{1,3},{3,1},{5,7},{7,5},{8,10},{10,8},{12,... | collective-permute-start | bytes 688136 | tf_op jit(solution)/shard_map/ppermute | solution.py:407
  12.4 30.6 %collective-permute-start.1 = (bf16[224,512]{1,0:T(8,128)(2,1)S(1)}, bf16[224,512]{1,0:T(8,128)(2,1)}, u32[]{:S(2)}, u32[]{:S(2)}) collective-permute-start(bf16[224,512]{1,0:T(8,128)(2,1)S(1)} %pad_maximum_fusion), channel_id=1, source_target_pairs={{0,4},{2,6},{4,0},{6,2},{1,5},{3,7},{5,1},{7,3},{8,12},{10,14},{12... | collective-permute-start | bytes 688136 | tf_op jit(solution)/shard_map/ppermute | solution.py:407
  43.1 22.2 %all-to-all-start.1 = ((bf16[8,2,16,896]{3,2,1,0:T(8,128)(2,1)}), bf16[8,2,16,896]{3,2,1,0:T(8,128)(2,1)}, u32[]{:S(2)}, u32[]{:S(2)}) async-start(bf16[8,2,16,896]{3,2,1,0:T(8,128)(2,1)} %bitcast.44), calls=%async_computation.1 | async-start | bytes 917504 | tf_op jit(solution)/shard_map/all_to_all | solution.py:489
  47.2 8.3 %collective-permute-start.12 = (bf16[224,512]{1,0:T(8,128)(2,1)}, bf16[224,512]{1,0:T(8,128)(2,1)}, u32[]{:S(2)}, u32[]{:S(2)}) collective-permute-start(bf16[224,512]{1,0:T(8,128)(2,1)} %collective-permute-done.1.refs_0_), channel_id=1, source_target_pairs={{0,8},{1,17},{8,0},{9,25},{16,24},{17,1},{24,16},{25,9},{2,10},{3,... | collective-permute-start | bytes 688136 | tf_op jit(solution)/shard_map/ppermute | solution.py:421
  48.7 8.8 %collective-permute-start.13 = (bf16[224,512]{1,0:T(8,128)(2,1)}, bf16[224,512]{1,0:T(8,128)(2,1)S(1)}, u32[]{:S(2)}, u32[]{:S(2)}) collective-permute-start(bf16[224,512]{1,0:T(8,128)(2,1)} %collective-permute-done.1.refs_0_), channel_id=1, source_target_pairs={{0,16},{1,9},{8,24},{9,1},{16,0},{17,25},{24,8},{25,17},{2,18},{3,... | collective-permute-start | bytes 688136 | tf_op jit(solution)/shard_map/ppermute | solution.py:421
  50.3 10.2 %collective-permute-start.5 = (bf16[224,512]{1,0:T(8,128)(2,1)}, bf16[224,512]{1,0:T(8,128)(2,1)}, u32[]{:S(2)}, u32[]{:S(2)}) collective-permute-start(bf16[224,512]{1,0:T(8,128)(2,1)} %collective-permute-done.refs_0_), channel_id=1, source_target_pairs={{0,8},{1,17},{8,0},{9,25},{16,24},{17,1},{24,16},{25,9},{2,10},{3,... | collective-permute-start | bytes 688136 | tf_op jit(solution)/shard_map/ppermute | solution.py:421
  50.8 9.6 %collective-permute-start.6 = (bf16[224,512]{1,0:T(8,128)(2,1)}, bf16[224,512]{1,0:T(8,128)(2,1)S(1)}, u32[]{:S(2)}, u32[]{:S(2)}) collective-permute-start(bf16[224,512]{1,0:T(8,128)(2,1)} %collective-permute-done.refs_0_), channel_id=1, source_target_pairs={{0,16},{1,9},{8,24},{9,1},{16,0},{17,25},{24,8},{25,17},{2,18},{3,... | collective-permute-start | bytes 688136 | tf_op jit(solution)/shard_map/ppermute | solution.py:421
  51.3 11.8 %collective-permute-start.8 = (bf16[224,512]{1,0:T(8,128)(2,1)}, bf16[224,512]{1,0:T(8,128)(2,1)}, u32[]{:S(2)}, u32[]{:S(2)}) collective-permute-start(bf16[224,512]{1,0:T(8,128)(2,1)} %collective-permute-done.1.refs_0_), channel_id=1, source_target_pairs={{0,2},{2,0},{4,6},{6,4},{1,3},{3,1},{5,7},{7,5},{8,10},{10,8},{12,... | collective-permute-start | bytes 688136 | tf_op jit(solution)/shard_map/ppermute | solution.py:407
  55.5 9.1 %collective-permute-start.14 = (bf16[224,512]{1,0:T(8,128)(2,1)}, bf16[224,512]{1,0:T(8,128)(2,1)S(1)}, u32[]{:S(2)}, u32[]{:S(2)}) collective-permute-start(bf16[224,512]{1,0:T(8,128)(2,1)} %collective-permute-done.12.refs_1_), channel_id=1, source_target_pairs={{0,16},{1,9},{8,24},{9,1},{16,0},{17,25},{24,8},{25,17},{2,18},{3,... | collective-permute-start | bytes 688136 | tf_op jit(solution)/shard_map/ppermute | solution.py:421
  58.3 14.9 %collective-permute-start.3 = (bf16[128,2048]{1,0:T(8,128)(2,1)}, bf16[128,2048]{1,0:T(8,128)(2,1)}, u32[]{:S(2)}, u32[]{:S(2)}) collective-permute-start(bf16[128,2048]{1,0:T(8,128)(2,1)} %bitcast.45), channel_id=1, source_target_pairs={{0,1},{1,0},{2,3},{3,2},{4,5},{5,4},{6,7},{7,6},{8,9},{9,8},{10,11... | collective-permute-start | bytes 1572872 | tf_op jit(solution)/shard_map/ppermute | solution.py:403
  60.4 12.8 %collective-permute-start.4 = (bf16[128,2048]{1,0:T(8,128)(2,1)}, bf16[128,2048]{1,0:T(8,128)(2,1)}, u32[]{:S(2)}, u32[]{:S(2)}) collective-permute-start(bf16[128,2048]{1,0:T(8,128)(2,1)} %bitcast.48), channel_id=1, source_target_pairs={{0,1},{1,0},{2,3},{3,2},{4,5},{5,4},{6,7},{7,6},{8,9},{9,8},{10,11... | collective-permute-start | bytes 1572872 | tf_op jit(solution)/shard_map/ppermute | solution.py:403
  61.1 7.8 %collective-permute-start.7 = (bf16[224,512]{1,0:T(8,128)(2,1)}, bf16[224,512]{1,0:T(8,128)(2,1)}, u32[]{:S(2)}, u32[]{:S(2)}) collective-permute-start(bf16[224,512]{1,0:T(8,128)(2,1)} %collective-permute-done.5.refs_1_), channel_id=1, source_target_pairs={{0,16},{1,9},{8,24},{9,1},{16,0},{17,25},{24,8},{25,17},{2,18},{3,... | collective-permute-start | bytes 688136 | tf_op jit(solution)/shard_map/ppermute | solution.py:421
  63.1 8.1 %collective-permute-start.9 = (bf16[224,512]{1,0:T(8,128)(2,1)}, bf16[224,512]{1,0:T(8,128)(2,1)}, u32[]{:S(2)}, u32[]{:S(2)}) collective-permute-start(bf16[224,512]{1,0:T(8,128)(2,1)} %collective-permute-done.8.refs_7_), channel_id=1, source_target_pairs={{0,8},{1,17},{8,0},{9,25},{16,24},{17,1},{24,16},{25,9},{2,10},{3,... | collective-permute-start | bytes 688136 | tf_op jit(solution)/shard_map/ppermute | solution.py:421
  65.3 7.9 %collective-permute-start.2 = (bf16[8,2,16,896]{3,2,1,0:T(8,128)(2,1)}, bf16[8,2,16,896]{3,2,1,0:T(8,128)(2,1)S(1)}, u32[]{:S(2)}, u32[]{:S(2)}) collective-permute-start(bf16[8,2,16,896]{3,2,1,0:T(8,128)(2,1)} %all-to-all-done.1.refs_0_), channel_id=1, source_target_pairs={{0,1},{1,0},{2,3},{3,2},{4,5},{5,4},{6,7},{7,6},{8,9},{9,8},{10,11... | collective-permute-start | bytes 1376264 | tf_op jit(solution)/shard_map/ppermute | solution.py:403
  69.0 15.3 %collective-permute-start.10 = (bf16[224,512]{1,0:T(8,128)(2,1)}, bf16[224,512]{1,0:T(8,128)(2,1)S(1)}, u32[]{:S(2)}, u32[]{:S(2)}) collective-permute-start(bf16[224,512]{1,0:T(8,128)(2,1)} %collective-permute-done.8.refs_7_), channel_id=1, source_target_pairs={{0,16},{1,9},{8,24},{9,1},{16,0},{17,25},{24,8},{25,17},{2,18},{3,... | collective-permute-start | bytes 688136 | tf_op jit(solution)/shard_map/ppermute | solution.py:421
  71.2 13.1 %collective-permute-start.11 = (bf16[224,512]{1,0:T(8,128)(2,1)}, bf16[224,512]{1,0:T(8,128)(2,1)S(1)}, u32[]{:S(2)}, u32[]{:S(2)}) collective-permute-start(bf16[224,512]{1,0:T(8,128)(2,1)} %collective-permute-done.9.refs_8_), channel_id=1, source_target_pairs={{0,16},{1,9},{8,24},{9,1},{16,0},{17,25},{24,8},{25,17},{2,18},{3,... | collective-permute-start | bytes 688136 | tf_op jit(solution)/shard_map/ppermute | solution.py:421
  82.4 18.8 %collective-permute-start.18 = (bf16[2,2,224,512]{3,2,1,0:T(8,128)(2,1)}, bf16[2,2,224,512]{3,2,1,0:T(8,128)(2,1)}, u32[]{:S(2)}, u32[]{:S(2)}) collective-permute-start(bf16[2,2,224,512]{3,2,1,0:T(8,128)(2,1)} %get-tuple-element.54), channel_id=1, source_target_pairs={{0,16},{1,9},{8,24},{9,1},{16,0},{17,25},{24,8},{25,17},{2,18},{3,... | collective-permute-start | bytes 2752520 | tf_op jit(solution)/shard_map/ppermute | solution.py:421
  93.3 14.6 %collective-permute-start.20 = (bf16[2,2,224,512]{3,2,1,0:T(8,128)(2,1)}, bf16[2,2,224,512]{3,2,1,0:T(8,128)(2,1)}, u32[]{:S(2)}, u32[]{:S(2)}) collective-permute-start(bf16[2,2,224,512]{3,2,1,0:T(8,128)(2,1)} %get-tuple-element.58), channel_id=1, source_target_pairs={{0,16},{1,9},{8,24},{9,1},{16,0},{17,25},{24,8},{25,17},{2,18},{3,... | collective-permute-start | bytes 2752520 | tf_op jit(solution)/shard_map/ppermute | solution.py:421
  93.6 1.8 %collective-permute-start.17 = (bf16[8,2,16,896]{3,2,1,0:T(8,128)(2,1)S(1)}, bf16[8,2,16,896]{3,2,1,0:T(8,128)(2,1)S(1)}, u32[]{:S(2)}, u32[]{:S(2)}) collective-permute-start(bf16[8,2,16,896]{3,2,1,0:T(8,128)(2,1)S(1)} %get-tuple-element.50), channel_id=1, source_target_pairs={{0,1},{1,0},{2,3},{3,2},{4,5},{5,4},{6,7},{7,6},{8,9},{9,8},{10,11... | collective-permute-start | bytes 1376264 | tf_op jit(solution)/shard_map/ppermute | solution.py:403
  96.3 27.2 %all-to-all-start.2 = ((bf16[8,2,16,896]{3,2,1,0:T(8,128)(2,1)}), bf16[8,2,16,896]{3,2,1,0:T(8,128)(2,1)}, u32[]{:S(2)}, u32[]{:S(2)}) async-start(bf16[8,2,16,896]{3,2,1,0:T(8,128)(2,1)} %bitcast.37), calls=%async_computation.2 | async-start | bytes 917504 | tf_op jit(solution)/shard_map/all_to_all | solution.py:517
  102.9 9.2 %collective-permute-start.19 = (bf16[2,224,512]{2,1,0:T(8,128)(2,1)S(1)}, bf16[2,224,512]{2,1,0:T(8,128)(2,1)S(1)}, u32[]{:S(2)}, u32[]{:S(2)}) collective-permute-start(bf16[2,224,512]{2,1,0:T(8,128)(2,1)S(1)} %get-tuple-element.56), channel_id=1, source_target_pairs={{0,8},{1,17},{8,0},{9,25},{16,24},{17,1},{24,16},{25,9},{2,10},{3,... | collective-permute-start | bytes 1376264 | tf_op jit(solution)/shard_map/ppermute | solution.py:421
  109.5 8.5 %collective-permute-start.22 = (bf16[2,224,512]{2,1,0:T(8,128)(2,1)S(1)}, bf16[2,224,512]{2,1,0:T(8,128)(2,1)S(1)}, u32[]{:S(2)}, u32[]{:S(2)}) collective-permute-start(bf16[2,224,512]{2,1,0:T(8,128)(2,1)S(1)} %get-tuple-element.62), channel_id=1, source_target_pairs={{0,8},{1,17},{8,0},{9,25},{16,24},{17,1},{24,16},{25,9},{2,10},{3,... | collective-permute-start | bytes 1376264 | tf_op jit(solution)/shard_map/ppermute | solution.py:421
  111.6 40.4 %collective-permute-start.15 = (bf16[128,2048]{1,0:T(8,128)(2,1)}, bf16[128,2048]{1,0:T(8,128)(2,1)}, u32[]{:S(2)}, u32[]{:S(2)}) collective-permute-start(bf16[128,2048]{1,0:T(8,128)(2,1)} %get-tuple-element.46), channel_id=1, source_target_pairs={{0,1},{1,0},{2,3},{3,2},{4,5},{5,4},{6,7},{7,6},{8,9},{9,8},{10,11... | collective-permute-start | bytes 1572872 | tf_op jit(solution)/shard_map/ppermute | solution.py:403
  111.6 40.4 %collective-permute-start.16 = (bf16[128,2048]{1,0:T(8,128)(2,1)}, bf16[128,2048]{1,0:T(8,128)(2,1)}, u32[]{:S(2)}, u32[]{:S(2)}) collective-permute-start(bf16[128,2048]{1,0:T(8,128)(2,1)} %get-tuple-element.48), channel_id=1, source_target_pairs={{0,1},{1,0},{2,3},{3,2},{4,5},{5,4},{6,7},{7,6},{8,9},{9,8},{10,11... | collective-permute-start | bytes 1572872 | tf_op jit(solution)/shard_map/ppermute | solution.py:403
  119.0 11.0 %collective-permute-start.23 = (bf16[1,224,512]{2,1,0:T(8,128)(2,1)}, bf16[1,224,512]{2,1,0:T(8,128)(2,1)}, u32[]{:S(2)}, u32[]{:S(2)}) collective-permute-start(bf16[1,224,512]{2,1,0:T(8,128)(2,1)} %get-tuple-element.63), channel_id=1, source_target_pairs={{0,2},{2,0},{4,6},{6,4},{1,3},{3,1},{5,7},{7,5},{8,10},{10,8},{12,... | collective-permute-start | bytes 688136 | tf_op jit(solution)/shard_map/ppermute | solution.py:407
  121.1 14.2 %collective-permute-start.24 = (bf16[1,224,512]{2,1,0:T(8,128)(2,1)}, bf16[1,224,512]{2,1,0:T(8,128)(2,1)}, u32[]{:S(2)}, u32[]{:S(2)}) collective-permute-start(bf16[1,224,512]{2,1,0:T(8,128)(2,1)} %get-tuple-element.64), channel_id=1, source_target_pairs={{0,6},{2,4},{4,2},{6,0},{1,7},{3,5},{5,3},{7,1},{8,14},{10,12},{12... | collective-permute-start | bytes 688136 | tf_op jit(solution)/shard_map/ppermute | solution.py:407
  123.4 19.2 %collective-permute-start.21 = (bf16[1,224,512]{2,1,0:T(8,128)(2,1)}, bf16[1,224,512]{2,1,0:T(8,128)(2,1)}, u32[]{:S(2)}, u32[]{:S(2)}) collective-permute-start(bf16[1,224,512]{2,1,0:T(8,128)(2,1)} %get-tuple-element.61), channel_id=1, source_target_pairs={{0,4},{2,6},{4,0},{6,2},{1,5},{3,7},{5,1},{7,3},{8,12},{10,14},{12... | collective-permute-start | bytes 688136 | tf_op jit(solution)/shard_map/ppermute | solution.py:407
  143.9 6.8 %collective-permute-start.25 = (bf16[224,512]{1,0:T(8,128)(2,1)S(1)}, bf16[224,512]{1,0:T(8,128)(2,1)S(1)}, u32[]{:S(2)}, u32[]{:S(2)}) collective-permute-start(bf16[224,512]{1,0:T(8,128)(2,1)S(1)} %bitcast.31), channel_id=1, source_target_pairs={{0,8},{1,17},{8,0},{9,25},{16,24},{17,1},{24,16},{25,9},{2,10},{3,... | collective-permute-start | bytes 688136 | tf_op jit(solution)/shard_map/ppermute | solution.py:421
  146.0 27.7 %all-to-all-start.3 = ((bf16[8,4,16,896]{3,2,1,0:T(8,128)(2,1)}), bf16[8,4,16,896]{3,2,1,0:T(8,128)(2,1)S(1)}, u32[]{:S(2)}, u32[]{:S(2)}) async-start(bf16[8,4,16,896]{3,2,1,0:T(8,128)(2,1)} %bitcast.36), calls=%async_computation.3 | async-start | bytes 1835008 | tf_op jit(solution)/shard_map/all_to_all | solution.py:558
  149.9 6.1 %collective-permute-start.26 = (bf16[224,512]{1,0:T(8,128)(2,1)S(1)}, bf16[224,512]{1,0:T(8,128)(2,1)S(1)}, u32[]{:S(2)}, u32[]{:S(2)}) collective-permute-start(bf16[224,512]{1,0:T(8,128)(2,1)S(1)} %bitcast.32), channel_id=1, source_target_pairs={{0,16},{1,9},{8,24},{9,1},{16,0},{17,25},{24,8},{25,17},{2,18},{3,... | collective-permute-start | bytes 688136 | tf_op jit(solution)/shard_map/ppermute | solution.py:421
  150.7 7.8 %collective-permute-start.27 = (bf16[224,512]{1,0:T(8,128)(2,1)S(1)}, bf16[224,512]{1,0:T(8,128)(2,1)S(1)}, u32[]{:S(2)}, u32[]{:S(2)}) collective-permute-start(bf16[224,512]{1,0:T(8,128)(2,1)S(1)} %collective-permute-done.25.refs_1_), channel_id=1, source_target_pairs={{0,16},{1,9},{8,24},{9,1},{16,0},{17,25},{24,8},{25,17},{2,18},{3,... | collective-permute-start | bytes 688136 | tf_op jit(solution)/shard_map/ppermute | solution.py:421
  (12 other events, 158.2 us)

commit v2 on v1

--- a/solution.py
+++ b/solution.py
@@ -192,43 +192,60 @@
     steps = len(kinds)
     own_enc, other_enc = take(2)
     token_refs = (take(2), take(2))
-    weight_refs = [take({"whole": 1, "columns": 2, "rows": lines}[kind]) for kind in kinds]
+    weight_refs = [take({"columns": 2, "rows": lines}[kind]) for kind in kinds]
     if last:
         (back_in,) = take(1)
         take(4)
     out_refs = (take(2), take(2))
     back_refs = take(2 if last else 1)
     grad_halves = take(2)
-    rows, rows_t, back, weight = refs
+    rows, rows_t, back, weight, weight_done = refs[:5]
+    if last:
+        back_held, back_done = refs[5:]
     step = pl.program_id(0)
     shares, mine, piece, width = own_enc.shape
     span = shares * piece
     scale = 1.0 / math.sqrt(HD)
-    part_rows, columns = width // lines, weight.shape[1] // 2
+    part_rows, columns = width // lines, weight.shape[2] // 2
+
+    def weight_copies(shard):
+        kind, found = kinds[shard], weight_refs[shard]
+        if kind == "columns":
+            places = [(slice(None), pl.ds(k * columns, columns)) for k in range(2)]
+        else:
+            places = [
+                (pl.ds(pl.multiple_of(plan[steps + i] * part_rows, 16), part_rows), slice(None))
+                for i in range(lines)
+            ]
+        return [
+            pltpu.make_async_copy(part, weight.at[shard, *place], weight_done.at[shard, i])
+            for i, (part, place) in enumerate(zip(found, places))
+        ]
+
+    def back_copy():
+        return pltpu.make_async_copy(back_in, back_held, back_done)
 
     @pl.when(step == 0)
     def _():
+        for shard in range(steps):
+            for copy in weight_copies(shard):
+                copy.start()
+        if last:
+            back_copy().start()
         for s in range(2 * mine):
             source = own_enc if s < mine else other_enc
             rows[s * span : (s + 1) * span, :] = merge_rows(source[:, s % mine])
         rows_t[...] = rows[...].T
-        back[...] = back_in[...] if last else jnp.zeros_like(back)
-
-    for shard, (kind, found) in enumerate(zip(kinds, weight_refs)):
+        back[...] = jnp.zeros_like(back)
+
+    for shard in range(steps):
 
         @pl.when(step == shard)
-        def _(kind=kind, found=found):
-            if kind == "whole":
-                weight[...] = found[0][...]
-            elif kind == "columns":
-                weight[:, :columns] = found[0][...]
-                weight[:, columns:] = found[1][...]
-            else:
-                for i in range(lines):
-                    start = pl.multiple_of(plan[steps + i] * part_rows, 16)
-                    weight[pl.ds(start, part_rows), :] = found[i][...]
-
-    both = dot(rows[...], weight[...]).astype(jnp.bfloat16)
+        def _(shard=shard):
+            for copy in weight_copies(shard):
+                copy.wait()
+
+    both = dot(rows[...], weight[step]).astype(jnp.bfloat16)
     pairs = [(s, h) for s in range(2 * mine) for h in range(columns // HD)]
 
     def tokens_of(s, h):
@@ -275,13 +292,15 @@
         start = pl.multiple_of(plan[steps + i] * part_rows, 16)
         part_grad = dot(rows_t[pl.ds(start, part_rows), :], both_grad).astype(jnp.bfloat16)
         grad_halves[2 * i // lines][i % (lines // 2), 0] = part_grad
-    back[...] += dot_nt(both_grad, weight[...])
+    back[...] += dot_nt(both_grad, weight[step])
 
     @pl.when(step == steps - 1)
     def _():
         if not last:
-            back_refs[0][...] = back[...]
+            back_refs[0][...] = back[...].astype(jnp.bfloat16)
         else:
+            back_copy().wait()
+            back[...] += back_held[...].astype(jnp.float32)
             for s in range(2 * mine):
                 block = back[s * span : (s + 1) * span, :].reshape(shares, piece, width)
                 back_refs[s // mine][:, s % mine] = block.astype(jnp.bfloat16)
@@ -302,12 +321,12 @@
     enc_spec = whole(*own_enc.shape)
     out = functools.partial(jax.ShapeDtypeStruct, dtype=jnp.bfloat16)
     operands = [plan, own_enc, other_enc, *map(in_hbm, token_arrays), *arrays]
-    in_specs = [enc_spec] * 2 + [token_spec] * 4 + [whole(*value.shape) for value in arrays]
-    back_shapes, aliases = [jax.ShapeDtypeStruct((all_rows, width), jnp.float32)], {}
+    in_specs = [enc_spec] * 2 + [token_spec] * 4 + [pl.BlockSpec(memory_space=pl.ANY)] * len(arrays)
+    back_shapes, aliases = [out((all_rows, width))], {}
     if last:
         aliases = {len(operands) + 1 + i: i for i in range(4)}
         operands += [earlier[4], *map(in_hbm, earlier[:4])]
-        in_specs += [whole(all_rows, width)] + [pl.BlockSpec(memory_space=pl.ANY)] * 4
+        in_specs += [pl.BlockSpec(memory_space=pl.ANY)] * 5
         back_shapes = [out(own_enc.shape)] * 2
     return pl.pallas_call(
         functools.partial(attend_kernel, kinds, lines, last),
@@ -322,8 +341,10 @@
                 pltpu.VMEM((all_rows, width), jnp.bfloat16),
                 pltpu.VMEM((width, all_rows), jnp.bfloat16),
                 pltpu.VMEM((all_rows, width), jnp.float32),
-                pltpu.VMEM((width, 2 * columns), jnp.bfloat16),
-            ],
+                pltpu.VMEM((steps, width, 2 * columns), jnp.bfloat16),
+                pltpu.SemaphoreType.DMA((steps, max(lines, 2))),
+            ]
+            + [pltpu.VMEM((all_rows, width), jnp.bfloat16), pltpu.SemaphoreType.DMA] * last,
         ),
         out_shape=[pltpu.HBM((tokens, all_columns), jnp.bfloat16)] * 4
         + back_shapes
@@ -372,8 +393,26 @@
     )(*terms, *after)
 
 
-def join_kernel(count, plan, *refs):
-    parts, outs = refs[:count], refs[count:]
+def copy_kernel(plan, *refs):
+    out = refs[-1]
+    for i in range(plan.shape[0]):
+        out[i] = plan[i]
+
+
+def copy_plan(plan, others):
+    scalars = pl.BlockSpec(memory_space=pltpu.SMEM)
+    return pl.pallas_call(
+        copy_kernel,
+        in_specs=[scalars] + [pl.BlockSpec(memory_space=pl.ANY)] * len(others),
+        out_specs=scalars,
+        out_shape=jax.ShapeDtypeStruct(plan.shape, plan.dtype),
+        compiler_params=pltpu.CompilerParams(vmem_limit_bytes=SMALL_VMEM_BYTES),
+        cost_estimate=stated(4),
+    )(plan, *others)
+
+
+def join_kernel(plan, *refs):
+    parts, outs = refs[:-2], refs[-2:]
     part_rows, columns = parts[0].shape[0], outs[0].shape[1]
     for i, part in enumerate(parts):
         start = pl.multiple_of(plan[i] * part_rows, 16)
@@ -381,21 +420,21 @@
             out[pl.ds(start, part_rows), :] = part[:, k * columns : (k + 1) * columns].astype(out.dtype)
 
 
-def join_parts(plan, parts, outs, dtype, microseconds):
+def join_grads(plan, parts):
     part_rows, columns = parts[0].shape
     width = part_rows * len(parts)
     whole = lambda *shape: pl.BlockSpec(shape, lambda j, p: (0,) * len(shape))
     return pl.pallas_call(
-        functools.partial(join_kernel, len(parts)),
+        join_kernel,
         grid_spec=pltpu.PrefetchScalarGridSpec(
             num_scalar_prefetch=1,
             grid=(1,),
             in_specs=[whole(part_rows, columns)] * len(parts),
-            out_specs=[whole(width, columns // outs)] * outs,
-        ),
-        out_shape=[jax.ShapeDtypeStruct((width, columns // outs), dtype)] * outs,
+            out_specs=[whole(width, columns // 2)] * 2,
+        ),
+        out_shape=[jax.ShapeDtypeStruct((width, columns // 2), jnp.float32)] * 2,
         compiler_params=pltpu.CompilerParams(vmem_limit_bytes=SMALL_VMEM_BYTES),
-        cost_estimate=stated(microseconds),
+        cost_estimate=stated(8),
     )(plan, *parts)
 
 
@@ -491,11 +530,7 @@
     )
     shards = {0: ("columns", [in_hbm(key_weight), in_hbm(value_weight)])}
     for shift in range(1, chips):
-        found = gather_lines(part[shift], stages)
-        if shift == 1 or shift in even:
-            shards[shift] = ("whole", [*join_parts(part_lines, found, 1, jnp.bfloat16, 4)])
-        else:
-            shards[shift] = ("rows", found)
+        shards[shift] = ("rows", gather_lines(part[shift], stages))
     other_enc = swap_cores(own_enc)
 
     steps = ([0, *even], [*odd])
@@ -503,6 +538,8 @@
         jnp.concatenate([jnp.stack([(chip ^ shift) * 2 + core for shift in shifts]), part_lines])
         for shifts in steps
     ]
+    early = [value for shift in (1, *even) for value in shards[shift][1][lines // 2 :]]
+    plans[0] = copy_plan(plans[0], early)
     parted = [[shards[shift] for shift in shifts] for shifts in steps]
     first = attend(plans[0], lines, own_enc, other_enc, token_arrays, parted[0])
     last = attend(plans[1], lines, own_enc, other_enc, token_arrays, parted[1], first[:5])
@@ -547,13 +584,13 @@
         enc_up,
         enc_down,
         groups * holding,
-        [],
+        [terms[shift] for shift in even],
     )
     (share,) = sum_blocks([*terms.values()], (1,), [in_hbm(placed)])
     share = share[0]
     if lax.axis_size("far") > 1:
         share = lax.psum(share, "far")
-    weight_grads = join_parts(part_lines, gather_lines(share, stages), 2, jnp.float32, 10)
+    weight_grads = join_grads(part_lines, gather_lines(share, stages))
 
     returned = lax.all_to_all(
         placed.reshape(groups, holding, piece, width), SEQ, split_axis=0, concat_axis=0, tiled=True

time: 175 us -> 168 us (0.960); the launches traced: 175 us -> 165 us
  waiting for transfers between devices: 66.2 us -> 49.1 us
  starting transfers between devices: 53.1 us -> 64.4 us
  local copies, waits for them, and re-layouts: 8.31 us -> 4.34 us
    all_to_all x1, waiting for transfers between devices: 13.4 us -> 4.22 us  [on_device(): lax.all_to_all(placed.reshape(groups, holding, piece, width), SEQ, split_...]
    ppermute x6, waiting for transfers between devices: 15.3 us -> 8.32 us  [swap_chips(): lax.ppermute(value, 'z', [(z, z ^ shift) for z in range(lax.axis_size('z'...]
    ppermute x16, starting transfers between devices: 22.5 us -> 28.8 us  [swap_lines(): return lax.ppermute(value, ('line', 'core'), pairs)]
    unnamed x24 -> x16, local copies, waits for them, and re-layouts: 4 us -> 0.03 us
    ppermute x6, starting transfers between devices: 10.8 us -> 14.2 us  [swap_chips(): lax.ppermute(value, 'z', [(z, z ^ shift) for z in range(lax.axis_size('z'...]
    pallas_call x3 -> x2, Pallas kernels: 5.29 us -> 3.01 us  [the longest x1 1.87 us: join_grads(): pl.pallas_call(join_kernel, grid_spec=pltpu.PrefetchScalarGridSpec(num_sc...]
    pallas_call x2, Pallas kernels: 18.3 us -> 20.3 us  [attend(): pl.pallas_call(functools.partial(attend_kernel, kinds, lines, last), grid...]
  transfers between devices with their start and end apart: 32 -> 32, of which waited for: 13 -> 13; matrix products, arithmetic and copies ran while one was open for 2% -> 2% of each run, Pallas kernels for 25% -> 26%
where the time goes in v2:
time: 168 us; the launch traced here: 165 us
  starting transfers between devices  64.4 us (38%)
  waiting for transfers between devices  49.1 us (29%)
  Pallas kernels  43.6 us (26%)
  local copies, waits for them, and re-layouts  4.34 us (3%)
  other arithmetic  3.07 us (2%)
    ppermute x16, starting transfers between devices, swap_lines(): return lax.ppermute(value, ('line', 'core'), pairs)  28.8 us
    pallas_call x2, Pallas kernels, attend(): pl.pallas_call(functools.partial(attend_kernel, kinds, lines, last), grid...  20.3 us
    all_to_all x1, waiting for transfers between devices, on_device(): lax.all_to_all(pieces, SEQ, split_axis=0, concat_axis=0, tiled=True)  18.3 us
    ppermute x16, waiting for transfers between devices, swap_lines(): return lax.ppermute(value, ('line', 'core'), pairs)  16.5 us
    ppermute x6, starting transfers between devices, swap_chips(): lax.ppermute(value, 'z', [(z, z ^ shift) for z in range(lax.axis_size('z'...  14.2 us
    ppermute x6, waiting for transfers between devices, swap_chips(): lax.ppermute(value, 'z', [(z, z ^ shift) for z in range(lax.axis_size('z'...  8.32 us
    pallas_call x6, Pallas kernels, sum_blocks(): pl.pallas_call(functools.partial(sum_kernel, len(terms), sizes), grid=(ti...  7.05 us
    pallas_call x1, Pallas kernels, encode_rows(): pl.pallas_call(encode_kernel, grid_spec=pltpu.PrefetchScalarGridSpec(num_...  6.76 us
  transfers between devices with their start and end apart: 32, of which 13 were waited for; matrix products, arithmetic and copies ran while one was open for 2% of the time, Pallas kernels for 26%

profile of v2, /device:TPU:0, one launch (start us, length us, event | category | flops | bytes accessed | tf_op | source)
XLA Modules:
  0.0 165.4 jit_solution(16503074331242561137)
XLA Ops:
  0.7 2.3 %copy.23 = bf16[4,8,16,896]{3,2,0,1:T(8,128)(2,1)} copy(bf16[4,8,16,896]{3,2,1,0:T(8,128)(2,1)} %bitcast.40) | data formatting | bytes 1835008 | tf_op jit(solution)/shard_map/reshape;squeeze | solution.py:518
  3.0 6.3 %all-to-all-start = ((bf16[8,4,16,896]{3,2,1,0:T(8,128)(2,1)}), bf16[8,4,16,896]{3,2,1,0:T(8,128)(2,1)}, u32[]{:S(2)}, u32[]{:S(2)}) async-start(bf16[8,4,16,896]{3,2,1,0:T(8,128)(2,1)} %bitcast.39), calls=%async_computation | async-start | bytes 1835008 | tf_op jit(solution)/shard_map/all_to_all | solution.py:519
  11.0 2.0 %collective-permute-start = (bf16[224,512]{1,0:T(8,128)(2,1)}, bf16[224,512]{1,0:T(8,128)(2,1)S(1)}, u32[]{:S(2)}, u32[]{:S(2)}) collective-permute-start(bf16[224,512]{1,0:T(8,128)(2,1)} %pad_maximum_fusion), channel_id=1, source_target_pairs={{0,2},{2,0},{4,6},{6,4},{1,3},{3,1},{5,7},{7,5},{8,10},{10,8},{12,... | collective-permute-start | bytes 688136 | tf_op jit(solution)/shard_map/ppermute | solution.py:446
  13.0 2.4 %collective-permute-start.1 = (bf16[224,512]{1,0:T(8,128)(2,1)}, bf16[224,512]{1,0:T(8,128)(2,1)}, u32[]{:S(2)}, u32[]{:S(2)}) collective-permute-start(bf16[224,512]{1,0:T(8,128)(2,1)} %pad_maximum_fusion), channel_id=1, source_target_pairs={{0,4},{2,6},{4,0},{6,2},{1,5},{3,7},{5,1},{7,3},{8,12},{10,14},{12... | collective-permute-start | bytes 688136 | tf_op jit(solution)/shard_map/ppermute | solution.py:446
  15.4 18.3 %all-to-all-done = bf16[8,4,16,896]{3,2,1,0:T(8,128)(2,1)} async-done(((bf16[8,4,16,896]{3,2,1,0:T(8,128)(2,1)}), bf16[8,4,16,896]{3,2,1,0:T(8,128)(2,1)}, u32[]{:S(2)}, u32[]{:S(2)}) %all-to-all-start) | async-done | bytes 917536 | tf_op jit(solution)/shard_map/all_to_all | solution.py:519
  33.7 6.8 %shard_map.146 = (bf16[16,16,896]{2,1,0:T(8,128)(2,1)}, bf16[16,16,896]{2,1,0:T(8,128)(2,1)}, bf16[256,1792]{1,0:T(8,128)(2,1)}) custom-call(s32[16]{0:T(128)S(1)} %bitcast.34, bf16[32,16,896]{2,1,0:T(8,128)(2,1)} %bitcast.5.rows_ref, f32[1,896]{1,0:T(1,128)S(1)} %reshape.106.gain_ref, bf16[896,1792]{1,0:T(8,128)(2,1)S(1)} %copy-done, bf16[1792,896]{1,0:T(8,128)(2,1)} %down_ref.3), custom_call_target="tpu_custom_call" | custom-call | flops 1644167168 | bytes 9175040 | tf_op jit(solution)/shard_map/pallas_call | solution.py:89
  40.5 2.6 %collective-permute-done.1.refs_8_ = bf16[224,512]{1,0:T(8,128)(2,1)} collective-permute-done((bf16[224,512]{1,0:T(8,128)(2,1)}, bf16[224,512]{1,0:T(8,128)(2,1)}, u32[]{:S(2)}, u32[]{:S(2)}) %collective-permute-start.1) | collective-permute-done | bytes 229408 | tf_op jit(solution)/shard_map/ppermute | solution.py:446
  43.1 4.1 %all-to-all-start.1 = ((bf16[8,2,16,896]{3,2,1,0:T(8,128)(2,1)}), bf16[8,2,16,896]{3,2,1,0:T(8,128)(2,1)}, u32[]{:S(2)}, u32[]{:S(2)}) async-start(bf16[8,2,16,896]{3,2,1,0:T(8,128)(2,1)} %bitcast.44), calls=%async_computation.1 | async-start | bytes 917504 | tf_op jit(solution)/shard_map/all_to_all | solution.py:528
  51.3 1.8 %collective-permute-start.8 = (bf16[224,512]{1,0:T(8,128)(2,1)}, bf16[224,512]{1,0:T(8,128)(2,1)}, u32[]{:S(2)}, u32[]{:S(2)}) collective-permute-start(bf16[224,512]{1,0:T(8,128)(2,1)} %collective-permute-done.1.refs_8_), channel_id=1, source_target_pairs={{0,2},{2,0},{4,6},{6,4},{1,3},{3,1},{5,7},{7,5},{8,10},{10,8},{12,... | collective-permute-start | bytes 688136 | tf_op jit(solution)/shard_map/ppermute | solution.py:446
  53.2 2.1 %collective-permute-done.13.refs_9_ = bf16[224,512]{1,0:T(8,128)(2,1)} collective-permute-done((bf16[224,512]{1,0:T(8,128)(2,1)}, bf16[224,512]{1,0:T(8,128)(2,1)}, u32[]{:S(2)}, u32[]{:S(2)}) %collective-permute-start.13) | collective-permute-done | bytes 229408 | tf_op jit(solution)/shard_map/ppermute | solution.py:460
  56.8 3.4 %collective-permute-done.5.refs_7_ = bf16[224,512]{1,0:T(8,128)(2,1)} collective-permute-done((bf16[224,512]{1,0:T(8,128)(2,1)S(1)}, bf16[224,512]{1,0:T(8,128)(2,1)}, u32[]{:S(2)}, u32[]{:S(2)}) %collective-permute-start.5) | collective-permute-done | bytes 229408 | tf_op jit(solution)/shard_map/ppermute | solution.py:460
  64.4 4.5 %collective-permute-done.7.refs_1_.refs_9_ = bf16[224,512]{1,0:T(8,128)(2,1)} collective-permute-done((bf16[224,512]{1,0:T(8,128)(2,1)}, bf16[224,512]{1,0:T(8,128)(2,1)}, u32[]{:S(2)}, u32[]{:S(2)}) %collective-permute-start.7) | collective-permute-done | bytes 229408 | tf_op jit(solution)/shard_map/ppermute | solution.py:460
  72.1 9.7 %shard_map.148 = (bf16[128,2048]{1,0:T(8,128)(2,1)}, bf16[128,2048]{1,0:T(8,128)(2,1)}, bf16[128,2048]{1,0:T(8,128)(2,1)}, bf16[128,2048]{1,0:T(8,128)(2,1)}, bf...) custom-call(s32[6]{0:T(128)S(1)} %shard_map.147.plan, ...), custom_call_target="tpu_custom_call" | custom-call | flops 2818572288 | bytes 6553600 | tf_op jit(solution)/shard_map/pallas_call | solution.py:331
  83.5 10.6 %shard_map.149 = (bf16[128,2048]{1,0:T(8,128)(2,1)}, bf16[128,2048]{1,0:T(8,128)(2,1)}, bf16[128,2048]{1,0:T(8,128)(2,1)}, bf16[128,2048]{1,0:T(8,128)(2,1)}, bf...) custom-call(s32[6]{0:T(128)S(1)} %get-tuple-element.70.plan, ...), custom_call_target="tpu_custom_call", output_to_operand_aliasing={{0}: (16, {}), {1}: (17, {}), {2}: (18, {}), {3}: (19, {})} | custom-call | flops 2818572288 | bytes 6553600 | tf_op jit(solution)/shard_map/pallas_call | solution.py:331
  94.6 1.8 %collective-permute-done.17 = bf16[8,2,16,896]{3,2,1,0:T(8,128)(2,1)S(1)} collective-permute-done((bf16[8,2,16,896]{3,2,1,0:T(8,128)(2,1)S(1)}, bf16[8,2,16,896]{3,2,1,0:T(8,128)(2,1)S(1)}, u32[]{:S(2)}, u32[]{:S(2)}) %collective-permute-start.17) | collective-permute-done | bytes 458784 | tf_op jit(solution)/shard_map/ppermute | solution.py:442
  97.3 5.3 %all-to-all-start.2 = ((bf16[8,2,16,896]{3,2,1,0:T(8,128)(2,1)}), bf16[8,2,16,896]{3,2,1,0:T(8,128)(2,1)}, u32[]{:S(2)}, u32[]{:S(2)}) async-start(bf16[8,2,16,896]{3,2,1,0:T(8,128)(2,1)} %bitcast.37), calls=%async_computation.2 | async-start | bytes 917504 | tf_op jit(solution)/shard_map/all_to_all | solution.py:554
  102.6 1.6 shard_map.151
  105.7 2.4 %collective-permute-done.20 = bf16[2,2,224,512]{3,2,1,0:T(8,128)(2,1)} collective-permute-done((bf16[2,2,224,512]{3,2,1,0:T(8,128)(2,1)}, bf16[2,2,224,512]{3,2,1,0:T(8,128)(2,1)}, u32[]{:S(2)}, u32[]{:S(2)}) %collective-permute-start.20) | collective-permute-done | bytes 917536 | tf_op jit(solution)/shard_map/ppermute | solution.py:460
  108.1 1.6 shard_map.152
  109.7 2.2 %collective-permute-start.22 = (bf16[2,224,512]{2,1,0:T(8,128)(2,1)S(1)}, bf16[2,224,512]{2,1,0:T(8,128)(2,1)S(1)}, u32[]{:S(2)}, u32[]{:S(2)}) collective-permute-start(bf16[2,224,512]{2,1,0:T(8,128)(2,1)S(1)} %get-tuple-element.62), channel_id=1, source_target_pairs={{0,8},{1,17},{8,0},{9,25},{16,24},{17,1},{24,16},{25,9},{2,10},{3,... | collective-permute-start | bytes 1376264 | tf_op jit(solution)/shard_map/ppermute | solution.py:460
  113.6 2.9 %collective-permute-start.21 = (bf16[1,224,512]{2,1,0:T(8,128)(2,1)}, bf16[1,224,512]{2,1,0:T(8,128)(2,1)}, u32[]{:S(2)}, u32[]{:S(2)}) collective-permute-start(bf16[1,224,512]{2,1,0:T(8,128)(2,1)} %get-tuple-element.60), channel_id=1, source_target_pairs={{0,4},{2,6},{4,0},{6,2},{1,5},{3,7},{5,1},{7,3},{8,12},{10,14},{12... | collective-permute-start | bytes 688136 | tf_op jit(solution)/shard_map/ppermute | solution.py:446
  119.3 2.7 %collective-permute-start.23 = (bf16[1,224,512]{2,1,0:T(8,128)(2,1)}, bf16[1,224,512]{2,1,0:T(8,128)(2,1)}, u32[]{:S(2)}, u32[]{:S(2)}) collective-permute-start(bf16[1,224,512]{2,1,0:T(8,128)(2,1)} %get-tuple-element.63), channel_id=1, source_target_pairs={{0,2},{2,0},{4,6},{6,4},{1,3},{3,1},{5,7},{7,5},{8,10},{10,8},{12,... | collective-permute-start | bytes 688136 | tf_op jit(solution)/shard_map/ppermute | solution.py:446
  122.0 2.4 %collective-permute-start.24 = (bf16[1,224,512]{2,1,0:T(8,128)(2,1)}, bf16[1,224,512]{2,1,0:T(8,128)(2,1)}, u32[]{:S(2)}, u32[]{:S(2)}) collective-permute-start(bf16[1,224,512]{2,1,0:T(8,128)(2,1)} %get-tuple-element.64), channel_id=1, source_target_pairs={{0,6},{2,4},{4,2},{6,0},{1,7},{3,5},{5,3},{7,1},{8,14},{10,12},{12... | collective-permute-start | bytes 688136 | tf_op jit(solution)/shard_map/ppermute | solution.py:446
  124.4 5.3 %collective-permute-done.21.refs_0_.refs_1_ = bf16[1,224,512]{2,1,0:T(8,128)(2,1)} collective-permute-done((bf16[1,224,512]{2,1,0:T(8,128)(2,1)}, bf16[1,224,512]{2,1,0:T(8,128)(2,1)}, u32[]{:S(2)}, u32[]{:S(2)}) %collective-permute-start.21) | collective-permute-done | bytes 229408 | tf_op jit(solution)/shard_map/ppermute | solution.py:446
  129.6 6.5 %shard_map.154.refs_4_ = bf16[32,16,896]{2,1,0:T(8,128)(2,1)} custom-call(s32[16]{0:T(128)S(1)} %bitcast.35, bf16[16,16,896]{2,1,0:T(8,128)(2,1)} %bitcast.16.grad_ref, bf16[16,16,896]{2,1,0:T(8,128)(2,1)} %get-tuple-element.51.used_ref, bf16[256,1792]{1,0:T(8,128)(2,1)} %get-tuple-element.52.slope_ref, f32[1,896]{1,0:T(1,128)S(1)} %reshape.106.gain_ref, ...), custom_call_target="tpu_custom_call" | custom-call | flops 1644167168 | bytes 9175040 | tf_op jit(solution)/shard_map/pallas_call | solution.py:162
  136.1 4.5 %all-to-all-start.3 = ((bf16[8,4,16,896]{3,2,1,0:T(8,128)(2,1)}), bf16[8,4,16,896]{3,2,1,0:T(8,128)(2,1)S(1)}, u32[]{:S(2)}, u32[]{:S(2)}) async-start(bf16[8,4,16,896]{3,2,1,0:T(8,128)(2,1)} %bitcast.36), calls=%async_computation.3 | async-start | bytes 1835008 | tf_op jit(solution)/shard_map/all_to_all | solution.py:595
  143.3 4.6 %collective-permute-start.26 = (bf16[224,512]{1,0:T(8,128)(2,1)S(1)}, bf16[224,512]{1,0:T(8,128)(2,1)S(1)}, u32[]{:S(2)}, u32[]{:S(2)}) collective-permute-start(bf16[224,512]{1,0:T(8,128)(2,1)S(1)} %bitcast.32), channel_id=1, source_target_pairs={{0,16},{1,9},{8,24},{9,1},{16,0},{17,25},{24,8},{25,17},{2,18},{3,... | collective-permute-start | bytes 688136 | tf_op jit(solution)/shard_map/ppermute | solution.py:460
  148.0 6.3 %collective-permute-start.27 = (bf16[224,512]{1,0:T(8,128)(2,1)S(1)}, bf16[224,512]{1,0:T(8,128)(2,1)S(1)}, u32[]{:S(2)}, u32[]{:S(2)}) collective-permute-start(bf16[224,512]{1,0:T(8,128)(2,1)S(1)} %collective-permute-done.25.refs_1_), channel_id=1, source_target_pairs={{0,16},{1,9},{8,24},{9,1},{16,0},{17,25},{24,8},{25,17},{2,18},{3,... | collective-permute-start | bytes 688136 | tf_op jit(solution)/shard_map/ppermute | solution.py:460
  154.3 2.3 %select_bitcast_fusion = (bf16[1,128,2048]{2,1,0:T(8,128)(2,1)}, bf16[1,128,2048]{2,1,0:T(8,128)(2,1)}) fusion(bf16[128,2048]{1,0:T(8,128)(2,1)S(1)} %copy-done.5, bf16[128,2048]{1,0:T(8,128)(2,1)} %collective-permute-done.16, pred[2048]{0:T(1024)(128)(4,1)S(1)} %fusion.1, bf16[128,2048]{1,0:T(8,128)(2,1)S(1)} %copy-done.4, ...), kind=kLoop, calls=%fused_computation.1 | loop fusion | flops 524288 | bytes 3147776 | tf_op jit(solution)/shard_map/broadcast_in_dim | solution.py:601
  156.6 1.7 %collective-permute-done.27.refs_3_ = bf16[224,512]{1,0:T(8,128)(2,1)S(1)} collective-permute-done((bf16[224,512]{1,0:T(8,128)(2,1)S(1)}, bf16[224,512]{1,0:T(8,128)(2,1)S(1)}, u32[]{:S(2)}, u32[]{:S(2)}) %collective-permute-start.27) | collective-permute-done | bytes 229408 | tf_op jit(solution)/shard_map/ppermute | solution.py:460
  158.3 1.9 %shard_map.157 = (f32[896,256]{1,0:T(8,128)}, f32[896,256]{1,0:T(8,128)}) custom-call(s32[4]{0:T(128)S(1)} %fusion.5.plan, bf16[224,512]{1,0:T(8,128)(2,1)S(1)} %bitcast.33, bf16[224,512]{1,0:T(8,128)(2,1)S(1)} %collective-permute-done.25.refs_1_, bf16[224,512]{1,0:T(8,128)(2,1)S(1)} %collective-permute-done.26.refs_2_, ...), custom_call_target="tpu_custom_call" | custom-call | flops 8000000000 | bytes 24000000 | tf_op jit(solution)/shard_map/pallas_call | solution.py:427
  160.2 4.2 %all-to-all-done.3 = bf16[8,4,16,896]{3,2,1,0:T(8,128)(2,1)S(1)} async-done(((bf16[8,4,16,896]{3,2,1,0:T(8,128)(2,1)}), bf16[8,4,16,896]{3,2,1,0:T(8,128)(2,1)S(1)}, u32[]{:S(2)}, u32[]{:S(2)}) %all-to-all-start.3) | async-done | bytes 917536 | tf_op jit(solution)/shard_map/all_to_all | solution.py:595
  (69 shorter events, 27.3 us)
Async XLA Ops:
  3.0 30.7 %all-to-all-start = ((bf16[8,4,16,896]{3,2,1,0:T(8,128)(2,1)}), bf16[8,4,16,896]{3,2,1,0:T(8,128)(2,1)}, u32[]{:S(2)}, u32[]{:S(2)}) async-start(bf16[8,4,16,896]{3,2,1,0:T(8,128)(2,1)} %bitcast.39), calls=%async_computation | async-start | bytes 1835008 | tf_op jit(solution)/shard_map/all_to_all | solution.py:519
  11.0 29.5 %collective-permute-start = (bf16[224,512]{1,0:T(8,128)(2,1)}, bf16[224,512]{1,0:T(8,128)(2,1)S(1)}, u32[]{:S(2)}, u32[]{:S(2)}) collective-permute-start(bf16[224,512]{1,0:T(8,128)(2,1)} %pad_maximum_fusion), channel_id=1, source_target_pairs={{0,2},{2,0},{4,6},{6,4},{1,3},{3,1},{5,7},{7,5},{8,10},{10,8},{12,... | collective-permute-start | bytes 688136 | tf_op jit(solution)/shard_map/ppermute | solution.py:446
  13.0 30.0 %collective-permute-start.1 = (bf16[224,512]{1,0:T(8,128)(2,1)}, bf16[224,512]{1,0:T(8,128)(2,1)}, u32[]{:S(2)}, u32[]{:S(2)}) collective-permute-start(bf16[224,512]{1,0:T(8,128)(2,1)} %pad_maximum_fusion), channel_id=1, source_target_pairs={{0,4},{2,6},{4,0},{6,2},{1,5},{3,7},{5,1},{7,3},{8,12},{10,14},{12... | collective-permute-start | bytes 688136 | tf_op jit(solution)/shard_map/ppermute | solution.py:446
  43.1 21.2 %all-to-all-start.1 = ((bf16[8,2,16,896]{3,2,1,0:T(8,128)(2,1)}), bf16[8,2,16,896]{3,2,1,0:T(8,128)(2,1)}, u32[]{:S(2)}, u32[]{:S(2)}) async-start(bf16[8,2,16,896]{3,2,1,0:T(8,128)(2,1)} %bitcast.44), calls=%async_computation.1 | async-start | bytes 917504 | tf_op jit(solution)/shard_map/all_to_all | solution.py:528
  47.2 8.1 %collective-permute-start.13 = (bf16[224,512]{1,0:T(8,128)(2,1)}, bf16[224,512]{1,0:T(8,128)(2,1)}, u32[]{:S(2)}, u32[]{:S(2)}) collective-permute-start(bf16[224,512]{1,0:T(8,128)(2,1)} %collective-permute-done.1.refs_8_), channel_id=1, source_target_pairs={{0,8},{1,17},{8,0},{9,25},{16,24},{17,1},{24,16},{25,9},{2,10},{3,... | collective-permute-start | bytes 688136 | tf_op jit(solution)/shard_map/ppermute | solution.py:460
  48.8 11.4 %collective-permute-start.5 = (bf16[224,512]{1,0:T(8,128)(2,1)S(1)}, bf16[224,512]{1,0:T(8,128)(2,1)}, u32[]{:S(2)}, u32[]{:S(2)}) collective-permute-start(bf16[224,512]{1,0:T(8,128)(2,1)S(1)} %collective-permute-done.refs_6_), channel_id=1, source_target_pairs={{0,8},{1,17},{8,0},{9,25},{16,24},{17,1},{24,16},{25,9},{2,10},{3,... | collective-permute-start | bytes 688136 | tf_op jit(solution)/shard_map/ppermute | solution.py:460
  49.3 10.9 %collective-permute-start.12 = (bf16[224,512]{1,0:T(8,128)(2,1)}, bf16[224,512]{1,0:T(8,128)(2,1)}, u32[]{:S(2)}, u32[]{:S(2)}) collective-permute-start(bf16[224,512]{1,0:T(8,128)(2,1)} %collective-permute-done.1.refs_8_), channel_id=1, source_target_pairs={{0,16},{1,9},{8,24},{9,1},{16,0},{17,25},{24,8},{25,17},{2,18},{3,... | collective-permute-start | bytes 688136 | tf_op jit(solution)/shard_map/ppermute | solution.py:460
  50.8 9.9 %collective-permute-start.6 = (bf16[224,512]{1,0:T(8,128)(2,1)S(1)}, bf16[224,512]{1,0:T(8,128)(2,1)}, u32[]{:S(2)}, u32[]{:S(2)}) collective-permute-start(bf16[224,512]{1,0:T(8,128)(2,1)S(1)} %collective-permute-done.refs_6_), channel_id=1, source_target_pairs={{0,16},{1,9},{8,24},{9,1},{16,0},{17,25},{24,8},{25,17},{2,18},{3,... | collective-permute-start | bytes 688136 | tf_op jit(solution)/shard_map/ppermute | solution.py:460
  51.3 11.4 %collective-permute-start.8 = (bf16[224,512]{1,0:T(8,128)(2,1)}, bf16[224,512]{1,0:T(8,128)(2,1)}, u32[]{:S(2)}, u32[]{:S(2)}) collective-permute-start(bf16[224,512]{1,0:T(8,128)(2,1)} %collective-permute-done.1.refs_8_), channel_id=1, source_target_pairs={{0,2},{2,0},{4,6},{6,4},{1,3},{3,1},{5,7},{7,5},{8,10},{10,8},{12,... | collective-permute-start | bytes 688136 | tf_op jit(solution)/shard_map/ppermute | solution.py:446
  55.3 8.9 %collective-permute-start.14 = (bf16[224,512]{1,0:T(8,128)(2,1)}, bf16[224,512]{1,0:T(8,128)(2,1)}, u32[]{:S(2)}, u32[]{:S(2)}) collective-permute-start(bf16[224,512]{1,0:T(8,128)(2,1)} %collective-permute-done.13.refs_9_), channel_id=1, source_target_pairs={{0,16},{1,9},{8,24},{9,1},{16,0},{17,25},{24,8},{25,17},{2,18},{3,... | collective-permute-start | bytes 688136 | tf_op jit(solution)/shard_map/ppermute | solution.py:460
  60.2 11.9 %collective-permute-start.3 = (bf16[128,2048]{1,0:T(8,128)(2,1)}, bf16[128,2048]{1,0:T(8,128)(2,1)}, u32[]{:S(2)}, u32[]{:S(2)}) collective-permute-start(bf16[128,2048]{1,0:T(8,128)(2,1)} %bitcast.45), channel_id=1, source_target_pairs={{0,1},{1,0},{2,3},{3,2},{4,5},{5,4},{6,7},{7,6},{8,9},{9,8},{10,11... | collective-permute-start | bytes 1572872 | tf_op jit(solution)/shard_map/ppermute | solution.py:442
  60.2 11.9 %collective-permute-start.4 = (bf16[128,2048]{1,0:T(8,128)(2,1)}, bf16[128,2048]{1,0:T(8,128)(2,1)}, u32[]{:S(2)}, u32[]{:S(2)}) collective-permute-start(bf16[128,2048]{1,0:T(8,128)(2,1)} %bitcast.48), channel_id=1, source_target_pairs={{0,1},{1,0},{2,3},{3,2},{4,5},{5,4},{6,7},{7,6},{8,9},{9,8},{10,11... | collective-permute-start | bytes 1572872 | tf_op jit(solution)/shard_map/ppermute | solution.py:442
  60.7 8.2 %collective-permute-start.7 = (bf16[224,512]{1,0:T(8,128)(2,1)}, bf16[224,512]{1,0:T(8,128)(2,1)}, u32[]{:S(2)}, u32[]{:S(2)}) collective-permute-start(bf16[224,512]{1,0:T(8,128)(2,1)} %collective-permute-done.5.refs_7_), channel_id=1, source_target_pairs={{0,16},{1,9},{8,24},{9,1},{16,0},{17,25},{24,8},{25,17},{2,18},{3,... | collective-permute-start | bytes 688136 | tf_op jit(solution)/shard_map/ppermute | solution.py:460
  62.7 7.8 %collective-permute-start.9 = (bf16[224,512]{1,0:T(8,128)(2,1)}, bf16[224,512]{1,0:T(8,128)(2,1)}, u32[]{:S(2)}, u32[]{:S(2)}) collective-permute-start(bf16[224,512]{1,0:T(8,128)(2,1)} %collective-permute-done.8.refs_10_), channel_id=1, source_target_pairs={{0,8},{1,17},{8,0},{9,25},{16,24},{17,1},{24,16},{25,9},{2,10},{3,... | collective-permute-start | bytes 688136 | tf_op jit(solution)/shard_map/ppermute | solution.py:460
  64.2 7.9 %collective-permute-start.2 = (bf16[8,2,16,896]{3,2,1,0:T(8,128)(2,1)}, bf16[8,2,16,896]{3,2,1,0:T(8,128)(2,1)S(1)}, u32[]{:S(2)}, u32[]{:S(2)}) collective-permute-start(bf16[8,2,16,896]{3,2,1,0:T(8,128)(2,1)} %all-to-all-done.1.refs_0_), channel_id=1, source_target_pairs={{0,1},{1,0},{2,3},{3,2},{4,5},{5,4},{6,7},{7,6},{8,9},{9,8},{10,11... | collective-permute-start | bytes 1376264 | tf_op jit(solution)/shard_map/ppermute | solution.py:442
  68.9 14.6 %collective-permute-start.10 = (bf16[224,512]{1,0:T(8,128)(2,1)}, bf16[224,512]{1,0:T(8,128)(2,1)S(1)}, u32[]{:S(2)}, u32[]{:S(2)}) collective-permute-start(bf16[224,512]{1,0:T(8,128)(2,1)} %collective-permute-done.8.refs_10_), channel_id=1, source_target_pairs={{0,16},{1,9},{8,24},{9,1},{16,0},{17,25},{24,8},{25,17},{2,18},{3,... | collective-permute-start | bytes 688136 | tf_op jit(solution)/shard_map/ppermute | solution.py:460
  70.4 13.0 %collective-permute-start.11 = (bf16[224,512]{1,0:T(8,128)(2,1)}, bf16[224,512]{1,0:T(8,128)(2,1)S(1)}, u32[]{:S(2)}, u32[]{:S(2)}) collective-permute-start(bf16[224,512]{1,0:T(8,128)(2,1)} %collective-permute-done.9.refs_11_), channel_id=1, source_target_pairs={{0,16},{1,9},{8,24},{9,1},{16,0},{17,25},{24,8},{25,17},{2,18},{3,... | collective-permute-start | bytes 688136 | tf_op jit(solution)/shard_map/ppermute | solution.py:460
  81.9 20.7 %collective-permute-start.18 = (bf16[2,2,224,512]{3,2,1,0:T(8,128)(2,1)}, bf16[2,2,224,512]{3,2,1,0:T(8,128)(2,1)}, u32[]{:S(2)}, u32[]{:S(2)}) collective-permute-start(bf16[2,2,224,512]{3,2,1,0:T(8,128)(2,1)} %get-tuple-element.54), channel_id=1, source_target_pairs={{0,16},{1,9},{8,24},{9,1},{16,0},{17,25},{24,8},{25,17},{2,18},{3,... | collective-permute-start | bytes 2752520 | tf_op jit(solution)/shard_map/ppermute | solution.py:460
  94.1 14.0 %collective-permute-start.20 = (bf16[2,2,224,512]{3,2,1,0:T(8,128)(2,1)}, bf16[2,2,224,512]{3,2,1,0:T(8,128)(2,1)}, u32[]{:S(2)}, u32[]{:S(2)}) collective-permute-start(bf16[2,2,224,512]{3,2,1,0:T(8,128)(2,1)} %get-tuple-element.58), channel_id=1, source_target_pairs={{0,16},{1,9},{8,24},{9,1},{16,0},{17,25},{24,8},{25,17},{2,18},{3,... | collective-permute-start | bytes 2752520 | tf_op jit(solution)/shard_map/ppermute | solution.py:460
  94.6 1.8 %collective-permute-start.17 = (bf16[8,2,16,896]{3,2,1,0:T(8,128)(2,1)S(1)}, bf16[8,2,16,896]{3,2,1,0:T(8,128)(2,1)S(1)}, u32[]{:S(2)}, u32[]{:S(2)}) collective-permute-start(bf16[8,2,16,896]{3,2,1,0:T(8,128)(2,1)S(1)} %get-tuple-element.50), channel_id=1, source_target_pairs={{0,1},{1,0},{2,3},{3,2},{4,5},{5,4},{6,7},{7,6},{8,9},{9,8},{10,11... | collective-permute-start | bytes 1376264 | tf_op jit(solution)/shard_map/ppermute | solution.py:442
  97.3 27.1 %all-to-all-start.2 = ((bf16[8,2,16,896]{3,2,1,0:T(8,128)(2,1)}), bf16[8,2,16,896]{3,2,1,0:T(8,128)(2,1)}, u32[]{:S(2)}, u32[]{:S(2)}) async-start(bf16[8,2,16,896]{3,2,1,0:T(8,128)(2,1)} %bitcast.37), calls=%async_computation.2 | async-start | bytes 917504 | tf_op jit(solution)/shard_map/all_to_all | solution.py:554
  104.3 8.5 %collective-permute-start.19 = (bf16[2,224,512]{2,1,0:T(8,128)(2,1)S(1)}, bf16[2,224,512]{2,1,0:T(8,128)(2,1)S(1)}, u32[]{:S(2)}, u32[]{:S(2)}) collective-permute-start(bf16[2,224,512]{2,1,0:T(8,128)(2,1)S(1)} %get-tuple-element.56), channel_id=1, source_target_pairs={{0,8},{1,17},{8,0},{9,25},{16,24},{17,1},{24,16},{25,9},{2,10},{3,... | collective-permute-start | bytes 1376264 | tf_op jit(solution)/shard_map/ppermute | solution.py:460
  109.7 8.7 %collective-permute-start.22 = (bf16[2,224,512]{2,1,0:T(8,128)(2,1)S(1)}, bf16[2,224,512]{2,1,0:T(8,128)(2,1)S(1)}, u32[]{:S(2)}, u32[]{:S(2)}) collective-permute-start(bf16[2,224,512]{2,1,0:T(8,128)(2,1)S(1)} %get-tuple-element.62), channel_id=1, source_target_pairs={{0,8},{1,17},{8,0},{9,25},{16,24},{17,1},{24,16},{25,9},{2,10},{3,... | collective-permute-start | bytes 1376264 | tf_op jit(solution)/shard_map/ppermute | solution.py:460
  113.6 16.0 %collective-permute-start.21 = (bf16[1,224,512]{2,1,0:T(8,128)(2,1)}, bf16[1,224,512]{2,1,0:T(8,128)(2,1)}, u32[]{:S(2)}, u32[]{:S(2)}) collective-permute-start(bf16[1,224,512]{2,1,0:T(8,128)(2,1)} %get-tuple-element.60), channel_id=1, source_target_pairs={{0,4},{2,6},{4,0},{6,2},{1,5},{3,7},{5,1},{7,3},{8,12},{10,14},{12... | collective-permute-start | bytes 688136 | tf_op jit(solution)/shard_map/ppermute | solution.py:446
  116.6 37.8 %collective-permute-start.15 = (bf16[128,2048]{1,0:T(8,128)(2,1)}, bf16[128,2048]{1,0:T(8,128)(2,1)}, u32[]{:S(2)}, u32[]{:S(2)}) collective-permute-start(bf16[128,2048]{1,0:T(8,128)(2,1)} %get-tuple-element.46), channel_id=1, source_target_pairs={{0,1},{1,0},{2,3},{3,2},{4,5},{5,4},{6,7},{7,6},{8,9},{9,8},{10,11... | collective-permute-start | bytes 1572872 | tf_op jit(solution)/shard_map/ppermute | solution.py:442
  116.6 37.8 %collective-permute-start.16 = (bf16[128,2048]{1,0:T(8,128)(2,1)}, bf16[128,2048]{1,0:T(8,128)(2,1)}, u32[]{:S(2)}, u32[]{:S(2)}) collective-permute-start(bf16[128,2048]{1,0:T(8,128)(2,1)} %get-tuple-element.48), channel_id=1, source_target_pairs={{0,1},{1,0},{2,3},{3,2},{4,5},{5,4},{6,7},{7,6},{8,9},{9,8},{10,11... | collective-permute-start | bytes 1572872 | tf_op jit(solution)/shard_map/ppermute | solution.py:442
  119.3 21.3 %collective-permute-start.23 = (bf16[1,224,512]{2,1,0:T(8,128)(2,1)}, bf16[1,224,512]{2,1,0:T(8,128)(2,1)}, u32[]{:S(2)}, u32[]{:S(2)}) collective-permute-start(bf16[1,224,512]{2,1,0:T(8,128)(2,1)} %get-tuple-element.63), channel_id=1, source_target_pairs={{0,2},{2,0},{4,6},{6,4},{1,3},{3,1},{5,7},{7,5},{8,10},{10,8},{12,... | collective-permute-start | bytes 688136 | tf_op jit(solution)/shard_map/ppermute | solution.py:446
  122.0 18.7 %collective-permute-start.24 = (bf16[1,224,512]{2,1,0:T(8,128)(2,1)}, bf16[1,224,512]{2,1,0:T(8,128)(2,1)}, u32[]{:S(2)}, u32[]{:S(2)}) collective-permute-start(bf16[1,224,512]{2,1,0:T(8,128)(2,1)} %get-tuple-element.64), channel_id=1, source_target_pairs={{0,6},{2,4},{4,2},{6,0},{1,7},{3,5},{5,3},{7,1},{8,14},{10,12},{12... | collective-permute-start | bytes 688136 | tf_op jit(solution)/shard_map/ppermute | solution.py:446
  136.1 28.3 %all-to-all-start.3 = ((bf16[8,4,16,896]{3,2,1,0:T(8,128)(2,1)}), bf16[8,4,16,896]{3,2,1,0:T(8,128)(2,1)S(1)}, u32[]{:S(2)}, u32[]{:S(2)}) async-start(bf16[8,4,16,896]{3,2,1,0:T(8,128)(2,1)} %bitcast.36), calls=%async_computation.3 | async-start | bytes 1835008 | tf_op jit(solution)/shard_map/all_to_all | solution.py:595
  141.9 6.1 %collective-permute-start.25 = (bf16[224,512]{1,0:T(8,128)(2,1)S(1)}, bf16[224,512]{1,0:T(8,128)(2,1)S(1)}, u32[]{:S(2)}, u32[]{:S(2)}) collective-permute-start(bf16[224,512]{1,0:T(8,128)(2,1)S(1)} %bitcast.31), channel_id=1, source_target_pairs={{0,8},{1,17},{8,0},{9,25},{16,24},{17,1},{24,16},{25,9},{2,10},{3,... | collective-permute-start | bytes 688136 | tf_op jit(solution)/shard_map/ppermute | solution.py:460
  143.3 13.3 %collective-permute-start.26 = (bf16[224,512]{1,0:T(8,128)(2,1)S(1)}, bf16[224,512]{1,0:T(8,128)(2,1)S(1)}, u32[]{:S(2)}, u32[]{:S(2)}) collective-permute-start(bf16[224,512]{1,0:T(8,128)(2,1)S(1)} %bitcast.32), channel_id=1, source_target_pairs={{0,16},{1,9},{8,24},{9,1},{16,0},{17,25},{24,8},{25,17},{2,18},{3,... | collective-permute-start | bytes 688136 | tf_op jit(solution)/shard_map/ppermute | solution.py:460
  148.0 10.3 %collective-permute-start.27 = (bf16[224,512]{1,0:T(8,128)(2,1)S(1)}, bf16[224,512]{1,0:T(8,128)(2,1)S(1)}, u32[]{:S(2)}, u32[]{:S(2)}) collective-permute-start(bf16[224,512]{1,0:T(8,128)(2,1)S(1)} %collective-permute-done.25.refs_1_), channel_id=1, source_target_pairs={{0,16},{1,9},{8,24},{9,1},{16,0},{17,25},{24,8},{25,17},{2,18},{3,... | collective-permute-start | bytes 688136 | tf_op jit(solution)/shard_map/ppermute | solution.py:460
  (8 other events, 183.0 us)

commit v3 on v1

--- a/solution.py
+++ b/solution.py
@@ -192,14 +192,14 @@
     steps = len(kinds)
     own_enc, other_enc = take(2)
     token_refs = (take(2), take(2))
-    weight_refs = [take({"whole": 1, "columns": 2, "rows": lines}[kind]) for kind in kinds]
+    weight_refs = [take({"columns": 2, "rows": lines}[kind]) for kind in kinds]
     if last:
         (back_in,) = take(1)
         take(4)
     out_refs = (take(2), take(2))
     back_refs = take(2 if last else 1)
     grad_halves = take(2)
-    rows, rows_t, back, weight = refs
+    rows, turned, rows_t, back, weight = refs
     step = pl.program_id(0)
     shares, mine, piece, width = own_enc.shape
     span = shares * piece
@@ -211,16 +211,17 @@
         for s in range(2 * mine):
             source = own_enc if s < mine else other_enc
             rows[s * span : (s + 1) * span, :] = merge_rows(source[:, s % mine])
-        rows_t[...] = rows[...].T
-        back[...] = back_in[...] if last else jnp.zeros_like(back)
+        turned[...] = rows[...].T
+        for i in range(lines):
+            start = pl.multiple_of(plan[steps + i] * part_rows, 16)
+            rows_t[i * part_rows : (i + 1) * part_rows, :] = turned[pl.ds(start, part_rows), :]
+        back[...] = back_in[...].astype(jnp.float32) if last else jnp.zeros_like(back)
 
     for shard, (kind, found) in enumerate(zip(kinds, weight_refs)):
 
         @pl.when(step == shard)
         def _(kind=kind, found=found):
-            if kind == "whole":
-                weight[...] = found[0][...]
-            elif kind == "columns":
+            if kind == "columns":
                 weight[:, :columns] = found[0][...]
                 weight[:, columns:] = found[1][...]
             else:
@@ -271,16 +272,17 @@
         ],
         axis=0,
     )
+    part_grads = dot(rows_t[...], both_grad).astype(jnp.bfloat16)
     for i in range(lines):
-        start = pl.multiple_of(plan[steps + i] * part_rows, 16)
-        part_grad = dot(rows_t[pl.ds(start, part_rows), :], both_grad).astype(jnp.bfloat16)
-        grad_halves[2 * i // lines][i % (lines // 2), 0] = part_grad
+        grad_halves[2 * i // lines][i % (lines // 2), 0] = part_grads[
+            i * part_rows : (i + 1) * part_rows
+        ]
     back[...] += dot_nt(both_grad, weight[...])
 
     @pl.when(step == steps - 1)
     def _():
         if not last:
-            back_refs[0][...] = back[...]
+            back_refs[0][...] = back[...].astype(jnp.bfloat16)
         else:
             for s in range(2 * mine):
                 block = back[s * span : (s + 1) * span, :].reshape(shares, piece, width)
@@ -303,7 +305,7 @@
     out = functools.partial(jax.ShapeDtypeStruct, dtype=jnp.bfloat16)
     operands = [plan, own_enc, other_enc, *map(in_hbm, token_arrays), *arrays]
     in_specs = [enc_spec] * 2 + [token_spec] * 4 + [whole(*value.shape) for value in arrays]
-    back_shapes, aliases = [jax.ShapeDtypeStruct((all_rows, width), jnp.float32)], {}
+    back_shapes, aliases = [out((all_rows, width))], {}
     if last:
         aliases = {len(operands) + 1 + i: i for i in range(4)}
         operands += [earlier[4], *map(in_hbm, earlier[:4])]
@@ -320,6 +322,7 @@
             + [pl.BlockSpec((lines // 2, 1, part_rows, 2 * columns), lambda j, p: (0, j, 0, 0))] * 2,
             scratch_shapes=[
                 pltpu.VMEM((all_rows, width), jnp.bfloat16),
+                pltpu.VMEM((width, all_rows), jnp.bfloat16),
                 pltpu.VMEM((width, all_rows), jnp.bfloat16),
                 pltpu.VMEM((all_rows, width), jnp.float32),
                 pltpu.VMEM((width, 2 * columns), jnp.bfloat16),
@@ -372,8 +375,26 @@
     )(*terms, *after)
 
 
-def join_kernel(count, plan, *refs):
-    parts, outs = refs[:count], refs[count:]
+def copy_kernel(plan, *refs):
+    out = refs[-1]
+    for i in range(plan.shape[0]):
+        out[i] = plan[i]
+
+
+def copy_plan(plan, others):
+    scalars = pl.BlockSpec(memory_space=pltpu.SMEM)
+    return pl.pallas_call(
+        copy_kernel,
+        in_specs=[scalars] + [pl.BlockSpec(memory_space=pl.ANY)] * len(others),
+        out_specs=scalars,
+        out_shape=jax.ShapeDtypeStruct(plan.shape, plan.dtype),
+        compiler_params=pltpu.CompilerParams(vmem_limit_bytes=SMALL_VMEM_BYTES),
+        cost_estimate=stated(4),
+    )(plan, *others)
+
+
+def join_kernel(plan, *refs):
+    parts, outs = refs[:-2], refs[-2:]
     part_rows, columns = parts[0].shape[0], outs[0].shape[1]
     for i, part in enumerate(parts):
         start = pl.multiple_of(plan[i] * part_rows, 16)
@@ -381,21 +402,21 @@
             out[pl.ds(start, part_rows), :] = part[:, k * columns : (k + 1) * columns].astype(out.dtype)
 
 
-def join_parts(plan, parts, outs, dtype, microseconds):
+def join_grads(plan, parts):
     part_rows, columns = parts[0].shape
     width = part_rows * len(parts)
     whole = lambda *shape: pl.BlockSpec(shape, lambda j, p: (0,) * len(shape))
     return pl.pallas_call(
-        functools.partial(join_kernel, len(parts)),
+        join_kernel,
         grid_spec=pltpu.PrefetchScalarGridSpec(
             num_scalar_prefetch=1,
             grid=(1,),
             in_specs=[whole(part_rows, columns)] * len(parts),
-            out_specs=[whole(width, columns // outs)] * outs,
-        ),
-        out_shape=[jax.ShapeDtypeStruct((width, columns // outs), dtype)] * outs,
+            out_specs=[whole(width, columns // 2)] * 2,
+        ),
+        out_shape=[jax.ShapeDtypeStruct((width, columns // 2), jnp.float32)] * 2,
         compiler_params=pltpu.CompilerParams(vmem_limit_bytes=SMALL_VMEM_BYTES),
-        cost_estimate=stated(microseconds),
+        cost_estimate=stated(8),
     )(plan, *parts)
 
 
@@ -491,11 +512,7 @@
     )
     shards = {0: ("columns", [in_hbm(key_weight), in_hbm(value_weight)])}
     for shift in range(1, chips):
-        found = gather_lines(part[shift], stages)
-        if shift == 1 or shift in even:
-            shards[shift] = ("whole", [*join_parts(part_lines, found, 1, jnp.bfloat16, 4)])
-        else:
-            shards[shift] = ("rows", found)
+        shards[shift] = ("rows", gather_lines(part[shift], stages))
     other_enc = swap_cores(own_enc)
 
     steps = ([0, *even], [*odd])
@@ -503,6 +520,8 @@
         jnp.concatenate([jnp.stack([(chip ^ shift) * 2 + core for shift in shifts]), part_lines])
         for shifts in steps
     ]
+    early = [value for shift in (1, *even) for value in shards[shift][1][lines // 2 :]]
+    plans[0] = copy_plan(plans[0], early)
     parted = [[shards[shift] for shift in shifts] for shifts in steps]
     first = attend(plans[0], lines, own_enc, other_enc, token_arrays, parted[0])
     last = attend(plans[1], lines, own_enc, other_enc, token_arrays, parted[1], first[:5])
@@ -547,13 +566,13 @@
         enc_up,
         enc_down,
         groups * holding,
-        [],
+        [terms[shift] for shift in even],
     )
     (share,) = sum_blocks([*terms.values()], (1,), [in_hbm(placed)])
     share = share[0]
     if lax.axis_size("far") > 1:
         share = lax.psum(share, "far")
-    weight_grads = join_parts(part_lines, gather_lines(share, stages), 2, jnp.float32, 10)
+    weight_grads = join_grads(part_lines, gather_lines(share, stages))
 
     returned = lax.all_to_all(
         placed.reshape(groups, holding, piece, width), SEQ, split_axis=0, concat_axis=0, tiled=True

time: 175 us -> 166 us (0.949); the launches traced: 175 us -> 164 us
  waiting for transfers between devices: 66.2 us -> 49.1 us
  starting transfers between devices: 53.1 us -> 64.4 us
  local copies, waits for them, and re-layouts: 8.31 us -> 4.34 us
    all_to_all x1, waiting for transfers between devices: 13.4 us -> 4.22 us  [on_device(): lax.all_to_all(placed.reshape(groups, holding, piece, width), SEQ, split_...]
    ppermute x6, waiting for transfers between devices: 15.3 us -> 8.31 us  [swap_chips(): lax.ppermute(value, 'z', [(z, z ^ shift) for z in range(lax.axis_size('z'...]
    ppermute x16, starting transfers between devices: 22.5 us -> 28.8 us  [swap_lines(): return lax.ppermute(value, ('line', 'core'), pairs)]
    unnamed x24 -> x16, local copies, waits for them, and re-layouts: 4 us -> 0.03 us
    ppermute x6, starting transfers between devices: 10.8 us -> 14.2 us  [swap_chips(): lax.ppermute(value, 'z', [(z, z ^ shift) for z in range(lax.axis_size('z'...]
    pallas_call x3 -> x2, Pallas kernels: 5.29 us -> 3.01 us  [the longest x1 1.87 us: join_grads(): pl.pallas_call(join_kernel, grid_spec=pltpu.PrefetchScalarGridSpec(num_sc...]
  transfers between devices with their start and end apart: 32 -> 32, of which waited for: 13 -> 13; matrix products, arithmetic and copies ran while one was open for 2% -> 2% of each run, Pallas kernels for 25% -> 26%
where the time goes in v3:
time: 166 us; the launch traced here: 164 us
  starting transfers between devices  64.4 us (39%)
  waiting for transfers between devices  49.1 us (30%)
  Pallas kernels  42.2 us (25%)
  local copies, waits for them, and re-layouts  4.34 us (3%)
  other arithmetic  3.07 us (2%)
    ppermute x16, starting transfers between devices, swap_lines(): return lax.ppermute(value, ('line', 'core'), pairs)  28.8 us
    pallas_call x2, Pallas kernels, attend(): pl.pallas_call(functools.partial(attend_kernel, kinds, lines, last), grid...  18.8 us
    all_to_all x1, waiting for transfers between devices, on_device(): lax.all_to_all(pieces, SEQ, split_axis=0, concat_axis=0, tiled=True)  18.3 us
    ppermute x16, waiting for transfers between devices, swap_lines(): return lax.ppermute(value, ('line', 'core'), pairs)  16.5 us
    ppermute x6, starting transfers between devices, swap_chips(): lax.ppermute(value, 'z', [(z, z ^ shift) for z in range(lax.axis_size('z'...  14.2 us
    ppermute x6, waiting for transfers between devices, swap_chips(): lax.ppermute(value, 'z', [(z, z ^ shift) for z in range(lax.axis_size('z'...  8.31 us
    pallas_call x6, Pallas kernels, sum_blocks(): pl.pallas_call(functools.partial(sum_kernel, len(terms), sizes), grid=(ti...  7.05 us
    pallas_call x1, Pallas kernels, encode_rows(): pl.pallas_call(encode_kernel, grid_spec=pltpu.PrefetchScalarGridSpec(num_...  6.77 us
  transfers between devices with their start and end apart: 32, of which 13 were waited for; matrix products, arithmetic and copies ran while one was open for 2% of the time, Pallas kernels for 26%

profile of v3, /device:TPU:0, one launch (start us, length us, event | category | flops | bytes accessed | tf_op | source)
XLA Modules:
  0.0 163.9 jit_solution(14752692172162337727)
XLA Ops:
  0.7 2.3 %copy.23 = bf16[4,8,16,896]{3,2,0,1:T(8,128)(2,1)} copy(bf16[4,8,16,896]{3,2,1,0:T(8,128)(2,1)} %bitcast.40) | data formatting | bytes 1835008 | tf_op jit(solution)/shard_map/reshape;squeeze | solution.py:500
  3.0 6.3 %all-to-all-start = ((bf16[8,4,16,896]{3,2,1,0:T(8,128)(2,1)}), bf16[8,4,16,896]{3,2,1,0:T(8,128)(2,1)}, u32[]{:S(2)}, u32[]{:S(2)}) async-start(bf16[8,4,16,896]{3,2,1,0:T(8,128)(2,1)} %bitcast.39), calls=%async_computation | async-start | bytes 1835008 | tf_op jit(solution)/shard_map/all_to_all | solution.py:501
  11.0 2.0 %collective-permute-start = (bf16[224,512]{1,0:T(8,128)(2,1)}, bf16[224,512]{1,0:T(8,128)(2,1)S(1)}, u32[]{:S(2)}, u32[]{:S(2)}) collective-permute-start(bf16[224,512]{1,0:T(8,128)(2,1)} %pad_maximum_fusion), channel_id=1, source_target_pairs={{0,2},{2,0},{4,6},{6,4},{1,3},{3,1},{5,7},{7,5},{8,10},{10,8},{12,... | collective-permute-start | bytes 688136 | tf_op jit(solution)/shard_map/ppermute | solution.py:428
  13.0 2.4 %collective-permute-start.1 = (bf16[224,512]{1,0:T(8,128)(2,1)}, bf16[224,512]{1,0:T(8,128)(2,1)}, u32[]{:S(2)}, u32[]{:S(2)}) collective-permute-start(bf16[224,512]{1,0:T(8,128)(2,1)} %pad_maximum_fusion), channel_id=1, source_target_pairs={{0,4},{2,6},{4,0},{6,2},{1,5},{3,7},{5,1},{7,3},{8,12},{10,14},{12... | collective-permute-start | bytes 688136 | tf_op jit(solution)/shard_map/ppermute | solution.py:428
  15.4 18.3 %all-to-all-done = bf16[8,4,16,896]{3,2,1,0:T(8,128)(2,1)} async-done(((bf16[8,4,16,896]{3,2,1,0:T(8,128)(2,1)}), bf16[8,4,16,896]{3,2,1,0:T(8,128)(2,1)}, u32[]{:S(2)}, u32[]{:S(2)}) %all-to-all-start) | async-done | bytes 917536 | tf_op jit(solution)/shard_map/all_to_all | solution.py:501
  33.7 6.8 %shard_map.146 = (bf16[16,16,896]{2,1,0:T(8,128)(2,1)}, bf16[16,16,896]{2,1,0:T(8,128)(2,1)}, bf16[256,1792]{1,0:T(8,128)(2,1)}) custom-call(s32[16]{0:T(128)S(1)} %bitcast.34, bf16[32,16,896]{2,1,0:T(8,128)(2,1)} %bitcast.5.rows_ref, f32[1,896]{1,0:T(1,128)S(1)} %reshape.106.gain_ref, bf16[896,1792]{1,0:T(8,128)(2,1)S(1)} %copy-done, bf16[1792,896]{1,0:T(8,128)(2,1)} %down_ref.3), custom_call_target="tpu_custom_call" | custom-call | flops 1644167168 | bytes 9175040 | tf_op jit(solution)/shard_map/pallas_call | solution.py:89
  40.5 2.6 %collective-permute-done.1.refs_8_ = bf16[224,512]{1,0:T(8,128)(2,1)} collective-permute-done((bf16[224,512]{1,0:T(8,128)(2,1)}, bf16[224,512]{1,0:T(8,128)(2,1)}, u32[]{:S(2)}, u32[]{:S(2)}) %collective-permute-start.1) | collective-permute-done | bytes 229408 | tf_op jit(solution)/shard_map/ppermute | solution.py:428
  43.1 4.1 %all-to-all-start.1 = ((bf16[8,2,16,896]{3,2,1,0:T(8,128)(2,1)}), bf16[8,2,16,896]{3,2,1,0:T(8,128)(2,1)}, u32[]{:S(2)}, u32[]{:S(2)}) async-start(bf16[8,2,16,896]{3,2,1,0:T(8,128)(2,1)} %bitcast.44), calls=%async_computation.1 | async-start | bytes 917504 | tf_op jit(solution)/shard_map/all_to_all | solution.py:510
  51.3 1.8 %collective-permute-start.8 = (bf16[224,512]{1,0:T(8,128)(2,1)}, bf16[224,512]{1,0:T(8,128)(2,1)}, u32[]{:S(2)}, u32[]{:S(2)}) collective-permute-start(bf16[224,512]{1,0:T(8,128)(2,1)} %collective-permute-done.1.refs_8_), channel_id=1, source_target_pairs={{0,2},{2,0},{4,6},{6,4},{1,3},{3,1},{5,7},{7,5},{8,10},{10,8},{12,... | collective-permute-start | bytes 688136 | tf_op jit(solution)/shard_map/ppermute | solution.py:428
  53.2 2.1 %collective-permute-done.13.refs_9_ = bf16[224,512]{1,0:T(8,128)(2,1)} collective-permute-done((bf16[224,512]{1,0:T(8,128)(2,1)}, bf16[224,512]{1,0:T(8,128)(2,1)}, u32[]{:S(2)}, u32[]{:S(2)}) %collective-permute-start.13) | collective-permute-done | bytes 229408 | tf_op jit(solution)/shard_map/ppermute | solution.py:442
  56.8 3.4 %collective-permute-done.5.refs_7_ = bf16[224,512]{1,0:T(8,128)(2,1)} collective-permute-done((bf16[224,512]{1,0:T(8,128)(2,1)S(1)}, bf16[224,512]{1,0:T(8,128)(2,1)}, u32[]{:S(2)}, u32[]{:S(2)}) %collective-permute-start.5) | collective-permute-done | bytes 229408 | tf_op jit(solution)/shard_map/ppermute | solution.py:442
  64.4 4.5 %collective-permute-done.7.refs_1_.refs_9_ = bf16[224,512]{1,0:T(8,128)(2,1)} collective-permute-done((bf16[224,512]{1,0:T(8,128)(2,1)}, bf16[224,512]{1,0:T(8,128)(2,1)}, u32[]{:S(2)}, u32[]{:S(2)}) %collective-permute-start.7) | collective-permute-done | bytes 229408 | tf_op jit(solution)/shard_map/ppermute | solution.py:442
  72.1 9.5 %shard_map.148 = (bf16[128,2048]{1,0:T(8,128)(2,1)}, bf16[128,2048]{1,0:T(8,128)(2,1)}, bf16[128,2048]{1,0:T(8,128)(2,1)}, bf16[128,2048]{1,0:T(8,128)(2,1)}, bf...) custom-call(s32[6]{0:T(128)S(1)} %shard_map.147.plan, ...), custom_call_target="tpu_custom_call" | custom-call | flops 2818572288 | bytes 6553600 | tf_op jit(solution)/shard_map/pallas_call | solution.py:314
  83.2 9.4 %shard_map.149 = (bf16[128,2048]{1,0:T(8,128)(2,1)}, bf16[128,2048]{1,0:T(8,128)(2,1)}, bf16[128,2048]{1,0:T(8,128)(2,1)}, bf16[128,2048]{1,0:T(8,128)(2,1)}, bf...) custom-call(s32[6]{0:T(128)S(1)} %get-tuple-element.70.plan, ...), custom_call_target="tpu_custom_call", output_to_operand_aliasing={{0}: (16, {}), {1}: (17, {}), {2}: (18, {}), {3}: (19, {})} | custom-call | flops 2818572288 | bytes 6553600 | tf_op jit(solution)/shard_map/pallas_call | solution.py:314
  93.2 1.8 %collective-permute-done.17 = bf16[8,2,16,896]{3,2,1,0:T(8,128)(2,1)S(1)} collective-permute-done((bf16[8,2,16,896]{3,2,1,0:T(8,128)(2,1)S(1)}, bf16[8,2,16,896]{3,2,1,0:T(8,128)(2,1)S(1)}, u32[]{:S(2)}, u32[]{:S(2)}) %collective-permute-start.17) | collective-permute-done | bytes 458784 | tf_op jit(solution)/shard_map/ppermute | solution.py:424
  95.8 5.3 %all-to-all-start.2 = ((bf16[8,2,16,896]{3,2,1,0:T(8,128)(2,1)}), bf16[8,2,16,896]{3,2,1,0:T(8,128)(2,1)}, u32[]{:S(2)}, u32[]{:S(2)}) async-start(bf16[8,2,16,896]{3,2,1,0:T(8,128)(2,1)} %bitcast.37), calls=%async_computation.2 | async-start | bytes 917504 | tf_op jit(solution)/shard_map/all_to_all | solution.py:536
  101.1 1.6 shard_map.151
  104.2 2.4 %collective-permute-done.20 = bf16[2,2,224,512]{3,2,1,0:T(8,128)(2,1)} collective-permute-done((bf16[2,2,224,512]{3,2,1,0:T(8,128)(2,1)}, bf16[2,2,224,512]{3,2,1,0:T(8,128)(2,1)}, u32[]{:S(2)}, u32[]{:S(2)}) %collective-permute-start.20) | collective-permute-done | bytes 917536 | tf_op jit(solution)/shard_map/ppermute | solution.py:442
  106.6 1.6 shard_map.152
  108.2 2.2 %collective-permute-start.22 = (bf16[2,224,512]{2,1,0:T(8,128)(2,1)S(1)}, bf16[2,224,512]{2,1,0:T(8,128)(2,1)S(1)}, u32[]{:S(2)}, u32[]{:S(2)}) collective-permute-start(bf16[2,224,512]{2,1,0:T(8,128)(2,1)S(1)} %get-tuple-element.62), channel_id=1, source_target_pairs={{0,8},{1,17},{8,0},{9,25},{16,24},{17,1},{24,16},{25,9},{2,10},{3,... | collective-permute-start | bytes 1376264 | tf_op jit(solution)/shard_map/ppermute | solution.py:442
  112.1 2.9 %collective-permute-start.21 = (bf16[1,224,512]{2,1,0:T(8,128)(2,1)}, bf16[1,224,512]{2,1,0:T(8,128)(2,1)}, u32[]{:S(2)}, u32[]{:S(2)}) collective-permute-start(bf16[1,224,512]{2,1,0:T(8,128)(2,1)} %get-tuple-element.60), channel_id=1, source_target_pairs={{0,4},{2,6},{4,0},{6,2},{1,5},{3,7},{5,1},{7,3},{8,12},{10,14},{12... | collective-permute-start | bytes 688136 | tf_op jit(solution)/shard_map/ppermute | solution.py:428
  117.8 2.7 %collective-permute-start.23 = (bf16[1,224,512]{2,1,0:T(8,128)(2,1)}, bf16[1,224,512]{2,1,0:T(8,128)(2,1)}, u32[]{:S(2)}, u32[]{:S(2)}) collective-permute-start(bf16[1,224,512]{2,1,0:T(8,128)(2,1)} %get-tuple-element.63), channel_id=1, source_target_pairs={{0,2},{2,0},{4,6},{6,4},{1,3},{3,1},{5,7},{7,5},{8,10},{10,8},{12,... | collective-permute-start | bytes 688136 | tf_op jit(solution)/shard_map/ppermute | solution.py:428
  120.5 2.4 %collective-permute-start.24 = (bf16[1,224,512]{2,1,0:T(8,128)(2,1)}, bf16[1,224,512]{2,1,0:T(8,128)(2,1)}, u32[]{:S(2)}, u32[]{:S(2)}) collective-permute-start(bf16[1,224,512]{2,1,0:T(8,128)(2,1)} %get-tuple-element.64), channel_id=1, source_target_pairs={{0,6},{2,4},{4,2},{6,0},{1,7},{3,5},{5,3},{7,1},{8,14},{10,12},{12... | collective-permute-start | bytes 688136 | tf_op jit(solution)/shard_map/ppermute | solution.py:428
  122.9 5.3 %collective-permute-done.21.refs_0_.refs_1_ = bf16[1,224,512]{2,1,0:T(8,128)(2,1)} collective-permute-done((bf16[1,224,512]{2,1,0:T(8,128)(2,1)}, bf16[1,224,512]{2,1,0:T(8,128)(2,1)}, u32[]{:S(2)}, u32[]{:S(2)}) %collective-permute-start.21) | collective-permute-done | bytes 229408 | tf_op jit(solution)/shard_map/ppermute | solution.py:428
  128.1 6.5 %shard_map.154.refs_4_ = bf16[32,16,896]{2,1,0:T(8,128)(2,1)} custom-call(s32[16]{0:T(128)S(1)} %bitcast.35, bf16[16,16,896]{2,1,0:T(8,128)(2,1)} %bitcast.16.grad_ref, bf16[16,16,896]{2,1,0:T(8,128)(2,1)} %get-tuple-element.51.used_ref, bf16[256,1792]{1,0:T(8,128)(2,1)} %get-tuple-element.52.slope_ref, f32[1,896]{1,0:T(1,128)S(1)} %reshape.106.gain_ref, ...), custom_call_target="tpu_custom_call" | custom-call | flops 1644167168 | bytes 9175040 | tf_op jit(solution)/shard_map/pallas_call | solution.py:162
  134.6 4.5 %all-to-all-start.3 = ((bf16[8,4,16,896]{3,2,1,0:T(8,128)(2,1)}), bf16[8,4,16,896]{3,2,1,0:T(8,128)(2,1)S(1)}, u32[]{:S(2)}, u32[]{:S(2)}) async-start(bf16[8,4,16,896]{3,2,1,0:T(8,128)(2,1)} %bitcast.36), calls=%async_computation.3 | async-start | bytes 1835008 | tf_op jit(solution)/shard_map/all_to_all | solution.py:577
  141.8 4.6 %collective-permute-start.26 = (bf16[224,512]{1,0:T(8,128)(2,1)S(1)}, bf16[224,512]{1,0:T(8,128)(2,1)S(1)}, u32[]{:S(2)}, u32[]{:S(2)}) collective-permute-start(bf16[224,512]{1,0:T(8,128)(2,1)S(1)} %bitcast.32), channel_id=1, source_target_pairs={{0,16},{1,9},{8,24},{9,1},{16,0},{17,25},{24,8},{25,17},{2,18},{3,... | collective-permute-start | bytes 688136 | tf_op jit(solution)/shard_map/ppermute | solution.py:442
  146.5 6.3 %collective-permute-start.27 = (bf16[224,512]{1,0:T(8,128)(2,1)S(1)}, bf16[224,512]{1,0:T(8,128)(2,1)S(1)}, u32[]{:S(2)}, u32[]{:S(2)}) collective-permute-start(bf16[224,512]{1,0:T(8,128)(2,1)S(1)} %collective-permute-done.25.refs_1_), channel_id=1, source_target_pairs={{0,16},{1,9},{8,24},{9,1},{16,0},{17,25},{24,8},{25,17},{2,18},{3,... | collective-permute-start | bytes 688136 | tf_op jit(solution)/shard_map/ppermute | solution.py:442
  152.8 2.3 %select_bitcast_fusion = (bf16[1,128,2048]{2,1,0:T(8,128)(2,1)}, bf16[1,128,2048]{2,1,0:T(8,128)(2,1)}) fusion(bf16[128,2048]{1,0:T(8,128)(2,1)S(1)} %copy-done.5, bf16[128,2048]{1,0:T(8,128)(2,1)} %collective-permute-done.16, pred[2048]{0:T(1024)(128)(4,1)S(1)} %fusion.1, bf16[128,2048]{1,0:T(8,128)(2,1)S(1)} %copy-done.4, ...), kind=kLoop, calls=%fused_computation.1 | loop fusion | flops 524288 | bytes 3147776 | tf_op jit(solution)/shard_map/broadcast_in_dim | solution.py:583
  155.1 1.7 %collective-permute-done.27.refs_3_ = bf16[224,512]{1,0:T(8,128)(2,1)S(1)} collective-permute-done((bf16[224,512]{1,0:T(8,128)(2,1)S(1)}, bf16[224,512]{1,0:T(8,128)(2,1)S(1)}, u32[]{:S(2)}, u32[]{:S(2)}) %collective-permute-start.27) | collective-permute-done | bytes 229408 | tf_op jit(solution)/shard_map/ppermute | solution.py:442
  156.8 1.9 %shard_map.157 = (f32[896,256]{1,0:T(8,128)}, f32[896,256]{1,0:T(8,128)}) custom-call(s32[4]{0:T(128)S(1)} %fusion.5.plan, bf16[224,512]{1,0:T(8,128)(2,1)S(1)} %bitcast.33, bf16[224,512]{1,0:T(8,128)(2,1)S(1)} %collective-permute-done.25.refs_1_, bf16[224,512]{1,0:T(8,128)(2,1)S(1)} %collective-permute-done.26.refs_2_, ...), custom_call_target="tpu_custom_call" | custom-call | flops 8000000000 | bytes 24000000 | tf_op jit(solution)/shard_map/pallas_call | solution.py:409
  158.7 4.2 %all-to-all-done.3 = bf16[8,4,16,896]{3,2,1,0:T(8,128)(2,1)S(1)} async-done(((bf16[8,4,16,896]{3,2,1,0:T(8,128)(2,1)}), bf16[8,4,16,896]{3,2,1,0:T(8,128)(2,1)S(1)}, u32[]{:S(2)}, u32[]{:S(2)}) %all-to-all-start.3) | async-done | bytes 917536 | tf_op jit(solution)/shard_map/all_to_all | solution.py:577
  (69 shorter events, 27.3 us)
Async XLA Ops:
  3.0 30.7 %all-to-all-start = ((bf16[8,4,16,896]{3,2,1,0:T(8,128)(2,1)}), bf16[8,4,16,896]{3,2,1,0:T(8,128)(2,1)}, u32[]{:S(2)}, u32[]{:S(2)}) async-start(bf16[8,4,16,896]{3,2,1,0:T(8,128)(2,1)} %bitcast.39), calls=%async_computation | async-start | bytes 1835008 | tf_op jit(solution)/shard_map/all_to_all | solution.py:501
  11.0 29.5 %collective-permute-start = (bf16[224,512]{1,0:T(8,128)(2,1)}, bf16[224,512]{1,0:T(8,128)(2,1)S(1)}, u32[]{:S(2)}, u32[]{:S(2)}) collective-permute-start(bf16[224,512]{1,0:T(8,128)(2,1)} %pad_maximum_fusion), channel_id=1, source_target_pairs={{0,2},{2,0},{4,6},{6,4},{1,3},{3,1},{5,7},{7,5},{8,10},{10,8},{12,... | collective-permute-start | bytes 688136 | tf_op jit(solution)/shard_map/ppermute | solution.py:428
  13.0 30.0 %collective-permute-start.1 = (bf16[224,512]{1,0:T(8,128)(2,1)}, bf16[224,512]{1,0:T(8,128)(2,1)}, u32[]{:S(2)}, u32[]{:S(2)}) collective-permute-start(bf16[224,512]{1,0:T(8,128)(2,1)} %pad_maximum_fusion), channel_id=1, source_target_pairs={{0,4},{2,6},{4,0},{6,2},{1,5},{3,7},{5,1},{7,3},{8,12},{10,14},{12... | collective-permute-start | bytes 688136 | tf_op jit(solution)/shard_map/ppermute | solution.py:428
  43.1 21.2 %all-to-all-start.1 = ((bf16[8,2,16,896]{3,2,1,0:T(8,128)(2,1)}), bf16[8,2,16,896]{3,2,1,0:T(8,128)(2,1)}, u32[]{:S(2)}, u32[]{:S(2)}) async-start(bf16[8,2,16,896]{3,2,1,0:T(8,128)(2,1)} %bitcast.44), calls=%async_computation.1 | async-start | bytes 917504 | tf_op jit(solution)/shard_map/all_to_all | solution.py:510
  47.2 8.1 %collective-permute-start.13 = (bf16[224,512]{1,0:T(8,128)(2,1)}, bf16[224,512]{1,0:T(8,128)(2,1)}, u32[]{:S(2)}, u32[]{:S(2)}) collective-permute-start(bf16[224,512]{1,0:T(8,128)(2,1)} %collective-permute-done.1.refs_8_), channel_id=1, source_target_pairs={{0,8},{1,17},{8,0},{9,25},{16,24},{17,1},{24,16},{25,9},{2,10},{3,... | collective-permute-start | bytes 688136 | tf_op jit(solution)/shard_map/ppermute | solution.py:442
  48.8 11.4 %collective-permute-start.5 = (bf16[224,512]{1,0:T(8,128)(2,1)S(1)}, bf16[224,512]{1,0:T(8,128)(2,1)}, u32[]{:S(2)}, u32[]{:S(2)}) collective-permute-start(bf16[224,512]{1,0:T(8,128)(2,1)S(1)} %collective-permute-done.refs_6_), channel_id=1, source_target_pairs={{0,8},{1,17},{8,0},{9,25},{16,24},{17,1},{24,16},{25,9},{2,10},{3,... | collective-permute-start | bytes 688136 | tf_op jit(solution)/shard_map/ppermute | solution.py:442
  49.3 10.9 %collective-permute-start.12 = (bf16[224,512]{1,0:T(8,128)(2,1)}, bf16[224,512]{1,0:T(8,128)(2,1)}, u32[]{:S(2)}, u32[]{:S(2)}) collective-permute-start(bf16[224,512]{1,0:T(8,128)(2,1)} %collective-permute-done.1.refs_8_), channel_id=1, source_target_pairs={{0,16},{1,9},{8,24},{9,1},{16,0},{17,25},{24,8},{25,17},{2,18},{3,... | collective-permute-start | bytes 688136 | tf_op jit(solution)/shard_map/ppermute | solution.py:442
  50.8 9.9 %collective-permute-start.6 = (bf16[224,512]{1,0:T(8,128)(2,1)S(1)}, bf16[224,512]{1,0:T(8,128)(2,1)}, u32[]{:S(2)}, u32[]{:S(2)}) collective-permute-start(bf16[224,512]{1,0:T(8,128)(2,1)S(1)} %collective-permute-done.refs_6_), channel_id=1, source_target_pairs={{0,16},{1,9},{8,24},{9,1},{16,0},{17,25},{24,8},{25,17},{2,18},{3,... | collective-permute-start | bytes 688136 | tf_op jit(solution)/shard_map/ppermute | solution.py:442
  51.3 11.4 %collective-permute-start.8 = (bf16[224,512]{1,0:T(8,128)(2,1)}, bf16[224,512]{1,0:T(8,128)(2,1)}, u32[]{:S(2)}, u32[]{:S(2)}) collective-permute-start(bf16[224,512]{1,0:T(8,128)(2,1)} %collective-permute-done.1.refs_8_), channel_id=1, source_target_pairs={{0,2},{2,0},{4,6},{6,4},{1,3},{3,1},{5,7},{7,5},{8,10},{10,8},{12,... | collective-permute-start | bytes 688136 | tf_op jit(solution)/shard_map/ppermute | solution.py:428
  55.3 8.9 %collective-permute-start.14 = (bf16[224,512]{1,0:T(8,128)(2,1)}, bf16[224,512]{1,0:T(8,128)(2,1)}, u32[]{:S(2)}, u32[]{:S(2)}) collective-permute-start(bf16[224,512]{1,0:T(8,128)(2,1)} %collective-permute-done.13.refs_9_), channel_id=1, source_target_pairs={{0,16},{1,9},{8,24},{9,1},{16,0},{17,25},{24,8},{25,17},{2,18},{3,... | collective-permute-start | bytes 688136 | tf_op jit(solution)/shard_map/ppermute | solution.py:442
  60.2 11.9 %collective-permute-start.3 = (bf16[128,2048]{1,0:T(8,128)(2,1)}, bf16[128,2048]{1,0:T(8,128)(2,1)}, u32[]{:S(2)}, u32[]{:S(2)}) collective-permute-start(bf16[128,2048]{1,0:T(8,128)(2,1)} %bitcast.45), channel_id=1, source_target_pairs={{0,1},{1,0},{2,3},{3,2},{4,5},{5,4},{6,7},{7,6},{8,9},{9,8},{10,11... | collective-permute-start | bytes 1572872 | tf_op jit(solution)/shard_map/ppermute | solution.py:424
  60.2 11.9 %collective-permute-start.4 = (bf16[128,2048]{1,0:T(8,128)(2,1)}, bf16[128,2048]{1,0:T(8,128)(2,1)}, u32[]{:S(2)}, u32[]{:S(2)}) collective-permute-start(bf16[128,2048]{1,0:T(8,128)(2,1)} %bitcast.48), channel_id=1, source_target_pairs={{0,1},{1,0},{2,3},{3,2},{4,5},{5,4},{6,7},{7,6},{8,9},{9,8},{10,11... | collective-permute-start | bytes 1572872 | tf_op jit(solution)/shard_map/ppermute | solution.py:424
  60.7 8.2 %collective-permute-start.7 = (bf16[224,512]{1,0:T(8,128)(2,1)}, bf16[224,512]{1,0:T(8,128)(2,1)}, u32[]{:S(2)}, u32[]{:S(2)}) collective-permute-start(bf16[224,512]{1,0:T(8,128)(2,1)} %collective-permute-done.5.refs_7_), channel_id=1, source_target_pairs={{0,16},{1,9},{8,24},{9,1},{16,0},{17,25},{24,8},{25,17},{2,18},{3,... | collective-permute-start | bytes 688136 | tf_op jit(solution)/shard_map/ppermute | solution.py:442
  62.7 7.8 %collective-permute-start.9 = (bf16[224,512]{1,0:T(8,128)(2,1)}, bf16[224,512]{1,0:T(8,128)(2,1)}, u32[]{:S(2)}, u32[]{:S(2)}) collective-permute-start(bf16[224,512]{1,0:T(8,128)(2,1)} %collective-permute-done.8.refs_10_), channel_id=1, source_target_pairs={{0,8},{1,17},{8,0},{9,25},{16,24},{17,1},{24,16},{25,9},{2,10},{3,... | collective-permute-start | bytes 688136 | tf_op jit(solution)/shard_map/ppermute | solution.py:442
  64.2 7.9 %collective-permute-start.2 = (bf16[8,2,16,896]{3,2,1,0:T(8,128)(2,1)}, bf16[8,2,16,896]{3,2,1,0:T(8,128)(2,1)S(1)}, u32[]{:S(2)}, u32[]{:S(2)}) collective-permute-start(bf16[8,2,16,896]{3,2,1,0:T(8,128)(2,1)} %all-to-all-done.1.refs_0_), channel_id=1, source_target_pairs={{0,1},{1,0},{2,3},{3,2},{4,5},{5,4},{6,7},{7,6},{8,9},{9,8},{10,11... | collective-permute-start | bytes 1376264 | tf_op jit(solution)/shard_map/ppermute | solution.py:424
  68.9 14.3 %collective-permute-start.10 = (bf16[224,512]{1,0:T(8,128)(2,1)}, bf16[224,512]{1,0:T(8,128)(2,1)S(1)}, u32[]{:S(2)}, u32[]{:S(2)}) collective-permute-start(bf16[224,512]{1,0:T(8,128)(2,1)} %collective-permute-done.8.refs_10_), channel_id=1, source_target_pairs={{0,16},{1,9},{8,24},{9,1},{16,0},{17,25},{24,8},{25,17},{2,18},{3,... | collective-permute-start | bytes 688136 | tf_op jit(solution)/shard_map/ppermute | solution.py:442
  70.4 12.7 %collective-permute-start.11 = (bf16[224,512]{1,0:T(8,128)(2,1)}, bf16[224,512]{1,0:T(8,128)(2,1)S(1)}, u32[]{:S(2)}, u32[]{:S(2)}) collective-permute-start(bf16[224,512]{1,0:T(8,128)(2,1)} %collective-permute-done.9.refs_11_), channel_id=1, source_target_pairs={{0,16},{1,9},{8,24},{9,1},{16,0},{17,25},{24,8},{25,17},{2,18},{3,... | collective-permute-start | bytes 688136 | tf_op jit(solution)/shard_map/ppermute | solution.py:442
  81.6 19.5 %collective-permute-start.18 = (bf16[2,2,224,512]{3,2,1,0:T(8,128)(2,1)}, bf16[2,2,224,512]{3,2,1,0:T(8,128)(2,1)}, u32[]{:S(2)}, u32[]{:S(2)}) collective-permute-start(bf16[2,2,224,512]{3,2,1,0:T(8,128)(2,1)} %get-tuple-element.54), channel_id=1, source_target_pairs={{0,16},{1,9},{8,24},{9,1},{16,0},{17,25},{24,8},{25,17},{2,18},{3,... | collective-permute-start | bytes 2752520 | tf_op jit(solution)/shard_map/ppermute | solution.py:442
  92.6 14.0 %collective-permute-start.20 = (bf16[2,2,224,512]{3,2,1,0:T(8,128)(2,1)}, bf16[2,2,224,512]{3,2,1,0:T(8,128)(2,1)}, u32[]{:S(2)}, u32[]{:S(2)}) collective-permute-start(bf16[2,2,224,512]{3,2,1,0:T(8,128)(2,1)} %get-tuple-element.58), channel_id=1, source_target_pairs={{0,16},{1,9},{8,24},{9,1},{16,0},{17,25},{24,8},{25,17},{2,18},{3,... | collective-permute-start | bytes 2752520 | tf_op jit(solution)/shard_map/ppermute | solution.py:442
  93.2 1.8 %collective-permute-start.17 = (bf16[8,2,16,896]{3,2,1,0:T(8,128)(2,1)S(1)}, bf16[8,2,16,896]{3,2,1,0:T(8,128)(2,1)S(1)}, u32[]{:S(2)}, u32[]{:S(2)}) collective-permute-start(bf16[8,2,16,896]{3,2,1,0:T(8,128)(2,1)S(1)} %get-tuple-element.50), channel_id=1, source_target_pairs={{0,1},{1,0},{2,3},{3,2},{4,5},{5,4},{6,7},{7,6},{8,9},{9,8},{10,11... | collective-permute-start | bytes 1376264 | tf_op jit(solution)/shard_map/ppermute | solution.py:424
  95.8 27.1 %all-to-all-start.2 = ((bf16[8,2,16,896]{3,2,1,0:T(8,128)(2,1)}), bf16[8,2,16,896]{3,2,1,0:T(8,128)(2,1)}, u32[]{:S(2)}, u32[]{:S(2)}) async-start(bf16[8,2,16,896]{3,2,1,0:T(8,128)(2,1)} %bitcast.37), calls=%async_computation.2 | async-start | bytes 917504 | tf_op jit(solution)/shard_map/all_to_all | solution.py:536
  102.8 8.5 %collective-permute-start.19 = (bf16[2,224,512]{2,1,0:T(8,128)(2,1)S(1)}, bf16[2,224,512]{2,1,0:T(8,128)(2,1)S(1)}, u32[]{:S(2)}, u32[]{:S(2)}) collective-permute-start(bf16[2,224,512]{2,1,0:T(8,128)(2,1)S(1)} %get-tuple-element.56), channel_id=1, source_target_pairs={{0,8},{1,17},{8,0},{9,25},{16,24},{17,1},{24,16},{25,9},{2,10},{3,... | collective-permute-start | bytes 1376264 | tf_op jit(solution)/shard_map/ppermute | solution.py:442
  108.2 8.7 %collective-permute-start.22 = (bf16[2,224,512]{2,1,0:T(8,128)(2,1)S(1)}, bf16[2,224,512]{2,1,0:T(8,128)(2,1)S(1)}, u32[]{:S(2)}, u32[]{:S(2)}) collective-permute-start(bf16[2,224,512]{2,1,0:T(8,128)(2,1)S(1)} %get-tuple-element.62), channel_id=1, source_target_pairs={{0,8},{1,17},{8,0},{9,25},{16,24},{17,1},{24,16},{25,9},{2,10},{3,... | collective-permute-start | bytes 1376264 | tf_op jit(solution)/shard_map/ppermute | solution.py:442
  112.1 16.0 %collective-permute-start.21 = (bf16[1,224,512]{2,1,0:T(8,128)(2,1)}, bf16[1,224,512]{2,1,0:T(8,128)(2,1)}, u32[]{:S(2)}, u32[]{:S(2)}) collective-permute-start(bf16[1,224,512]{2,1,0:T(8,128)(2,1)} %get-tuple-element.60), channel_id=1, source_target_pairs={{0,4},{2,6},{4,0},{6,2},{1,5},{3,7},{5,1},{7,3},{8,12},{10,14},{12... | collective-permute-start | bytes 688136 | tf_op jit(solution)/shard_map/ppermute | solution.py:428
  115.1 37.8 %collective-permute-start.15 = (bf16[128,2048]{1,0:T(8,128)(2,1)}, bf16[128,2048]{1,0:T(8,128)(2,1)}, u32[]{:S(2)}, u32[]{:S(2)}) collective-permute-start(bf16[128,2048]{1,0:T(8,128)(2,1)} %get-tuple-element.46), channel_id=1, source_target_pairs={{0,1},{1,0},{2,3},{3,2},{4,5},{5,4},{6,7},{7,6},{8,9},{9,8},{10,11... | collective-permute-start | bytes 1572872 | tf_op jit(solution)/shard_map/ppermute | solution.py:424
  115.1 37.8 %collective-permute-start.16 = (bf16[128,2048]{1,0:T(8,128)(2,1)}, bf16[128,2048]{1,0:T(8,128)(2,1)}, u32[]{:S(2)}, u32[]{:S(2)}) collective-permute-start(bf16[128,2048]{1,0:T(8,128)(2,1)} %get-tuple-element.48), channel_id=1, source_target_pairs={{0,1},{1,0},{2,3},{3,2},{4,5},{5,4},{6,7},{7,6},{8,9},{9,8},{10,11... | collective-permute-start | bytes 1572872 | tf_op jit(solution)/shard_map/ppermute | solution.py:424
  117.8 21.3 %collective-permute-start.23 = (bf16[1,224,512]{2,1,0:T(8,128)(2,1)}, bf16[1,224,512]{2,1,0:T(8,128)(2,1)}, u32[]{:S(2)}, u32[]{:S(2)}) collective-permute-start(bf16[1,224,512]{2,1,0:T(8,128)(2,1)} %get-tuple-element.63), channel_id=1, source_target_pairs={{0,2},{2,0},{4,6},{6,4},{1,3},{3,1},{5,7},{7,5},{8,10},{10,8},{12,... | collective-permute-start | bytes 688136 | tf_op jit(solution)/shard_map/ppermute | solution.py:428
  120.5 18.7 %collective-permute-start.24 = (bf16[1,224,512]{2,1,0:T(8,128)(2,1)}, bf16[1,224,512]{2,1,0:T(8,128)(2,1)}, u32[]{:S(2)}, u32[]{:S(2)}) collective-permute-start(bf16[1,224,512]{2,1,0:T(8,128)(2,1)} %get-tuple-element.64), channel_id=1, source_target_pairs={{0,6},{2,4},{4,2},{6,0},{1,7},{3,5},{5,3},{7,1},{8,14},{10,12},{12... | collective-permute-start | bytes 688136 | tf_op jit(solution)/shard_map/ppermute | solution.py:428
  134.6 28.3 %all-to-all-start.3 = ((bf16[8,4,16,896]{3,2,1,0:T(8,128)(2,1)}), bf16[8,4,16,896]{3,2,1,0:T(8,128)(2,1)S(1)}, u32[]{:S(2)}, u32[]{:S(2)}) async-start(bf16[8,4,16,896]{3,2,1,0:T(8,128)(2,1)} %bitcast.36), calls=%async_computation.3 | async-start | bytes 1835008 | tf_op jit(solution)/shard_map/all_to_all | solution.py:577
  140.4 6.1 %collective-permute-start.25 = (bf16[224,512]{1,0:T(8,128)(2,1)S(1)}, bf16[224,512]{1,0:T(8,128)(2,1)S(1)}, u32[]{:S(2)}, u32[]{:S(2)}) collective-permute-start(bf16[224,512]{1,0:T(8,128)(2,1)S(1)} %bitcast.31), channel_id=1, source_target_pairs={{0,8},{1,17},{8,0},{9,25},{16,24},{17,1},{24,16},{25,9},{2,10},{3,... | collective-permute-start | bytes 688136 | tf_op jit(solution)/shard_map/ppermute | solution.py:442
  141.8 13.3 %collective-permute-start.26 = (bf16[224,512]{1,0:T(8,128)(2,1)S(1)}, bf16[224,512]{1,0:T(8,128)(2,1)S(1)}, u32[]{:S(2)}, u32[]{:S(2)}) collective-permute-start(bf16[224,512]{1,0:T(8,128)(2,1)S(1)} %bitcast.32), channel_id=1, source_target_pairs={{0,16},{1,9},{8,24},{9,1},{16,0},{17,25},{24,8},{25,17},{2,18},{3,... | collective-permute-start | bytes 688136 | tf_op jit(solution)/shard_map/ppermute | solution.py:442
  146.5 10.3 %collective-permute-start.27 = (bf16[224,512]{1,0:T(8,128)(2,1)S(1)}, bf16[224,512]{1,0:T(8,128)(2,1)S(1)}, u32[]{:S(2)}, u32[]{:S(2)}) collective-permute-start(bf16[224,512]{1,0:T(8,128)(2,1)S(1)} %collective-permute-done.25.refs_1_), channel_id=1, source_target_pairs={{0,16},{1,9},{8,24},{9,1},{16,0},{17,25},{24,8},{25,17},{2,18},{3,... | collective-permute-start | bytes 688136 | tf_op jit(solution)/shard_map/ppermute | solution.py:442
  (8 other events, 182.7 us)

commit v4 on v3

--- a/solution.py
+++ b/solution.py
@@ -66,14 +66,12 @@
 
     before = dot(normed[...], up_ref[...])
     square = before * before
-    bend = jnp.tanh(GELU_RATE * before * (1.0 + GELU_CUBE * square))
-    half = 0.5 * (1.0 + bend)
-    activity = (before * half).astype(jnp.bfloat16)
-    slope = half + 0.5 * before * (1.0 - bend * bend) * (
-        GELU_RATE * (1.0 + 3.0 * GELU_CUBE * square)
-    )
+    bend = jnp.tanh(before * (GELU_RATE + GELU_RATE * GELU_CUBE * square))
+    half = 0.5 + 0.5 * bend
+    activity = before * half
+    slope = half + activity * (1.0 - bend) * (GELU_RATE + 3.0 * GELU_RATE * GELU_CUBE * square)
     slope_ref[...] = slope.astype(slope_ref.dtype)
-    total[...] += dot(activity, down_ref[...])
+    total[...] += dot(activity.astype(jnp.bfloat16), down_ref[...])
 
     @pl.when(step == pl.num_programs(0) - 1)
     def _():
@@ -196,10 +194,12 @@
     if last:
         (back_in,) = take(1)
         take(4)
+    else:
+        take(1)
     out_refs = (take(2), take(2))
     back_refs = take(2 if last else 1)
     grad_halves = take(2)
-    rows, turned, rows_t, back, weight = refs
+    rows, rows_t, back, weight = refs
     step = pl.program_id(0)
     shares, mine, piece, width = own_enc.shape
     span = shares * piece
@@ -211,10 +211,7 @@
         for s in range(2 * mine):
             source = own_enc if s < mine else other_enc
             rows[s * span : (s + 1) * span, :] = merge_rows(source[:, s % mine])
-        turned[...] = rows[...].T
-        for i in range(lines):
-            start = pl.multiple_of(plan[steps + i] * part_rows, 16)
-            rows_t[i * part_rows : (i + 1) * part_rows, :] = turned[pl.ds(start, part_rows), :]
+        rows_t[...] = rows[...].T
         back[...] = back_in[...].astype(jnp.float32) if last else jnp.zeros_like(back)
 
     for shard, (kind, found) in enumerate(zip(kinds, weight_refs)):
@@ -272,11 +269,10 @@
         ],
         axis=0,
     )
-    part_grads = dot(rows_t[...], both_grad).astype(jnp.bfloat16)
     for i in range(lines):
-        grad_halves[2 * i // lines][i % (lines // 2), 0] = part_grads[
-            i * part_rows : (i + 1) * part_rows
-        ]
+        start = pl.multiple_of(plan[steps + i] * part_rows, 16)
+        part_grad = dot(rows_t[pl.ds(start, part_rows), :], both_grad).astype(jnp.bfloat16)
+        grad_halves[2 * i // lines][i % (lines // 2), 0] = part_grad
     back[...] += dot_nt(both_grad, weight[...])
 
     @pl.when(step == steps - 1)
@@ -289,7 +285,7 @@
                 back_refs[s // mine][:, s % mine] = block.astype(jnp.bfloat16)
 
 
-def attend(plan, lines, own_enc, other_enc, token_arrays, shards, earlier=None):
+def attend(plan, lines, own_enc, other_enc, token_arrays, shards, earlier=None, token=None):
     last = earlier is not None
     steps = len(shards)
     kinds, arrays = [kind for kind, _ in shards], sum([found for _, found in shards], [])
@@ -305,6 +301,9 @@
     out = functools.partial(jax.ShapeDtypeStruct, dtype=jnp.bfloat16)
     operands = [plan, own_enc, other_enc, *map(in_hbm, token_arrays), *arrays]
     in_specs = [enc_spec] * 2 + [token_spec] * 4 + [whole(*value.shape) for value in arrays]
+    if token is not None:
+        operands.append(token)
+        in_specs.append(pl.BlockSpec(memory_space=pl.ANY))
     back_shapes, aliases = [out((all_rows, width))], {}
     if last:
         aliases = {len(operands) + 1 + i: i for i in range(4)}
@@ -323,7 +322,6 @@
             scratch_shapes=[
                 pltpu.VMEM((all_rows, width), jnp.bfloat16),
                 pltpu.VMEM((width, all_rows), jnp.bfloat16),
-                pltpu.VMEM((width, all_rows), jnp.bfloat16),
                 pltpu.VMEM((all_rows, width), jnp.float32),
                 pltpu.VMEM((width, 2 * columns), jnp.bfloat16),
             ],
@@ -375,22 +373,62 @@
     )(*terms, *after)
 
 
-def copy_kernel(plan, *refs):
-    out = refs[-1]
-    for i in range(plan.shape[0]):
-        out[i] = plan[i]
-
-
-def copy_plan(plan, others):
-    scalars = pl.BlockSpec(memory_space=pltpu.SMEM)
+def token_kernel(*refs):
+    refs[-1][...] = jnp.zeros_like(refs[-1])
+
+
+def token_after(others):
     return pl.pallas_call(
-        copy_kernel,
-        in_specs=[scalars] + [pl.BlockSpec(memory_space=pl.ANY)] * len(others),
-        out_specs=scalars,
-        out_shape=jax.ShapeDtypeStruct(plan.shape, plan.dtype),
+        token_kernel,
+        in_specs=[pl.BlockSpec(memory_space=pl.ANY)] * len(others),
+        out_specs=pl.BlockSpec(memory_space=pltpu.VMEM),
+        out_shape=jax.ShapeDtypeStruct((8, 128), jnp.float32),
         compiler_params=pltpu.CompilerParams(vmem_limit_bytes=SMALL_VMEM_BYTES),
         cost_estimate=stated(4),
-    )(plan, *others)
+    )(*others)
+
+
+def share_kernel(pool, out, held, read, wrote):
+    holding, groups = pool.shape[:2]
+    half = groups // 2
+    ranges = [pl.ds(part * half, half) for part in range(2)]
+    reads = [
+        [
+            pltpu.make_async_copy(pool.at[slot, shares], held.at[shares, slot], read.at[part, slot])
+            for slot in range(holding)
+        ]
+        for part, shares in enumerate(ranges)
+    ]
+    writes = [
+        pltpu.make_async_copy(held.at[shares], out.at[shares], wrote.at[part])
+        for part, shares in enumerate(ranges)
+    ]
+    for copy in reads[0] + reads[1]:
+        copy.start()
+    for part in range(2):
+        for copy in reads[part]:
+            copy.wait()
+        writes[part].start()
+    for copy in writes:
+        copy.wait()
+
+
+def share_rows(pool):
+    holding, groups, piece, width = pool.shape
+    shape = (groups, holding, piece, width)
+    return pl.pallas_call(
+        share_kernel,
+        in_specs=[pl.BlockSpec(memory_space=pl.ANY)],
+        out_specs=pl.BlockSpec(memory_space=pl.ANY),
+        out_shape=pltpu.HBM(shape, pool.dtype),
+        scratch_shapes=[
+            pltpu.VMEM(shape, pool.dtype),
+            pltpu.SemaphoreType.DMA((2, holding)),
+            pltpu.SemaphoreType.DMA((2,)),
+        ],
+        compiler_params=pltpu.CompilerParams(vmem_limit_bytes=SMALL_VMEM_BYTES),
+        cost_estimate=pl.CostEstimate(flops=0, bytes_accessed=4 * pool.size, transcendentals=0),
+    )(in_hbm(pool))
 
 
 def join_kernel(plan, *refs):
@@ -497,7 +535,7 @@
         shift //= 2
     part[1] = swap_chips(part[0], 1)
 
-    pieces = neighbour_pool[0].reshape(holding, groups, piece, width).transpose(1, 0, 2, 3)
+    pieces = share_rows(neighbour_pool[0].reshape(holding, groups, piece, width))
     received = lax.all_to_all(pieces, SEQ, split_axis=0, concat_axis=0, tiled=True)
     received = received.reshape(groups * holding, piece, width)
 
@@ -521,9 +559,9 @@
         for shifts in steps
     ]
     early = [value for shift in (1, *even) for value in shards[shift][1][lines // 2 :]]
-    plans[0] = copy_plan(plans[0], early)
+    token = token_after(early)
     parted = [[shards[shift] for shift in shifts] for shifts in steps]
-    first = attend(plans[0], lines, own_enc, other_enc, token_arrays, parted[0])
+    first = attend(plans[0], lines, own_enc, other_enc, token_arrays, parted[0], token=token)
     last = attend(plans[1], lines, own_enc, other_enc, token_arrays, parted[1], first[:5])
     outs, own_back, other_back = last[:4], last[4], last[5]
 

time: 166 us -> 165 us (level)
  local copies, waits for them, and re-layouts: 4.34 us -> 2 us
    another operation x1 -> x0, local copies, waits for them, and re-layouts: 2.34 us -> none  [on_device(): neighbour_pool[0].reshape(holding, groups, piece, width)]
  transfers between devices with their start and end apart: 32 -> 32, of which waited for: 13 -> 14; matrix products, arithmetic and copies ran while one was open for 2% -> 2% of each run, Pallas kernels for 26% -> 25%
where the time goes in v4:
time: 165 us; the launch traced here: 163 us
  starting transfers between devices  64.4 us (39%)
  waiting for transfers between devices  49.3 us (30%)
  Pallas kernels  43.1 us (26%)
  other arithmetic  3.07 us (2%)
  local copies, waits for them, and re-layouts  2 us (1%)
    ppermute x16, starting transfers between devices, swap_lines(): return lax.ppermute(value, ('line', 'core'), pairs)  28.8 us
    pallas_call x2, Pallas kernels, attend(): pl.pallas_call(functools.partial(attend_kernel, kinds, lines, last), grid...  18.8 us
    all_to_all x1, waiting for transfers between devices, on_device(): lax.all_to_all(pieces, SEQ, split_axis=0, concat_axis=0, tiled=True)  18.3 us
    ppermute x16, waiting for transfers between devices, swap_lines(): return lax.ppermute(value, ('line', 'core'), pairs)  16.5 us
    ppermute x6, starting transfers between devices, swap_chips(): lax.ppermute(value, 'z', [(z, z ^ shift) for z in range(lax.axis_size('z'...  14.2 us
    ppermute x6, waiting for transfers between devices, swap_chips(): lax.ppermute(value, 'z', [(z, z ^ shift) for z in range(lax.axis_size('z'...  8.44 us
    pallas_call x6, Pallas kernels, sum_blocks(): pl.pallas_call(functools.partial(sum_kernel, len(terms), sizes), grid=(ti...  7.05 us
    pallas_call x1, Pallas kernels, encode_rows(): pl.pallas_call(encode_kernel, grid_spec=pltpu.PrefetchScalarGridSpec(num_...  6.63 us
  transfers between devices with their start and end apart: 32, of which 14 were waited for; matrix products, arithmetic and copies ran while one was open for 2% of the time, Pallas kernels for 25%

profile of v4, /device:TPU:0, one launch (start us, length us, event | category | flops | bytes accessed | tf_op | source)
XLA Modules:
  0.0 162.7 jit_solution(13434232714241497774)
XLA Ops:
  0.7 2.2 %shard_map.146 = bf16[8,4,16,896]{3,2,1,0:T(8,128)(2,1)} custom-call(bf16[4,8,16,896]{3,2,1,0:T(8,128)(2,1)} %bitcast.36), custom_call_target="tpu_custom_call" | custom-call | bytes 1835008 | tf_op jit(solution)/shard_map/pallas_call | solution.py:419
  2.9 6.3 %all-to-all-start = ((bf16[8,4,16,896]{3,2,1,0:T(8,128)(2,1)}), bf16[8,4,16,896]{3,2,1,0:T(8,128)(2,1)}, u32[]{:S(2)}, u32[]{:S(2)}) async-start(bf16[8,4,16,896]{3,2,1,0:T(8,128)(2,1)} %shard_map.146), calls=%async_computation | async-start | bytes 1835008 | tf_op jit(solution)/shard_map/all_to_all | solution.py:539
  10.9 2.0 %collective-permute-start = (bf16[224,512]{1,0:T(8,128)(2,1)}, bf16[224,512]{1,0:T(8,128)(2,1)S(1)}, u32[]{:S(2)}, u32[]{:S(2)}) collective-permute-start(bf16[224,512]{1,0:T(8,128)(2,1)} %pad_maximum_fusion), channel_id=1, source_target_pairs={{0,2},{2,0},{4,6},{6,4},{1,3},{3,1},{5,7},{7,5},{8,10},{10,8},{12,... | collective-permute-start | bytes 688136 | tf_op jit(solution)/shard_map/ppermute | solution.py:466
  13.0 2.4 %collective-permute-start.1 = (bf16[224,512]{1,0:T(8,128)(2,1)}, bf16[224,512]{1,0:T(8,128)(2,1)}, u32[]{:S(2)}, u32[]{:S(2)}) collective-permute-start(bf16[224,512]{1,0:T(8,128)(2,1)} %pad_maximum_fusion), channel_id=1, source_target_pairs={{0,4},{2,6},{4,0},{6,2},{1,5},{3,7},{5,1},{7,3},{8,12},{10,14},{12... | collective-permute-start | bytes 688136 | tf_op jit(solution)/shard_map/ppermute | solution.py:466
  15.3 18.3 %all-to-all-done = bf16[8,4,16,896]{3,2,1,0:T(8,128)(2,1)} async-done(((bf16[8,4,16,896]{3,2,1,0:T(8,128)(2,1)}), bf16[8,4,16,896]{3,2,1,0:T(8,128)(2,1)}, u32[]{:S(2)}, u32[]{:S(2)}) %all-to-all-start) | async-done | bytes 917536 | tf_op jit(solution)/shard_map/all_to_all | solution.py:539
  33.6 6.6 %shard_map.147 = (bf16[16,16,896]{2,1,0:T(8,128)(2,1)}, bf16[16,16,896]{2,1,0:T(8,128)(2,1)}, bf16[256,1792]{1,0:T(8,128)(2,1)}) custom-call(s32[16]{0:T(128)S(1)} %bitcast.31, bf16[32,16,896]{2,1,0:T(8,128)(2,1)} %bitcast.4.rows_ref, f32[1,896]{1,0:T(1,128)S(1)} %reshape.106.gain_ref, bf16[896,1792]{1,0:T(8,128)(2,1)S(1)} %copy-done, bf16[1792,896]{1,0:T(8,128)(2,1)} %down_ref.3), custom_call_target="tpu_custom_call" | custom-call | flops 1644167168 | bytes 9175040 | tf_op jit(solution)/shard_map/pallas_call | solution.py:87
  40.3 2.7 %collective-permute-done.1.refs_8_ = bf16[224,512]{1,0:T(8,128)(2,1)} collective-permute-done((bf16[224,512]{1,0:T(8,128)(2,1)}, bf16[224,512]{1,0:T(8,128)(2,1)}, u32[]{:S(2)}, u32[]{:S(2)}) %collective-permute-start.1) | collective-permute-done | bytes 229408 | tf_op jit(solution)/shard_map/ppermute | solution.py:466
  43.0 4.1 %all-to-all-start.1 = ((bf16[8,2,16,896]{3,2,1,0:T(8,128)(2,1)}), bf16[8,2,16,896]{3,2,1,0:T(8,128)(2,1)}, u32[]{:S(2)}, u32[]{:S(2)}) async-start(bf16[8,2,16,896]{3,2,1,0:T(8,128)(2,1)} %bitcast.40), calls=%async_computation.1 | async-start | bytes 917504 | tf_op jit(solution)/shard_map/all_to_all | solution.py:548
  51.2 1.8 %collective-permute-start.8 = (bf16[224,512]{1,0:T(8,128)(2,1)}, bf16[224,512]{1,0:T(8,128)(2,1)}, u32[]{:S(2)}, u32[]{:S(2)}) collective-permute-start(bf16[224,512]{1,0:T(8,128)(2,1)} %collective-permute-done.1.refs_8_), channel_id=1, source_target_pairs={{0,2},{2,0},{4,6},{6,4},{1,3},{3,1},{5,7},{7,5},{8,10},{10,8},{12,... | collective-permute-start | bytes 688136 | tf_op jit(solution)/shard_map/ppermute | solution.py:466
  53.1 2.1 %collective-permute-done.12.refs_9_ = bf16[224,512]{1,0:T(8,128)(2,1)} collective-permute-done((bf16[224,512]{1,0:T(8,128)(2,1)}, bf16[224,512]{1,0:T(8,128)(2,1)}, u32[]{:S(2)}, u32[]{:S(2)}) %collective-permute-start.12) | collective-permute-done | bytes 229408 | tf_op jit(solution)/shard_map/ppermute | solution.py:480
  56.7 3.4 %collective-permute-done.5.refs_7_ = bf16[224,512]{1,0:T(8,128)(2,1)} collective-permute-done((bf16[224,512]{1,0:T(8,128)(2,1)S(1)}, bf16[224,512]{1,0:T(8,128)(2,1)}, u32[]{:S(2)}, u32[]{:S(2)}) %collective-permute-start.5) | collective-permute-done | bytes 229408 | tf_op jit(solution)/shard_map/ppermute | solution.py:480
  64.3 4.5 %collective-permute-done.7.refs_1_.refs_9_ = bf16[224,512]{1,0:T(8,128)(2,1)} collective-permute-done((bf16[224,512]{1,0:T(8,128)(2,1)}, bf16[224,512]{1,0:T(8,128)(2,1)}, u32[]{:S(2)}, u32[]{:S(2)}) %collective-permute-start.7) | collective-permute-done | bytes 229408 | tf_op jit(solution)/shard_map/ppermute | solution.py:480
  70.9 9.5 %shard_map.149 = (bf16[128,2048]{1,0:T(8,128)(2,1)}, bf16[128,2048]{1,0:T(8,128)(2,1)}, bf16[128,2048]{1,0:T(8,128)(2,1)}, bf16[128,2048]{1,0:T(8,128)(2,1)}, bf...) custom-call(s32[6]{0:T(128)S(1)} %get-tuple-element.69.plan, ...), custom_call_target="tpu_custom_call" | custom-call | flops 2818572288 | bytes 6553600 | tf_op jit(solution)/shard_map/pallas_call | solution.py:313
  82.0 9.3 %shard_map.150 = (bf16[128,2048]{1,0:T(8,128)(2,1)}, bf16[128,2048]{1,0:T(8,128)(2,1)}, bf16[128,2048]{1,0:T(8,128)(2,1)}, bf16[128,2048]{1,0:T(8,128)(2,1)}, bf...) custom-call(s32[6]{0:T(128)S(1)} %get-tuple-element.70.plan, ...), custom_call_target="tpu_custom_call", output_to_operand_aliasing={{0}: (16, {}), {1}: (17, {}), {2}: (18, {}), {3}: (19, {})} | custom-call | flops 2818572288 | bytes 6553600 | tf_op jit(solution)/shard_map/pallas_call | solution.py:313
  91.9 1.8 %collective-permute-done.17 = bf16[8,2,16,896]{3,2,1,0:T(8,128)(2,1)S(1)} collective-permute-done((bf16[8,2,16,896]{3,2,1,0:T(8,128)(2,1)S(1)}, bf16[8,2,16,896]{3,2,1,0:T(8,128)(2,1)S(1)}, u32[]{:S(2)}, u32[]{:S(2)}) %collective-permute-start.17) | collective-permute-done | bytes 458784 | tf_op jit(solution)/shard_map/ppermute | solution.py:462
  94.5 5.3 %all-to-all-start.2 = ((bf16[8,2,16,896]{3,2,1,0:T(8,128)(2,1)}), bf16[8,2,16,896]{3,2,1,0:T(8,128)(2,1)}, u32[]{:S(2)}, u32[]{:S(2)}) async-start(bf16[8,2,16,896]{3,2,1,0:T(8,128)(2,1)} %bitcast.34), calls=%async_computation.2 | async-start | bytes 917504 | tf_op jit(solution)/shard_map/all_to_all | solution.py:574
  99.9 1.6 shard_map.152
  102.9 2.4 %collective-permute-done.20 = bf16[2,2,224,512]{3,2,1,0:T(8,128)(2,1)} collective-permute-done((bf16[2,2,224,512]{3,2,1,0:T(8,128)(2,1)}, bf16[2,2,224,512]{3,2,1,0:T(8,128)(2,1)}, u32[]{:S(2)}, u32[]{:S(2)}) %collective-permute-start.20) | collective-permute-done | bytes 917536 | tf_op jit(solution)/shard_map/ppermute | solution.py:480
  105.3 1.6 shard_map.153
  106.9 2.2 %collective-permute-start.22 = (bf16[2,224,512]{2,1,0:T(8,128)(2,1)S(1)}, bf16[2,224,512]{2,1,0:T(8,128)(2,1)S(1)}, u32[]{:S(2)}, u32[]{:S(2)}) collective-permute-start(bf16[2,224,512]{2,1,0:T(8,128)(2,1)S(1)} %get-tuple-element.62), channel_id=1, source_target_pairs={{0,8},{1,17},{8,0},{9,25},{16,24},{17,1},{24,16},{25,9},{2,10},{3,... | collective-permute-start | bytes 1376264 | tf_op jit(solution)/shard_map/ppermute | solution.py:480
  110.9 2.9 %collective-permute-start.21 = (bf16[1,224,512]{2,1,0:T(8,128)(2,1)}, bf16[1,224,512]{2,1,0:T(8,128)(2,1)}, u32[]{:S(2)}, u32[]{:S(2)}) collective-permute-start(bf16[1,224,512]{2,1,0:T(8,128)(2,1)} %get-tuple-element.60), channel_id=1, source_target_pairs={{0,4},{2,6},{4,0},{6,2},{1,5},{3,7},{5,1},{7,3},{8,12},{10,14},{12... | collective-permute-start | bytes 688136 | tf_op jit(solution)/shard_map/ppermute | solution.py:466
  116.6 2.7 %collective-permute-start.23 = (bf16[1,224,512]{2,1,0:T(8,128)(2,1)}, bf16[1,224,512]{2,1,0:T(8,128)(2,1)}, u32[]{:S(2)}, u32[]{:S(2)}) collective-permute-start(bf16[1,224,512]{2,1,0:T(8,128)(2,1)} %get-tuple-element.63), channel_id=1, source_target_pairs={{0,2},{2,0},{4,6},{6,4},{1,3},{3,1},{5,7},{7,5},{8,10},{10,8},{12,... | collective-permute-start | bytes 688136 | tf_op jit(solution)/shard_map/ppermute | solution.py:466
  119.2 2.4 %collective-permute-start.24 = (bf16[1,224,512]{2,1,0:T(8,128)(2,1)}, bf16[1,224,512]{2,1,0:T(8,128)(2,1)}, u32[]{:S(2)}, u32[]{:S(2)}) collective-permute-start(bf16[1,224,512]{2,1,0:T(8,128)(2,1)} %get-tuple-element.64), channel_id=1, source_target_pairs={{0,6},{2,4},{4,2},{6,0},{1,7},{3,5},{5,3},{7,1},{8,14},{10,12},{12... | collective-permute-start | bytes 688136 | tf_op jit(solution)/shard_map/ppermute | solution.py:466
  121.6 5.3 %collective-permute-done.21.refs_0_.refs_1_ = bf16[1,224,512]{2,1,0:T(8,128)(2,1)} collective-permute-done((bf16[1,224,512]{2,1,0:T(8,128)(2,1)}, bf16[1,224,512]{2,1,0:T(8,128)(2,1)}, u32[]{:S(2)}, u32[]{:S(2)}) %collective-permute-start.21) | collective-permute-done | bytes 229408 | tf_op jit(solution)/shard_map/ppermute | solution.py:466
  126.9 6.5 %shard_map.155.refs_4_ = bf16[32,16,896]{2,1,0:T(8,128)(2,1)} custom-call(s32[16]{0:T(128)S(1)} %bitcast.32, bf16[16,16,896]{2,1,0:T(8,128)(2,1)} %bitcast.15.grad_ref, bf16[16,16,896]{2,1,0:T(8,128)(2,1)} %get-tuple-element.51.used_ref, bf16[256,1792]{1,0:T(8,128)(2,1)} %get-tuple-element.52.slope_ref, f32[1,896]{1,0:T(1,128)S(1)} %reshape.106.gain_ref, ...), custom_call_target="tpu_custom_call" | custom-call | flops 1644167168 | bytes 9175040 | tf_op jit(solution)/shard_map/pallas_call | solution.py:160
  133.4 4.5 %all-to-all-start.3 = ((bf16[8,4,16,896]{3,2,1,0:T(8,128)(2,1)}), bf16[8,4,16,896]{3,2,1,0:T(8,128)(2,1)S(1)}, u32[]{:S(2)}, u32[]{:S(2)}) async-start(bf16[8,4,16,896]{3,2,1,0:T(8,128)(2,1)} %bitcast.33), calls=%async_computation.3 | async-start | bytes 1835008 | tf_op jit(solution)/shard_map/all_to_all | solution.py:615
  140.6 4.6 %collective-permute-start.26 = (bf16[224,512]{1,0:T(8,128)(2,1)S(1)}, bf16[224,512]{1,0:T(8,128)(2,1)S(1)}, u32[]{:S(2)}, u32[]{:S(2)}) collective-permute-start(bf16[224,512]{1,0:T(8,128)(2,1)S(1)} %bitcast.29), channel_id=1, source_target_pairs={{0,16},{1,9},{8,24},{9,1},{16,0},{17,25},{24,8},{25,17},{2,18},{3,... | collective-permute-start | bytes 688136 | tf_op jit(solution)/shard_map/ppermute | solution.py:480
  145.3 6.3 %collective-permute-start.27 = (bf16[224,512]{1,0:T(8,128)(2,1)S(1)}, bf16[224,512]{1,0:T(8,128)(2,1)S(1)}, u32[]{:S(2)}, u32[]{:S(2)}) collective-permute-start(bf16[224,512]{1,0:T(8,128)(2,1)S(1)} %collective-permute-done.25.refs_1_), channel_id=1, source_target_pairs={{0,16},{1,9},{8,24},{9,1},{16,0},{17,25},{24,8},{25,17},{2,18},{3,... | collective-permute-start | bytes 688136 | tf_op jit(solution)/shard_map/ppermute | solution.py:480
  151.6 2.3 %select_bitcast_fusion = (bf16[1,128,2048]{2,1,0:T(8,128)(2,1)}, bf16[1,128,2048]{2,1,0:T(8,128)(2,1)}) fusion(bf16[128,2048]{1,0:T(8,128)(2,1)S(1)} %copy-done.5, bf16[128,2048]{1,0:T(8,128)(2,1)} %collective-permute-done.16, pred[2048]{0:T(1024)(128)(4,1)S(1)} %fusion.1, bf16[128,2048]{1,0:T(8,128)(2,1)S(1)} %copy-done.4, ...), kind=kLoop, calls=%fused_computation | loop fusion | flops 524288 | bytes 3147776 | tf_op jit(solution)/shard_map/broadcast_in_dim | solution.py:621
  153.9 1.7 %collective-permute-done.27.refs_3_ = bf16[224,512]{1,0:T(8,128)(2,1)S(1)} collective-permute-done((bf16[224,512]{1,0:T(8,128)(2,1)S(1)}, bf16[224,512]{1,0:T(8,128)(2,1)S(1)}, u32[]{:S(2)}, u32[]{:S(2)}) %collective-permute-start.27) | collective-permute-done | bytes 229408 | tf_op jit(solution)/shard_map/ppermute | solution.py:480
  155.6 1.9 %shard_map.158 = (f32[896,256]{1,0:T(8,128)}, f32[896,256]{1,0:T(8,128)}) custom-call(s32[4]{0:T(128)S(1)} %fusion.5.plan, bf16[224,512]{1,0:T(8,128)(2,1)S(1)} %bitcast.30, bf16[224,512]{1,0:T(8,128)(2,1)S(1)} %collective-permute-done.25.refs_1_, bf16[224,512]{1,0:T(8,128)(2,1)S(1)} %collective-permute-done.26.refs_2_, ...), custom_call_target="tpu_custom_call" | custom-call | flops 8000000000 | bytes 24000000 | tf_op jit(solution)/shard_map/pallas_call | solution.py:447
  157.4 4.2 %all-to-all-done.3 = bf16[8,4,16,896]{3,2,1,0:T(8,128)(2,1)S(1)} async-done(((bf16[8,4,16,896]{3,2,1,0:T(8,128)(2,1)}), bf16[8,4,16,896]{3,2,1,0:T(8,128)(2,1)S(1)}, u32[]{:S(2)}, u32[]{:S(2)}) %all-to-all-start.3) | async-done | bytes 917536 | tf_op jit(solution)/shard_map/all_to_all | solution.py:615
  (69 shorter events, 26.1 us)
Async XLA Ops:
  2.9 30.7 %all-to-all-start = ((bf16[8,4,16,896]{3,2,1,0:T(8,128)(2,1)}), bf16[8,4,16,896]{3,2,1,0:T(8,128)(2,1)}, u32[]{:S(2)}, u32[]{:S(2)}) async-start(bf16[8,4,16,896]{3,2,1,0:T(8,128)(2,1)} %shard_map.146), calls=%async_computation | async-start | bytes 1835008 | tf_op jit(solution)/shard_map/all_to_all | solution.py:539
  10.9 29.3 %collective-permute-start = (bf16[224,512]{1,0:T(8,128)(2,1)}, bf16[224,512]{1,0:T(8,128)(2,1)S(1)}, u32[]{:S(2)}, u32[]{:S(2)}) collective-permute-start(bf16[224,512]{1,0:T(8,128)(2,1)} %pad_maximum_fusion), channel_id=1, source_target_pairs={{0,2},{2,0},{4,6},{6,4},{1,3},{3,1},{5,7},{7,5},{8,10},{10,8},{12,... | collective-permute-start | bytes 688136 | tf_op jit(solution)/shard_map/ppermute | solution.py:466
  13.0 30.0 %collective-permute-start.1 = (bf16[224,512]{1,0:T(8,128)(2,1)}, bf16[224,512]{1,0:T(8,128)(2,1)}, u32[]{:S(2)}, u32[]{:S(2)}) collective-permute-start(bf16[224,512]{1,0:T(8,128)(2,1)} %pad_maximum_fusion), channel_id=1, source_target_pairs={{0,4},{2,6},{4,0},{6,2},{1,5},{3,7},{5,1},{7,3},{8,12},{10,14},{12... | collective-permute-start | bytes 688136 | tf_op jit(solution)/shard_map/ppermute | solution.py:466
  43.0 21.2 %all-to-all-start.1 = ((bf16[8,2,16,896]{3,2,1,0:T(8,128)(2,1)}), bf16[8,2,16,896]{3,2,1,0:T(8,128)(2,1)}, u32[]{:S(2)}, u32[]{:S(2)}) async-start(bf16[8,2,16,896]{3,2,1,0:T(8,128)(2,1)} %bitcast.40), calls=%async_computation.1 | async-start | bytes 917504 | tf_op jit(solution)/shard_map/all_to_all | solution.py:548
  47.1 8.1 %collective-permute-start.12 = (bf16[224,512]{1,0:T(8,128)(2,1)}, bf16[224,512]{1,0:T(8,128)(2,1)}, u32[]{:S(2)}, u32[]{:S(2)}) collective-permute-start(bf16[224,512]{1,0:T(8,128)(2,1)} %collective-permute-done.1.refs_8_), channel_id=1, source_target_pairs={{0,8},{1,17},{8,0},{9,25},{16,24},{17,1},{24,16},{25,9},{2,10},{3,... | collective-permute-start | bytes 688136 | tf_op jit(solution)/shard_map/ppermute | solution.py:480
  48.7 11.4 %collective-permute-start.5 = (bf16[224,512]{1,0:T(8,128)(2,1)S(1)}, bf16[224,512]{1,0:T(8,128)(2,1)}, u32[]{:S(2)}, u32[]{:S(2)}) collective-permute-start(bf16[224,512]{1,0:T(8,128)(2,1)S(1)} %collective-permute-done.refs_6_), channel_id=1, source_target_pairs={{0,8},{1,17},{8,0},{9,25},{16,24},{17,1},{24,16},{25,9},{2,10},{3,... | collective-permute-start | bytes 688136 | tf_op jit(solution)/shard_map/ppermute | solution.py:480
  49.2 10.9 %collective-permute-start.13 = (bf16[224,512]{1,0:T(8,128)(2,1)}, bf16[224,512]{1,0:T(8,128)(2,1)}, u32[]{:S(2)}, u32[]{:S(2)}) collective-permute-start(bf16[224,512]{1,0:T(8,128)(2,1)} %collective-permute-done.1.refs_8_), channel_id=1, source_target_pairs={{0,16},{1,9},{8,24},{9,1},{16,0},{17,25},{24,8},{25,17},{2,18},{3,... | collective-permute-start | bytes 688136 | tf_op jit(solution)/shard_map/ppermute | solution.py:480
  50.7 9.9 %collective-permute-start.6 = (bf16[224,512]{1,0:T(8,128)(2,1)S(1)}, bf16[224,512]{1,0:T(8,128)(2,1)}, u32[]{:S(2)}, u32[]{:S(2)}) collective-permute-start(bf16[224,512]{1,0:T(8,128)(2,1)S(1)} %collective-permute-done.refs_6_), channel_id=1, source_target_pairs={{0,16},{1,9},{8,24},{9,1},{16,0},{17,25},{24,8},{25,17},{2,18},{3,... | collective-permute-start | bytes 688136 | tf_op jit(solution)/shard_map/ppermute | solution.py:480
  51.2 11.4 %collective-permute-start.8 = (bf16[224,512]{1,0:T(8,128)(2,1)}, bf16[224,512]{1,0:T(8,128)(2,1)}, u32[]{:S(2)}, u32[]{:S(2)}) collective-permute-start(bf16[224,512]{1,0:T(8,128)(2,1)} %collective-permute-done.1.refs_8_), channel_id=1, source_target_pairs={{0,2},{2,0},{4,6},{6,4},{1,3},{3,1},{5,7},{7,5},{8,10},{10,8},{12,... | collective-permute-start | bytes 688136 | tf_op jit(solution)/shard_map/ppermute | solution.py:466
  55.2 8.9 %collective-permute-start.14 = (bf16[224,512]{1,0:T(8,128)(2,1)}, bf16[224,512]{1,0:T(8,128)(2,1)}, u32[]{:S(2)}, u32[]{:S(2)}) collective-permute-start(bf16[224,512]{1,0:T(8,128)(2,1)} %collective-permute-done.12.refs_9_), channel_id=1, source_target_pairs={{0,16},{1,9},{8,24},{9,1},{16,0},{17,25},{24,8},{25,17},{2,18},{3,... | collective-permute-start | bytes 688136 | tf_op jit(solution)/shard_map/ppermute | solution.py:480
  60.1 10.8 %collective-permute-start.3 = (bf16[128,2048]{1,0:T(8,128)(2,1)}, bf16[128,2048]{1,0:T(8,128)(2,1)}, u32[]{:S(2)}, u32[]{:S(2)}) collective-permute-start(bf16[128,2048]{1,0:T(8,128)(2,1)} %bitcast.41), channel_id=1, source_target_pairs={{0,1},{1,0},{2,3},{3,2},{4,5},{5,4},{6,7},{7,6},{8,9},{9,8},{10,11... | collective-permute-start | bytes 1572872 | tf_op jit(solution)/shard_map/ppermute | solution.py:462
  60.1 10.8 %collective-permute-start.4 = (bf16[128,2048]{1,0:T(8,128)(2,1)}, bf16[128,2048]{1,0:T(8,128)(2,1)}, u32[]{:S(2)}, u32[]{:S(2)}) collective-permute-start(bf16[128,2048]{1,0:T(8,128)(2,1)} %bitcast.44), channel_id=1, source_target_pairs={{0,1},{1,0},{2,3},{3,2},{4,5},{5,4},{6,7},{7,6},{8,9},{9,8},{10,11... | collective-permute-start | bytes 1572872 | tf_op jit(solution)/shard_map/ppermute | solution.py:462
  60.6 8.2 %collective-permute-start.7 = (bf16[224,512]{1,0:T(8,128)(2,1)}, bf16[224,512]{1,0:T(8,128)(2,1)}, u32[]{:S(2)}, u32[]{:S(2)}) collective-permute-start(bf16[224,512]{1,0:T(8,128)(2,1)} %collective-permute-done.5.refs_7_), channel_id=1, source_target_pairs={{0,16},{1,9},{8,24},{9,1},{16,0},{17,25},{24,8},{25,17},{2,18},{3,... | collective-permute-start | bytes 688136 | tf_op jit(solution)/shard_map/ppermute | solution.py:480
  62.6 7.8 %collective-permute-start.9 = (bf16[224,512]{1,0:T(8,128)(2,1)}, bf16[224,512]{1,0:T(8,128)(2,1)}, u32[]{:S(2)}, u32[]{:S(2)}) collective-permute-start(bf16[224,512]{1,0:T(8,128)(2,1)} %collective-permute-done.8.refs_10_), channel_id=1, source_target_pairs={{0,8},{1,17},{8,0},{9,25},{16,24},{17,1},{24,16},{25,9},{2,10},{3,... | collective-permute-start | bytes 688136 | tf_op jit(solution)/shard_map/ppermute | solution.py:480
  64.1 6.8 %collective-permute-start.2 = (bf16[8,2,16,896]{3,2,1,0:T(8,128)(2,1)}, bf16[8,2,16,896]{3,2,1,0:T(8,128)(2,1)S(1)}, u32[]{:S(2)}, u32[]{:S(2)}) collective-permute-start(bf16[8,2,16,896]{3,2,1,0:T(8,128)(2,1)} %all-to-all-done.1.refs_0_), channel_id=1, source_target_pairs={{0,1},{1,0},{2,3},{3,2},{4,5},{5,4},{6,7},{7,6},{8,9},{9,8},{10,11... | collective-permute-start | bytes 1376264 | tf_op jit(solution)/shard_map/ppermute | solution.py:462
  68.9 13.1 %collective-permute-start.10 = (bf16[224,512]{1,0:T(8,128)(2,1)}, bf16[224,512]{1,0:T(8,128)(2,1)S(1)}, u32[]{:S(2)}, u32[]{:S(2)}) collective-permute-start(bf16[224,512]{1,0:T(8,128)(2,1)} %collective-permute-done.8.refs_10_), channel_id=1, source_target_pairs={{0,16},{1,9},{8,24},{9,1},{16,0},{17,25},{24,8},{25,17},{2,18},{3,... | collective-permute-start | bytes 688136 | tf_op jit(solution)/shard_map/ppermute | solution.py:480
  70.4 11.6 %collective-permute-start.11 = (bf16[224,512]{1,0:T(8,128)(2,1)}, bf16[224,512]{1,0:T(8,128)(2,1)S(1)}, u32[]{:S(2)}, u32[]{:S(2)}) collective-permute-start(bf16[224,512]{1,0:T(8,128)(2,1)} %collective-permute-done.9.refs_11_), channel_id=1, source_target_pairs={{0,16},{1,9},{8,24},{9,1},{16,0},{17,25},{24,8},{25,17},{2,18},{3,... | collective-permute-start | bytes 688136 | tf_op jit(solution)/shard_map/ppermute | solution.py:480
  80.4 19.5 %collective-permute-start.18 = (bf16[2,2,224,512]{3,2,1,0:T(8,128)(2,1)}, bf16[2,2,224,512]{3,2,1,0:T(8,128)(2,1)}, u32[]{:S(2)}, u32[]{:S(2)}) collective-permute-start(bf16[2,2,224,512]{3,2,1,0:T(8,128)(2,1)} %get-tuple-element.54), channel_id=1, source_target_pairs={{0,16},{1,9},{8,24},{9,1},{16,0},{17,25},{24,8},{25,17},{2,18},{3,... | collective-permute-start | bytes 2752520 | tf_op jit(solution)/shard_map/ppermute | solution.py:480
  91.3 14.0 %collective-permute-start.20 = (bf16[2,2,224,512]{3,2,1,0:T(8,128)(2,1)}, bf16[2,2,224,512]{3,2,1,0:T(8,128)(2,1)}, u32[]{:S(2)}, u32[]{:S(2)}) collective-permute-start(bf16[2,2,224,512]{3,2,1,0:T(8,128)(2,1)} %get-tuple-element.58), channel_id=1, source_target_pairs={{0,16},{1,9},{8,24},{9,1},{16,0},{17,25},{24,8},{25,17},{2,18},{3,... | collective-permute-start | bytes 2752520 | tf_op jit(solution)/shard_map/ppermute | solution.py:480
  91.9 1.8 %collective-permute-start.17 = (bf16[8,2,16,896]{3,2,1,0:T(8,128)(2,1)S(1)}, bf16[8,2,16,896]{3,2,1,0:T(8,128)(2,1)S(1)}, u32[]{:S(2)}, u32[]{:S(2)}) collective-permute-start(bf16[8,2,16,896]{3,2,1,0:T(8,128)(2,1)S(1)} %get-tuple-element.50), channel_id=1, source_target_pairs={{0,1},{1,0},{2,3},{3,2},{4,5},{5,4},{6,7},{7,6},{8,9},{9,8},{10,11... | collective-permute-start | bytes 1376264 | tf_op jit(solution)/shard_map/ppermute | solution.py:462
  94.5 27.1 %all-to-all-start.2 = ((bf16[8,2,16,896]{3,2,1,0:T(8,128)(2,1)}), bf16[8,2,16,896]{3,2,1,0:T(8,128)(2,1)}, u32[]{:S(2)}, u32[]{:S(2)}) async-start(bf16[8,2,16,896]{3,2,1,0:T(8,128)(2,1)} %bitcast.34), calls=%async_computation.2 | async-start | bytes 917504 | tf_op jit(solution)/shard_map/all_to_all | solution.py:574
  101.5 8.5 %collective-permute-start.19 = (bf16[2,224,512]{2,1,0:T(8,128)(2,1)S(1)}, bf16[2,224,512]{2,1,0:T(8,128)(2,1)S(1)}, u32[]{:S(2)}, u32[]{:S(2)}) collective-permute-start(bf16[2,224,512]{2,1,0:T(8,128)(2,1)S(1)} %get-tuple-element.56), channel_id=1, source_target_pairs={{0,8},{1,17},{8,0},{9,25},{16,24},{17,1},{24,16},{25,9},{2,10},{3,... | collective-permute-start | bytes 1376264 | tf_op jit(solution)/shard_map/ppermute | solution.py:480
  106.9 8.7 %collective-permute-start.22 = (bf16[2,224,512]{2,1,0:T(8,128)(2,1)S(1)}, bf16[2,224,512]{2,1,0:T(8,128)(2,1)S(1)}, u32[]{:S(2)}, u32[]{:S(2)}) collective-permute-start(bf16[2,224,512]{2,1,0:T(8,128)(2,1)S(1)} %get-tuple-element.62), channel_id=1, source_target_pairs={{0,8},{1,17},{8,0},{9,25},{16,24},{17,1},{24,16},{25,9},{2,10},{3,... | collective-permute-start | bytes 1376264 | tf_op jit(solution)/shard_map/ppermute | solution.py:480
  110.9 16.0 %collective-permute-start.21 = (bf16[1,224,512]{2,1,0:T(8,128)(2,1)}, bf16[1,224,512]{2,1,0:T(8,128)(2,1)}, u32[]{:S(2)}, u32[]{:S(2)}) collective-permute-start(bf16[1,224,512]{2,1,0:T(8,128)(2,1)} %get-tuple-element.60), channel_id=1, source_target_pairs={{0,4},{2,6},{4,0},{6,2},{1,5},{3,7},{5,1},{7,3},{8,12},{10,14},{12... | collective-permute-start | bytes 688136 | tf_op jit(solution)/shard_map/ppermute | solution.py:466
  113.8 37.8 %collective-permute-start.15 = (bf16[128,2048]{1,0:T(8,128)(2,1)}, bf16[128,2048]{1,0:T(8,128)(2,1)}, u32[]{:S(2)}, u32[]{:S(2)}) collective-permute-start(bf16[128,2048]{1,0:T(8,128)(2,1)} %get-tuple-element.46), channel_id=1, source_target_pairs={{0,1},{1,0},{2,3},{3,2},{4,5},{5,4},{6,7},{7,6},{8,9},{9,8},{10,11... | collective-permute-start | bytes 1572872 | tf_op jit(solution)/shard_map/ppermute | solution.py:462
  113.8 37.8 %collective-permute-start.16 = (bf16[128,2048]{1,0:T(8,128)(2,1)}, bf16[128,2048]{1,0:T(8,128)(2,1)}, u32[]{:S(2)}, u32[]{:S(2)}) collective-permute-start(bf16[128,2048]{1,0:T(8,128)(2,1)} %get-tuple-element.48), channel_id=1, source_target_pairs={{0,1},{1,0},{2,3},{3,2},{4,5},{5,4},{6,7},{7,6},{8,9},{9,8},{10,11... | collective-permute-start | bytes 1572872 | tf_op jit(solution)/shard_map/ppermute | solution.py:462
  116.6 21.3 %collective-permute-start.23 = (bf16[1,224,512]{2,1,0:T(8,128)(2,1)}, bf16[1,224,512]{2,1,0:T(8,128)(2,1)}, u32[]{:S(2)}, u32[]{:S(2)}) collective-permute-start(bf16[1,224,512]{2,1,0:T(8,128)(2,1)} %get-tuple-element.63), channel_id=1, source_target_pairs={{0,2},{2,0},{4,6},{6,4},{1,3},{3,1},{5,7},{7,5},{8,10},{10,8},{12,... | collective-permute-start | bytes 688136 | tf_op jit(solution)/shard_map/ppermute | solution.py:466
  119.2 18.7 %collective-permute-start.24 = (bf16[1,224,512]{2,1,0:T(8,128)(2,1)}, bf16[1,224,512]{2,1,0:T(8,128)(2,1)}, u32[]{:S(2)}, u32[]{:S(2)}) collective-permute-start(bf16[1,224,512]{2,1,0:T(8,128)(2,1)} %get-tuple-element.64), channel_id=1, source_target_pairs={{0,6},{2,4},{4,2},{6,0},{1,7},{3,5},{5,3},{7,1},{8,14},{10,12},{12... | collective-permute-start | bytes 688136 | tf_op jit(solution)/shard_map/ppermute | solution.py:466
  133.4 28.3 %all-to-all-start.3 = ((bf16[8,4,16,896]{3,2,1,0:T(8,128)(2,1)}), bf16[8,4,16,896]{3,2,1,0:T(8,128)(2,1)S(1)}, u32[]{:S(2)}, u32[]{:S(2)}) async-start(bf16[8,4,16,896]{3,2,1,0:T(8,128)(2,1)} %bitcast.33), calls=%async_computation.3 | async-start | bytes 1835008 | tf_op jit(solution)/shard_map/all_to_all | solution.py:615
  139.2 6.1 %collective-permute-start.25 = (bf16[224,512]{1,0:T(8,128)(2,1)S(1)}, bf16[224,512]{1,0:T(8,128)(2,1)S(1)}, u32[]{:S(2)}, u32[]{:S(2)}) collective-permute-start(bf16[224,512]{1,0:T(8,128)(2,1)S(1)} %bitcast.28), channel_id=1, source_target_pairs={{0,8},{1,17},{8,0},{9,25},{16,24},{17,1},{24,16},{25,9},{2,10},{3,... | collective-permute-start | bytes 688136 | tf_op jit(solution)/shard_map/ppermute | solution.py:480
  140.6 13.3 %collective-permute-start.26 = (bf16[224,512]{1,0:T(8,128)(2,1)S(1)}, bf16[224,512]{1,0:T(8,128)(2,1)S(1)}, u32[]{:S(2)}, u32[]{:S(2)}) collective-permute-start(bf16[224,512]{1,0:T(8,128)(2,1)S(1)} %bitcast.29), channel_id=1, source_target_pairs={{0,16},{1,9},{8,24},{9,1},{16,0},{17,25},{24,8},{25,17},{2,18},{3,... | collective-permute-start | bytes 688136 | tf_op jit(solution)/shard_map/ppermute | solution.py:480
  145.3 10.3 %collective-permute-start.27 = (bf16[224,512]{1,0:T(8,128)(2,1)S(1)}, bf16[224,512]{1,0:T(8,128)(2,1)S(1)}, u32[]{:S(2)}, u32[]{:S(2)}) collective-permute-start(bf16[224,512]{1,0:T(8,128)(2,1)S(1)} %collective-permute-done.25.refs_1_), channel_id=1, source_target_pairs={{0,16},{1,9},{8,24},{9,1},{16,0},{17,25},{24,8},{25,17},{2,18},{3,... | collective-permute-start | bytes 688136 | tf_op jit(solution)/shard_map/ppermute | solution.py:480
  (8 other events, 182.6 us)
